TPU v7x, 32 devices: a whole 2x2x4 slice. The times are simulated.
32 devices in a mesh: dp: 8 (over z, x), head: 4 (over y, core).
Axes of the slice: x: 2, y: 2, z: 4, core: 2. Of those that a mesh axis runs over, the one named last changes fastest.
Arguments:
- media_tokens: bfloat16 [128, 576, 1024], P(('dp', 'head')), may hold values from -6 to 6
- latents: bfloat16 [128, 64, 1024], P(('dp', 'head')), may hold values from -6 to 6
- cotangent: float32 [128, 64, 1024], P(('dp', 'head')), may hold values from -7.2 to 7.2
- counts: int32 [128], P('dp'), may hold values from 256 to 576, as said below
- attention_weights: float32 [4, 1024, 1024], P(None, 'dp', 'head')
- attention_first: float32 [4, 1024, 1024], P(None, 'dp', 'head'), may hold values from -2.2888184e-05 to 2.2888184e-05
- attention_second: float32 [4, 1024, 1024], P(None, 'dp', 'head'), may hold values from 1.9858518e-13 to 7.943407e-13
- expand_weight: float32 [1024, 4096], P('dp', 'head'), may hold values from -0.1875 to 0.1875
- expand_first: float32 [1024, 4096], P('dp', 'head'), may hold values from -2.2888184e-05 to 2.2888184e-05
- expand_second: float32 [1024, 4096], P('dp', 'head'), may hold values from 1.9858518e-13 to 7.943407e-13
- reduce_weight: float32 [4096, 1024], P('head', 'dp'), may hold values from -0.09375 to 0.09375
- reduce_first: float32 [4096, 1024], P('head', 'dp'), may hold values from -2.2888184e-05 to 2.2888184e-05
- reduce_second: float32 [4096, 1024], P('head', 'dp'), may hold values from 1.9858518e-13 to 7.943407e-13
- norm_params: float32 [6, 1024], replicated, may hold values from -1.2 to 2.52
- norm_first: float32 [6, 1024], replicated, may hold values from -9.1552734e-05 to 9.1552734e-05
- norm_second: float32 [6, 1024], replicated, may hold values from 3.1773629e-12 to 1.27094515e-11
Outputs:
- resampled: bfloat16 [128, 64, 1024], P(('dp', 'head'))
- media_grad: bfloat16 [128, 576, 1024], P(('dp', 'head'))
- latent_grad: bfloat16 [128, 64, 1024], P(('dp', 'head'))
- grad_norm: float32 [], replicated
- attention_new: float32 [4, 1024, 1024], P(None, 'dp', 'head')
- attention_first_new: float32 [4, 1024, 1024], P(None, 'dp', 'head')
- attention_second_new: float32 [4, 1024, 1024], P(None, 'dp', 'head')
- expand_new: float32 [1024, 4096], P('dp', 'head')
- expand_first_new: float32 [1024, 4096], P('dp', 'head')
- expand_second_new: float32 [1024, 4096], P('dp', 'head')
- reduce_new: float32 [4096, 1024], P('head', 'dp')
- reduce_first_new: float32 [4096, 1024], P('head', 'dp')
- reduce_second_new: float32 [4096, 1024], P('head', 'dp')
- norm_new: float32 [6, 1024], replicated
- norm_first_new: float32 [6, 1024], replicated
- norm_second_new: float32 [6, 1024], replicated
Inputs may be any that keep to these rules, and one draw needn't show every extreme that they name: `counts`: each image has either 256 or 576 patch rows; rows of its slot past that count are padding.
All inputs are finite; a program needn't handle non-finite values.
Results may differ from a plain program's by a relative error of at most 0.015.
Values may be sent and summed in bfloat16 or wider, within the bound.
A program may use at most 192 MiB of HBM per device.

v0:
```python
import jax
import jax.numpy as jnp
from jax import lax
from jax.sharding import PartitionSpec as P

D = 1024
HEADS = 16
STEP = 10


LN_EPS = 1e-05
BETA_ONE = 0.9
BETA_TWO = 0.999
ADAM_EPS = 1e-08
MATRIX_RATE = 0.1
NORM_RATE = 0.6
DECAY_RATE = 0.1
MAX_NORM = 0.05


def layer_norm(values, gain_row, shift_row):
    center = values - jnp.mean(values, axis=-1, keepdims=True)
    scaled = lax.rsqrt(jnp.mean(center * center, axis=-1, keepdims=True) + LN_EPS)
    normed = center * scaled
    return (normed * gain_row + shift_row, normed, scaled)


def norm_back(upstream, normed, scaled, gain_row):
    inner = upstream * gain_row
    result = scaled * (
        inner
        - jnp.mean(inner, axis=-1, keepdims=True)
        - normed * jnp.mean(inner * normed, axis=-1, keepdims=True)
    )
    lead_axes = tuple(range(upstream.ndim - 1))
    return (result, jnp.sum(upstream * normed, axis=lead_axes), jnp.sum(upstream, axis=lead_axes))


def head_scores(head_queries, head_pairs, lengths, patches):
    item_count, lat_rows = (head_queries.shape[0], head_queries.shape[1])
    columns = head_queries.shape[3]
    key_span = head_pairs.shape[1]
    head_size = D // HEADS
    heads_here = columns // head_size
    query_heads = head_queries[:, :, 0].reshape(item_count, lat_rows, heads_here, head_size)
    key_heads = head_pairs[:, :, 0].reshape(item_count, key_span, heads_here, head_size)
    value_heads = head_pairs[:, :, 1].reshape(item_count, key_span, heads_here, head_size)
    positions = jnp.arange(key_span, dtype=jnp.int32)
    visible = (positions[None, :] < lengths[:, None]) | (positions[None, :] >= patches)
    scores = jnp.einsum(
        "eqhc,ekhc->ehqk", query_heads, key_heads, preferred_element_type=jnp.float32
    ) * head_size ** (-0.5)
    scores = jnp.where(visible[:, None, None, :], scores, -1e30)
    return (query_heads, key_heads, value_heads, scores)


def attend_forward(head_queries, head_pairs, lengths, patches):
    query_heads, key_heads, value_heads, scores = head_scores(
        head_queries, head_pairs, lengths, patches
    )
    log_total = jax.nn.logsumexp(scores, axis=-1)
    softened = jnp.exp(scores - log_total[..., None]).astype(jnp.bfloat16)
    mixed = jnp.einsum("ehqk,ekhc->eqhc", softened, value_heads, preferred_element_type=jnp.float32)
    shape_out = (head_queries.shape[0], head_queries.shape[1], head_queries.shape[3])
    return (mixed.astype(jnp.bfloat16).reshape(shape_out), log_total)


def attend_backward(head_queries, head_pairs, lengths, patches, log_total, head_mixed_grad):
    query_heads, key_heads, value_heads, scores = head_scores(
        head_queries, head_pairs, lengths, patches
    )
    head_size = D // HEADS
    item_count, lat_rows = (head_queries.shape[0], head_queries.shape[1])
    columns = head_queries.shape[3]
    key_span = head_pairs.shape[1]
    exact = jnp.exp(scores - log_total[..., None])
    softened = exact.astype(jnp.bfloat16)
    mixed_heads = head_mixed_grad.reshape(query_heads.shape)
    prob_grad = jnp.einsum(
        "eqhc,ekhc->ehqk", mixed_heads, value_heads, preferred_element_type=jnp.float32
    )
    score_grad = (exact * (prob_grad - jnp.sum(exact * prob_grad, axis=-1, keepdims=True))).astype(
        jnp.bfloat16
    )
    factor = head_size ** (-0.5)
    query_back = (
        jnp.einsum("ehqk,ekhc->eqhc", score_grad, key_heads, preferred_element_type=jnp.float32)
        * factor
    ).astype(jnp.bfloat16)
    key_back = (
        jnp.einsum("ehqk,eqhc->ekhc", score_grad, query_heads, preferred_element_type=jnp.float32)
        * factor
    ).astype(jnp.bfloat16)
    value_back = jnp.einsum(
        "ehqk,eqhc->ekhc", softened, mixed_heads, preferred_element_type=jnp.float32
    ).astype(jnp.bfloat16)
    query_back = query_back.reshape(item_count, lat_rows, 1, columns)
    pair_back = jnp.stack(
        [
            key_back.reshape(item_count, key_span, columns),
            value_back.reshape(item_count, key_span, columns),
        ],
        axis=2,
    )
    return (query_back, pair_back)


def adam_step(master, first, second, gradient, step_rate, decay_rate):
    first_new = BETA_ONE * first + (1.0 - BETA_ONE) * gradient
    second_new = BETA_TWO * second + (1.0 - BETA_TWO) * gradient * gradient
    first_hat = first_new / (1.0 - BETA_ONE**STEP)
    second_hat = second_new / (1.0 - BETA_TWO**STEP)
    master_new = master - step_rate * (
        first_hat / (jnp.sqrt(second_hat) + ADAM_EPS) + decay_rate * master
    )
    return (master_new, first_new, second_new)


def on_device(
    media_tokens,
    latents,
    cotangent,
    counts,
    attention_weights,
    attention_first,
    attention_second,
    expand_weight,
    expand_first,
    expand_second,
    reduce_weight,
    reduce_first,
    reduce_second,
    norm_params,
    norm_first,
    norm_second,
):
    dp_count = lax.axis_size("dp")
    head_count = lax.axis_size("head")
    images, patches, width = media_tokens.shape
    lat_rows = latents.shape[1]
    key_span = patches + lat_rows
    row_block = attention_weights.shape[1]
    col_block = attention_weights.shape[2]
    gathered = lax.all_gather(
        attention_weights.astype(jnp.bfloat16)[None], ("dp", "head"), axis=0, tiled=True
    )
    full_weights = gathered.reshape(dp_count, head_count, 4, row_block, col_block)
    full_weights = full_weights.transpose(2, 0, 3, 1, 4).reshape(4, width, width)
    query_weight = full_weights[0]
    pair_weight = jnp.concatenate([full_weights[1], full_weights[2]], axis=1)
    output_weight = full_weights[3]
    expand_full, reduce_part = (
        lax.all_gather(expand_weight.astype(jnp.bfloat16), "dp", axis=0, tiled=True),
        lax.all_gather(reduce_weight.astype(jnp.bfloat16), "dp", axis=1, tiled=True),
    )
    media_norm, media_hat, media_scale = layer_norm(
        media_tokens.astype(jnp.float32), norm_params[0], norm_params[1]
    )
    latent_in = latents.astype(jnp.float32)
    latent_norm, latent_hat, latent_scale = layer_norm(latent_in, norm_params[2], norm_params[3])
    pair_input = jnp.concatenate(
        [media_norm.astype(jnp.bfloat16), latent_norm.astype(jnp.bfloat16)], axis=1
    )
    latent_low = pair_input[:, patches:]
    pairs = jnp.einsum("isd,de->ise", pair_input, pair_weight, preferred_element_type=jnp.float32)
    pairs = pairs.astype(jnp.bfloat16).reshape(images, key_span, 2, width)
    queries = jnp.einsum(
        "iqd,de->iqe", latent_low, query_weight, preferred_element_type=jnp.float32
    )
    queries = queries.astype(jnp.bfloat16).reshape(images, lat_rows, 1, width)
    head_queries, head_pairs = (
        lax.all_to_all(queries, "head", split_axis=3, concat_axis=0, tiled=True),
        lax.all_to_all(pairs, "head", split_axis=3, concat_axis=0, tiled=True),
    )
    head_mixed, log_total = attend_forward(head_queries, head_pairs, counts, patches)
    mixed = lax.all_to_all(head_mixed, "head", split_axis=0, concat_axis=2, tiled=True)
    middle = latent_in + jnp.einsum(
        "iqc,cd->iqd", mixed, output_weight, preferred_element_type=jnp.float32
    )
    ff_norm, ff_hat, ff_scale = layer_norm(middle, norm_params[4], norm_params[5])
    rows_all = lax.all_gather(
        ff_norm.astype(jnp.bfloat16).reshape(images * lat_rows, width), "head", axis=0, tiled=True
    )
    before = jnp.dot(rows_all, expand_full, preferred_element_type=jnp.float32)
    hidden, gelu_back = jax.vjp(jax.nn.gelu, before)
    hidden_low = hidden.astype(jnp.bfloat16)
    added = lax.psum_scatter(
        jnp.dot(hidden_low, reduce_part, preferred_element_type=jnp.float32).astype(jnp.bfloat16),
        "head",
        scatter_dimension=0,
        tiled=True,
    ).astype(jnp.float32)
    resampled = (middle + added.reshape(images, lat_rows, width)).astype(jnp.bfloat16)
    back_all = lax.all_gather(
        cotangent.astype(jnp.bfloat16).reshape(images * lat_rows, width), "head", axis=0, tiled=True
    )
    reduce_grad = jnp.einsum("nf,nd->df", hidden_low, back_all, preferred_element_type=jnp.float32)
    hidden_grad = jnp.einsum("nd,fd->nf", back_all, reduce_part, preferred_element_type=jnp.float32)
    before_grad = gelu_back(hidden_grad)[0].astype(jnp.bfloat16)
    expand_grad = jnp.einsum("nd,nf->df", rows_all, before_grad, preferred_element_type=jnp.float32)
    ff_back = lax.psum_scatter(
        jnp.einsum(
            "nf,df->nd", before_grad, expand_full, preferred_element_type=jnp.float32
        ).astype(jnp.bfloat16),
        "head",
        scatter_dimension=0,
        tiled=True,
    ).astype(jnp.float32)
    middle_part, ff_gain_grad, ff_shift_grad = norm_back(
        ff_back.reshape(images, lat_rows, width), ff_hat, ff_scale, norm_params[4]
    )
    middle_grad = cotangent + middle_part
    expand_share, reduce_share = (
        lax.psum_scatter(
            expand_grad.astype(jnp.bfloat16), "dp", scatter_dimension=0, tiled=True
        ).astype(jnp.float32),
        lax.psum_scatter(
            reduce_grad.astype(jnp.bfloat16), "dp", scatter_dimension=0, tiled=True
        ).astype(jnp.float32),
    )
    reduce_share = reduce_share.T
    hidden_squares = jnp.sum(expand_share * expand_share) + jnp.sum(reduce_share * reduce_share)
    branch_low = middle_grad.astype(jnp.bfloat16)
    output_grad = jnp.einsum("iqc,iqd->cd", mixed, branch_low, preferred_element_type=jnp.float32)
    mixed_grad = jnp.einsum(
        "iqd,cd->iqc", branch_low, output_weight, preferred_element_type=jnp.float32
    ).astype(jnp.bfloat16)
    head_mixed_grad = lax.all_to_all(mixed_grad, "head", split_axis=2, concat_axis=0, tiled=True)
    query_back, pair_back = attend_backward(
        head_queries, head_pairs, counts, patches, log_total, head_mixed_grad
    )
    query_back, pair_back = (
        lax.all_to_all(query_back, "head", split_axis=0, concat_axis=3, tiled=True),
        lax.all_to_all(pair_back, "head", split_axis=0, concat_axis=3, tiled=True),
    )
    pair_flat = pair_back.reshape(images, key_span, 2 * width)
    pair_weight_grad = jnp.einsum(
        "isd,ise->de", pair_input, pair_flat, preferred_element_type=jnp.float32
    )
    pair_input_grad = jnp.einsum(
        "ise,de->isd", pair_flat, pair_weight, preferred_element_type=jnp.float32
    )
    query_rows = query_back.reshape(images, lat_rows, width)
    query_grad = jnp.einsum(
        "iqd,iqe->de", latent_low, query_rows, preferred_element_type=jnp.float32
    )
    latent_side = pair_input_grad[:, patches:] + jnp.einsum(
        "iqe,de->iqd", query_rows, query_weight, preferred_element_type=jnp.float32
    )
    media_back, media_gain_grad, media_shift_grad = norm_back(
        pair_input_grad[:, :patches], media_hat, media_scale, norm_params[0]
    )
    latent_back, latent_gain_grad, latent_shift_grad = norm_back(
        latent_side, latent_hat, latent_scale, norm_params[2]
    )
    media_grad = media_back.astype(jnp.bfloat16)
    latent_grad = (middle_grad + latent_back).astype(jnp.bfloat16)
    attention_local = jnp.stack(
        [query_grad, pair_weight_grad[:, :width], pair_weight_grad[:, width:], output_grad]
    )
    norm_local = jnp.stack(
        [
            media_gain_grad,
            media_shift_grad,
            latent_gain_grad,
            latent_shift_grad,
            ff_gain_grad,
            ff_shift_grad,
        ]
    )
    attention_total, norm_total, hidden_total = lax.psum(
        (attention_local, norm_local, hidden_squares), ("dp", "head")
    )
    squares = (
        jnp.sum(attention_total * attention_total) + jnp.sum(norm_total * norm_total) + hidden_total
    )
    arranged = attention_total.reshape(4, dp_count, row_block, head_count, col_block)
    attention_share = lax.dynamic_slice(
        arranged,
        (0, lax.axis_index("dp"), 0, lax.axis_index("head"), 0),
        (4, 1, row_block, 1, col_block),
    ).reshape(4, row_block, col_block)
    grad_norm = jnp.sqrt(squares)
    clip_factor = jnp.minimum(1.0, MAX_NORM / (grad_norm + 1e-06))
    attention_new, attention_first_new, attention_second_new = adam_step(
        attention_weights,
        attention_first,
        attention_second,
        attention_share * clip_factor,
        MATRIX_RATE,
        DECAY_RATE,
    )
    expand_new, expand_first_new, expand_second_new = adam_step(
        expand_weight,
        expand_first,
        expand_second,
        expand_share * clip_factor,
        MATRIX_RATE,
        DECAY_RATE,
    )
    reduce_new, reduce_first_new, reduce_second_new = adam_step(
        reduce_weight,
        reduce_first,
        reduce_second,
        reduce_share * clip_factor,
        MATRIX_RATE,
        DECAY_RATE,
    )
    norm_new, norm_first_new, norm_second_new = adam_step(
        norm_params, norm_first, norm_second, norm_total * clip_factor, NORM_RATE, 0.0
    )
    return (
        resampled,
        media_grad,
        latent_grad,
        grad_norm,
        attention_new,
        attention_first_new,
        attention_second_new,
        expand_new,
        expand_first_new,
        expand_second_new,
        reduce_new,
        reduce_first_new,
        reduce_second_new,
        norm_new,
        norm_first_new,
        norm_second_new,
    )


def solution(mesh):
    in_specs = (
        P(("dp", "head"), None, None),
        P(("dp", "head"), None, None),
        P(("dp", "head"), None, None),
        P("dp"),
        P(None, "dp", "head"),
        P(None, "dp", "head"),
        P(None, "dp", "head"),
        P("dp", "head"),
        P("dp", "head"),
        P("dp", "head"),
        P("head", "dp"),
        P("head", "dp"),
        P("head", "dp"),
        P(),
        P(),
        P(),
    )
    out_specs = (
        P(("dp", "head"), None, None),
        P(("dp", "head"), None, None),
        P(("dp", "head"), None, None),
        P(),
        P(None, "dp", "head"),
        P(None, "dp", "head"),
        P(None, "dp", "head"),
        P("dp", "head"),
        P("dp", "head"),
        P("dp", "head"),
        P("head", "dp"),
        P("head", "dp"),
        P("head", "dp"),
        P(),
        P(),
        P(),
    )
    return jax.shard_map(
        on_device, mesh=mesh, in_specs=in_specs, out_specs=out_specs, check_vma=False
    )
```

profile of v0, /device:TPU:10, one launch (start us, length us, event | category | flops | bytes accessed | tf_op | source)
XLA Modules:
  0.0 1052.5 jit_solution(13185320142196273575)
XLA Ops:
  21.4 69.6 %all-gather.15.cloned.1.call-done = bf16[128,128,256]{2,1,0:T(8,128)(2,1)} async-done(((bf16[4,128,256]{2,1,0:T(8,128)(2,1)}), bf16[128,128,256]{2,1,0:T(8,128)(2,1)}) %all-gather.15.cloned.1.call-update) | async-done | bytes 8388624 | tf_op jit(solution)/shard_map/all_gather | solution.py:144
  91.0 10.1 copy.147
  119.7 16.6 %convolution_convert_fusion = bf16[4,640,2048]{2,1,0:T(8,128)(2,1)} fusion(bf16[4,64,1024]{2,1,0:T(8,128)(2,1)S(1)} %fusion.33, bf16[4,576,1024]{2,1,0:T(8,128)(2,1)} %fusion.7, bf16[1024,1024]{1,0:T(8,128)(2,1)} %bitcast.182, bf16[1024,1024]{1,0:T(8,128)(2,1)} %bitcast.180), kind=kOutput, calls=%fused_computation.30 | convolution fusion | flops 10761535488 | bytes 19922944 | tf_op jit(solution)/shard_map/isd,de->ise/dot_general | solution.py:165
  136.3 17.8 %reshape.209 = bf16[4,640,2,1024]{3,2,1,0:T(2,128)(2,1)} reshape(bf16[4,640,2048]{2,1,0:T(8,128)(2,1)} %convolution_convert_fusion) | data formatting | bytes 20971520 | tf_op jit(solution)/shard_map/reshape | solution.py:166
  154.0 27.7 %copy.99 = bf16[4,640,2,1024]{1,0,2,3:T(4,128)(2,1)} copy(bf16[4,640,2,1024]{3,2,1,0:T(2,128)(2,1)} %reshape.209) | data formatting | bytes 20971520 | tf_op jit(solution)/shard_map/reshape | solution.py:166
  192.0 122.8 %all-to-all-done = bf16[4,640,2,1024]{1,0,2,3:T(4,128)(2,1)} async-done(((bf16[4,640,2,1024]{1,0,2,3:T(4,128)(2,1)}), bf16[4,640,2,1024]{1,0,2,3:T(4,128)(2,1)}, u32[]{:S(2)}, u32[]{:S(2)}) %all-to-all-start) | async-done | bytes 10485792 | tf_op jit(solution)/shard_map/all_to_all | solution.py:173
  314.8 9.9 copy.100
  324.7 9.6 fusion.72
  372.9 14.2 %all-gather.7.cloned.1.call-done = bf16[1024,1024]{1,0:T(8,128)(2,1)} async-done(((bf16[256,1024]{1,0:T(8,128)(2,1)}), bf16[1024,1024]{1,0:T(8,128)(2,1)}) %all-gather.7.cloned.1.call-update) | async-done | bytes 2097168 | tf_op jit(solution)/shard_map/all_gather | solution.py:181
  387.1 10.0 fusion.23
  409.2 24.6 %reduce-scatter.7.cloned.1.call-done = bf16[256,1024]{1,0:T(8,128)(2,1)} async-done(((bf16[1024,1024]{1,0:T(8,128)(2,1)}), bf16[256,1024]{1,0:T(8,128)(2,1)}) %reduce-scatter.7.cloned.1.call-update) | async-done | bytes 524304 | tf_op jit(solution)/shard_map/reduce_scatter | solution.py:201
  436.8 30.9 %reduce-scatter.5.cloned.1.call-done = bf16[256,1024]{1,0:T(8,128)(2,1)} async-done(((bf16[1024,1024]{1,0:T(8,128)(2,1)}), bf16[256,1024]{1,0:T(8,128)(2,1)}) %reduce-scatter.5.cloned.1.call-update) | async-done | bytes 524304 | tf_op jit(solution)/shard_map/reduce_scatter | solution.py:187
  475.4 11.6 %all_to_all.96 = bf16[4,2,32768]{2,1,0:T(2,128)(2,1)S(1)} all-to-all(bf16[4,2,32768]{2,1,0:T(2,128)(2,1)S(1)} %reshape.236), channel_id=1, replica_groups=mesh['dp'=8,'head'=4] {'head'}, dimensions={0} | all-to-all | bytes 1048576 | tf_op jit(solution)/shard_map/all_to_all | solution.py:228
  488.1 12.3 %multiply_reduce_fusion.1 = (f32[16,4,64]{2,1,0:T(4,128)S(1)}, f32[16,4,64,640]{3,2,1,0:T(8,128)}) fusion(f32[16,4,64,640]{3,2,1,0:T(8,128)} %copy-done, f32[16,4,64]{2,1,0:T(4,128)S(1)} %log_add_fusion, pred[16,640]{1,0:T(8,128)(4,1)S(1)} %fusion.57, bf16[16,64,4,64]{1,3,2,0:T(8,128)(2,1)S(1)} %bitcast.167, bf16[16,640,4,64]{1,3,2,0:T(8,128)(2,1)} %bitcast.161), kind=kOutput, calls=%fused_computation.13 | convolution fusion | flops 348647424 | bytes 26781696 | tf_op jit(solution)/shard_map/eqhc,ekhc->ehqk/dot_general | solution.py:79
  562.1 96.8 %all-to-all-done.4 = bf16[16,640,2,256]{1,3,2,0:T(8,128)(2,1)} async-done(((bf16[16,640,2,256]{1,3,2,0:T(8,128)(2,1)}), bf16[16,640,2,256]{1,3,2,0:T(8,128)(2,1)}, u32[]{:S(2)}, u32[]{:S(2)}) %all-to-all-start.4) | async-done | bytes 10485792 | tf_op jit(solution)/shard_map/all_to_all | solution.py:234
  658.9 18.2 %copy.113 = bf16[4,4,640,2,256]{4,0,3,2,1:T(4,128)(2,1)} copy(bf16[4,4,640,2,256]{2,4,3,1,0:T(8,128)(2,1)} %bitcast.33) | data formatting | bytes 20971520 | tf_op jit(solution)/shard_map/all_to_all | solution.py:234
  677.1 17.7 %reshape.218 = bf16[4,640,2048]{2,1,0:T(8,128)(2,1)} reshape(bf16[4,640,2,4,256]{4,3,2,1,0:T(4,128)(2,1)} %bitcast.159) | data formatting | bytes 20971520 | tf_op jit(solution)/shard_map/reshape | solution.py:236
  694.8 15.8 %convolution_bitcast_fusion = f32[1024,2048]{1,0:T(8,128)S(1)} fusion(bf16[4,640,2048]{2,1,0:T(8,128)(2,1)} %reshape.218, bf16[4,64,1024]{2,1,0:T(8,128)(2,1)S(1)} %copy-done.21, bf16[4,576,1024]{2,1,0:T(8,128)(2,1)} %fusion.7), kind=kOutput, calls=%fused_computation.35 | convolution fusion | flops 10747904000 | bytes 24117248 | tf_op jit(solution)/shard_map/isd,ise->de/dot_general | solution.py:237
  712.3 9.7 pad_maximum_fusion
  731.3 15.9 %fusion.24 = f32[4,640,1024]{2,1,0:T(8,128)S(1)} fusion(bf16[4,640,2048]{2,1,0:T(8,128)(2,1)} %reshape.218, bf16[1024,1024]{1,0:T(8,128)(2,1)} %bitcast.183, bf16[1024,1024]{1,0:T(8,128)(2,1)} %bitcast.181), kind=kOutput, calls=%fused_computation.48 | convolution fusion | flops 10745806848 | bytes 25165824 | tf_op jit(solution)/shard_map/ise,de->isd/dot_general | solution.py:240
  757.4 42.4 %all-reduce = (f32[6,1024]{1,0:T(8,128)S(1)}, f32[]{:T(128)}) all-reduce(f32[6,1024]{1,0:T(8,128)S(1)} %stack.51, f32[]{:T(128)S(6)} %add.200), channel_id=1, replica_groups=mesh['dp'=8,'head'=4] {'dp','head'}, use_global_device_ids=true, to_apply=%region_25.26 | all-reduce | flops 6145 | bytes 49160 | tf_op jit(solution)/shard_map/psum | solution.py:271
  812.2 188.9 %all-reduce.3.cloned.1.call-done = f32[4,1024,1024]{2,1,0:T(8,128)} async-done(((f32[4,1024,1024]{2,1,0:T(8,128)}), f32[4,1024,1024]{2,1,0:T(8,128)}) %all-reduce.3.cloned.1.call-update) | async-done | bytes 16777232 | tf_op jit(solution)/shard_map/psum | solution.py:271
  1001.1 10.7 %multiply_reduce_fusion = f32[]{:T(128)} fusion(f32[4,1024,1024]{2,1,0:T(8,128)} %all-reduce.3.cloned.1.call-done), kind=kLoop, calls=%fused_computation.1 | loop fusion | flops 8388607 | bytes 16777220 | tf_op jit(solution)/shard_map/reduce_sum | solution.py:275
  1018.0 20.5 %reshape.221 = f32[4,8,128,4,256]{4,3,2,1,0:T(4,128)} reshape(f32[4,1024,1024]{2,1,0:T(8,128)} %all-reduce.3.cloned.1.call-done) | data formatting | bytes 33554432 | tf_op jit(solution)/shard_map/reshape | solution.py:277
  (234 shorter events, 206.7 us)
Async XLA Ops:
  8.0 83.0 %all-gather.15.cloned.1.call-start = ((), (), s32[]{:S(2)}) async-start(), calls=%async_computation.19 | async-start | bytes 8650752 | tf_op jit(solution)/shard_map/all_gather | solution.py:144
  17.9 101.8 %copy-start.20 = (bf16[4,64,1024]{2,1,0:T(8,128)(2,1)}, bf16[4,64,1024]{2,1,0:T(8,128)(2,1)S(1)}, u32[]{:S(2)}) copy-start(bf16[4,64,1024]{2,1,0:T(8,128)(2,1)S(1)} %fusion.33) | copy-start | bytes 1572868
  116.0 65.7 %all-to-all-start.1 = ((bf16[4,2,32768]{2,1,0:T(2,128)(2,1)}), bf16[4,2,32768]{2,1,0:T(2,128)(2,1)S(1)}, u32[]{:S(2)}, u32[]{:S(2)}) async-start(bf16[4,2,32768]{2,1,0:T(2,128)(2,1)} %reshape.234), calls=%async_computation.1 | async-start | bytes 1048576 | tf_op jit(solution)/shard_map/all_to_all | solution.py:172
  181.8 133.0 %all-to-all-start = ((bf16[4,640,2,1024]{1,0,2,3:T(4,128)(2,1)}), bf16[4,640,2,1024]{1,0,2,3:T(4,128)(2,1)}, u32[]{:S(2)}, u32[]{:S(2)}) async-start(bf16[4,640,2,1024]{1,0,2,3:T(4,128)(2,1)} %copy.99), calls=%async_computation | async-start | bytes 20971520 | tf_op jit(solution)/shard_map/all_to_all | solution.py:173
  187.9 178.4 %all-gather.13.cloned.1.call-start = ((), (), s32[]{:S(2)}) async-start(), calls=%async_computation.14 | async-start | bytes 2621440 | tf_op jit(solution)/shard_map/all_gather | solution.py:194
  188.8 177.5 %all-gather.11.cloned.1.call-start = ((), (), s32[]{:S(2)}) async-start(), calls=%async_computation.12 | async-start | bytes 2359296 | tf_op jit(solution)/shard_map/all_gather | solution.py:154
  189.7 183.2 %all-gather.9.cloned.1.call-start = ((), (), s32[]{:S(2)}) async-start(), calls=%async_computation.11 | async-start | bytes 2359296 | tf_op jit(solution)/shard_map/all_gather | solution.py:153
  191.9 142.3 %copy-start.4 = (bf16[4,64,1,4,256]{1,4,0,3,2:T(8,128)(2,1)}, bf16[4,64,1,4,256]{1,4,0,3,2:T(8,128)(2,1)S(1)}, u32[]{:S(2)}) copy-start(bf16[4,64,1,4,256]{1,4,0,3,2:T(8,128)(2,1)S(1)} %copy.130) | copy-start | bytes 1572868
  348.8 12.3 %all-to-all-start.2 = ((bf16[16,64,256]{2,1,0:T(8,128)(2,1)}), bf16[16,64,256]{2,1,0:T(8,128)(2,1)S(1)}, u32[]{:S(2)}, u32[]{:S(2)}) async-start(bf16[16,64,256]{2,1,0:T(8,128)(2,1)} %copy.104), calls=%async_computation.2 | async-start | bytes 1048576 | tf_op jit(solution)/shard_map/all_to_all | solution.py:176
  352.3 34.8 %all-gather.7.cloned.1.call-start = ((), (), s32[]{:S(2)}) async-start(), calls=%async_computation.10 | async-start | bytes 2621440 | tf_op jit(solution)/shard_map/all_gather | solution.py:181
  366.0 67.7 %reduce-scatter.7.cloned.1.call-start = ((), (), s32[]{:S(2)}) async-start(), calls=%async_computation.15 | async-start | bytes 2621440 | tf_op jit(solution)/shard_map/reduce_scatter | solution.py:201
  402.2 65.5 %reduce-scatter.5.cloned.1.call-start = ((), (), s32[]{:S(2)}) async-start(), calls=%async_computation.13 | async-start | bytes 2621440 | tf_op jit(solution)/shard_map/reduce_scatter | solution.py:187
  524.6 12.5 %all-to-all-start.5 = ((bf16[16,64,1,256]{3,1,2,0:T(8,128)(2,1)}), bf16[16,64,1,256]{3,1,2,0:T(8,128)(2,1)S(1)}, u32[]{:S(2)}, u32[]{:S(2)}) async-start(bf16[16,64,1,256]{3,1,2,0:T(8,128)(2,1)} %copy.114), calls=%async_computation.7 | async-start | bytes 1048576 | tf_op jit(solution)/shard_map/all_to_all | solution.py:233
  537.1 121.8 %all-to-all-start.4 = ((bf16[16,640,2,256]{1,3,2,0:T(8,128)(2,1)}), bf16[16,640,2,256]{1,3,2,0:T(8,128)(2,1)}, u32[]{:S(2)}, u32[]{:S(2)}) async-start(bf16[16,640,2,256]{1,3,2,0:T(8,128)(2,1)} %pad_maximum_fusion.1), calls=%async_computation.6 | async-start | bytes 20971520 | tf_op jit(solution)/shard_map/all_to_all | solution.py:234
  543.2 183.3 %reduce-scatter.9.cloned.1.call-start = ((), (), s32[]{:S(2)}) async-start(), calls=%async_computation.17 | async-start | bytes 2359296 | tf_op jit(solution)/shard_map/reduce_scatter | solution.py:214
  548.8 179.4 %reduce-scatter.11.cloned.1.call-start = ((), (), s32[]{:S(2)}) async-start(), calls=%async_computation.18 | async-start | bytes 2359296 | tf_op jit(solution)/shard_map/reduce_scatter | solution.py:217
  555.7 445.4 %all-reduce.3.cloned.1.call-start = ((), (), s32[]{:S(2)}) async-start(), calls=%async_computation.16 | async-start | bytes 33554432 | tf_op jit(solution)/shard_map/psum | solution.py:271
  559.3 117.8 %copy-start.22 = (bf16[4,64,1024]{2,1,0:T(8,128)(2,1)}, bf16[4,64,1024]{2,1,0:T(8,128)(2,1)S(1)}, u32[]{:S(2)}) copy-start(bf16[4,64,1024]{2,1,0:T(8,128)(2,1)S(1)} %reshape.220) | copy-start | bytes 1572868
  722.0 30.6 %slice-start.3 = ((s8[4718592]{0:T(1024)(128)(4,1)}), s8[524288]{0:T(1024)(128)(4,1)S(1)}, s32[]{:S(2)}) async-start(s8[4718592]{0:T(1024)(128)(4,1)} %bitcast.152), calls=%async_computation.23 | async-start | bytes 1048576
  812.2 201.6 %copy-start.16 = (f32[1024,128]{0,1:T(8,128)S(1)}, f32[1024,128]{0,1:T(8,128)}, u32[]{:S(2)}) copy-start(f32[1024,128]{0,1:T(8,128)} %copy.120) | copy-start | bytes 1572868
  812.2 201.7 %copy-start.19 = (bf16[128,1024]{1,0:T(8,128)(2,1)S(1)}, bf16[128,1024]{1,0:T(8,128)(2,1)}, u32[]{:S(2)}) copy-start(bf16[128,1024]{1,0:T(8,128)(2,1)} %reduce-scatter.11.cloned.1.call-done) | copy-start | bytes 786436
  1018.0 24.1 %copy-start.15 = (f32[128,1024]{1,0:T(8,128)S(1)}, f32[128,1024]{1,0:T(8,128)}, u32[]{:S(2)}) copy-start(f32[128,1024]{1,0:T(8,128)} %param.23) | copy-start | bytes 1572868
  1018.0 24.1 %copy-start.18 = (bf16[128,1024]{1,0:T(8,128)(2,1)S(1)}, bf16[128,1024]{1,0:T(8,128)(2,1)}, u32[]{:S(2)}) copy-start(bf16[128,1024]{1,0:T(8,128)(2,1)} %reduce-scatter.9.cloned.1.call-done) | copy-start | bytes 786436
  1018.0 24.1 %copy-start.26 = (f32[128,1024]{1,0:T(8,128)S(1)}, f32[128,1024]{1,0:T(8,128)}, u32[]{:S(2)}) copy-start(f32[128,1024]{1,0:T(8,128)} %param.24) | copy-start | bytes 1572868
  (46 other events, 443.5 us)
Sparse Core Ops, SparseCore 0:
  12.3 78.6 all-gather.14
  722.1 278.9 all-reduce.2
Sparse Core Ops, SparseCore 1:
  190.5 33.8 all-gather.12
  226.8 47.7 all-gather.10
  277.1 49.2 all-gather.8
  366.1 20.9 all-gather.6
  402.3 31.3 reduce-scatter.6
  436.4 31.3 reduce-scatter.4
  548.8 68.8 reduce-scatter.8
  621.1 66.7 reduce-scatter.10
where the time goes:
time: 1060 us; the launch traced here: 1050 us
  waiting for transfers between devices  554 us (52%)
  local copies, waits for them, and re-layouts  174 us (16%)
  matrix products  139 us (13%)
  other arithmetic  86.9 us (8%)
  blocking collectives  54 us (5%)
  starting transfers between devices  24.1 us (2%)
  between operations  21.4 us (2%)
    psum x1, waiting for transfers between devices, on_device(): lax.psum((attention_local, norm_local, hidden_squares), ('dp', 'head'))  189 us
    all_to_all x1, waiting for transfers between devices, on_device(): lax.all_to_all(pairs, 'head', split_axis=3, concat_axis=0, tiled=True)  123 us
    all_to_all x1, waiting for transfers between devices, on_device(): lax.all_to_all(pair_back, 'head', split_axis=0, concat_axis=3, tiled=True)  96.8 us
    all_gather x1, waiting for transfers between devices, on_device(): lax.all_gather(attention_weights.astype(jnp.bfloat16)[None], ('dp', 'head...  69.6 us
    reshape x2, local copies, waits for them, and re-layouts, on_device(): pairs = pairs.astype(jnp.bfloat16).reshape(images, key_span, 2, width)  45.5 us
    psum x1, blocking collectives, on_device(): lax.psum((attention_local, norm_local, hidden_squares), ('dp', 'head'))  42.4 us
    reduce_scatter x1, waiting for transfers between devices, on_device(): lax.psum_scatter(jnp.dot(hidden_low, reduce_part, preferred_element_type=...  30.9 us
    reduce_scatter x1, waiting for transfers between devices, on_device(): lax.psum_scatter(jnp.einsum('nf,df->nd', before_grad, expand_full, prefer...  24.6 us
  transfers between devices with their start and end apart: 15, of which 8 were waited for; matrix products, arithmetic and copies ran while one was open for 25% of the time, Pallas kernels for 0%

commit v1 on v0

v1 whole, which is shorter than its diff:
```python
import functools

import jax
import jax.numpy as jnp
from jax import lax
from jax.experimental import pallas as pl
from jax.experimental.pallas import tpu as pltpu
from jax.sharding import PartitionSpec as P

D = 1024
HEADS = 16
HEAD = D // HEADS
GROUP = 256
GROUPS = D // GROUP
STEP = 10

LN_EPS = 1e-05
BETA_ONE = 0.9
BETA_TWO = 0.999
ADAM_EPS = 1e-08
MATRIX_RATE = 0.1
NORM_RATE = 0.6
DECAY_RATE = 0.1
MAX_NORM = 0.05

MESH = pl.DeviceIdType.MESH
F32 = jnp.float32
BF16 = jnp.bfloat16
MIB = 2**20


def grid_of(dp_count, head_count):
    x = 1
    while 4 * x * x <= dp_count:
        x *= 2
    return {"z": dp_count // x, "x": x, "y": head_count // 2, "c": 2}


class Links:
    def __init__(self, sizes, send, recv, local):
        self.sizes, self.send, self.recv, self.local = sizes, send, recv, local
        self.used = self.used_local = 0
        dp, head = lax.axis_index("dp"), lax.axis_index("head")
        self.at = {
            "z": lax.div(dp, sizes["x"]),
            "x": lax.rem(dp, sizes["x"]),
            "y": lax.div(head, sizes["c"]),
            "c": lax.rem(head, sizes["c"]),
        }
        self.head = head

    def place(self, axis, k):
        return lax.rem(self.at[axis] + k, self.sizes[axis])

    def peer(self, axis, k):
        at = dict(self.at)
        at[axis] = self.place(axis, k)
        return {
            "dp": at["z"] * self.sizes["x"] + at["x"],
            "head": at["y"] * self.sizes["c"] + at["c"],
        }

    def greet(self):
        barrier = pltpu.get_barrier_semaphore()
        for axis, n in self.sizes.items():
            for k in range(1, n):
                pl.semaphore_signal(
                    barrier, inc=1, device_id=self.peer(axis, k), device_id_type=MESH
                )

    def meet(self):
        barrier = pltpu.get_barrier_semaphore()
        pl.semaphore_wait(barrier, sum(n - 1 for n in self.sizes.values()))

    def copy(self, src, dst, slot, axis, k):
        return pltpu.make_async_remote_copy(
            src_ref=src,
            dst_ref=dst,
            send_sem=self.send.at[slot],
            recv_sem=self.recv.at[slot],
            device_id=self.peer(axis, k),
            device_id_type=MESH,
        )

    def take(self):
        self.used += 1
        return self.used - 1

    def move(self, src, dst):
        self.used_local += 1
        made = pltpu.make_async_copy(src, dst, self.local.at[self.used_local - 1])
        made.start()
        return made


class Gather:
    def __init__(self, links, order, view):
        self.links, self.order, self.view = links, order, view
        self.sent, self.coming = [], {}

    def region(self, step, place):
        at = dict(self.links.at)
        for axis in self.order[:step]:
            at[axis] = None
        at[self.order[step]] = place
        return self.view(at)

    def start(self, step):
        axis, links = self.order[step], self.links
        mine = self.region(step, links.at[axis])
        self.coming[step] = []
        for k in range(1, links.sizes[axis]):
            slot = links.take()
            copy = links.copy(mine, mine, slot, axis, k)
            copy.start()
            self.sent.append(copy)
            lands = self.region(step, links.place(axis, links.sizes[axis] - k))
            self.coming[step].append(links.copy(lands, lands, slot, axis, k))

    def wait(self, step):
        for copy in self.coming[step]:
            copy.wait_recv()

    def go(self, step):
        self.wait(step)
        if step + 1 < len(self.order):
            self.start(step + 1)

    def close(self):
        for copy in self.sent:
            copy.wait_send()


def some(place):
    return slice(None) if place is None else place


def dot(a, b):
    return lax.dot_general(a, b, (((1,), (0,)), ((), ())), preferred_element_type=F32)


def dot_nt(a, b):
    return lax.dot_general(a, b, (((1,), (1,)), ((), ())), preferred_element_type=F32)


def dot_tn(a, b):
    return lax.dot_general(a, b, (((0,), (0,)), ((), ())), preferred_element_type=F32)


def normed(values):
    center = values - jnp.mean(values, axis=-1, keepdims=True)
    scale = lax.rsqrt(jnp.mean(center * center, axis=-1, keepdims=True) + LN_EPS)
    return center * scale, scale


def diagonal(rows):
    n = GROUP // HEAD
    lat = rows.shape[0]
    tall = jnp.concatenate([rows] * n, axis=0)
    row = lax.broadcasted_iota(jnp.int32, tall.shape, 0) // lat
    col = lax.broadcasted_iota(jnp.int32, tall.shape, 1) // HEAD
    return jnp.where(row == col, tall, jnp.zeros_like(tall))


def undiagonal(tall):
    n = GROUP // HEAD
    lat = tall.shape[0] // n
    col = lax.broadcasted_iota(jnp.int32, (lat, GROUP), 1) // HEAD
    total = jnp.where(col == 0, tall[:lat], 0.0)
    for h in range(1, n):
        total = total + jnp.where(col == h, tall[h * lat : (h + 1) * lat], 0.0)
    return total


def weight_block(weights, m, g, sizes):
    block = weights.shape[-1]
    per = GROUP // block
    parts = []
    for s in range(per):
        h = g * per + s
        part = weights[m, lax.div(h, sizes["c"]), lax.rem(h, sizes["c"])]
        parts.append(part.reshape(D, block))
    return parts[0] if per == 1 else jnp.concatenate(parts, axis=1)


def softmax_columns(keys, spread_queries, seen):
    scores = dot_nt(keys, spread_queries)
    scores = jnp.where(seen, scores, -1e30)
    raised = jnp.exp(scores - jnp.max(scores, axis=0, keepdims=True))
    return raised * (1.0 / jnp.sum(raised, axis=0, keepdims=True))


def forward_kernel(
    sizes,
    att_ref,
    expand_ref,
    reduce_ref,
    tokens_ref,
    latents_ref,
    cotangent_ref,
    counts_ref,
    norm_ref,
    att_out,
    ff_out,
    pairs_out,
    turned_out,
    queries_out,
    mixed_out,
    middle_out,
    rows_out,
    back_out,
    att,
    ff,
    tokens,
    inputs,
    turned,
    pairs,
    queries,
    mixed,
    middle,
    rows,
    back,
    send,
    recv,
    local,
):
    links = Links(sizes, send, recv, local)
    links.greet()
    images, patches, _ = tokens.shape
    span = inputs.shape[1]
    lat = span - patches
    at = links.at
    outs = []

    loads = [links.move(tokens_ref.at[i], tokens.at[i]) for i in range(images)]
    for m in range(4):
        att[m, at["y"], at["c"], at["z"], at["x"]] = att_ref[m].astype(BF16)
    back[at["y"], at["c"]] = cotangent_ref[...].astype(BF16)
    ff[0, at["z"], at["x"]] = expand_ref[...].astype(BF16)
    ff[1, at["z"], at["x"]] = reduce_ref[...].astype(BF16)

    half = att.shape[5] // 2

    def att_view(m, s):
        def view(p):
            return att.at[m, some(p["y"]), some(p["c"]), some(p["z"]), some(p["x"]), pl.ds(s * half, half)]

        return view

    def ff_view(m, s):
        def view(p):
            return ff.at[m, some(p["z"]), some(p["x"]), pl.ds(s * half, half)]

        return view

    def back_view(p):
        return back.at[some(p["y"]), some(p["c"])]

    def row_view(i):
        def view(p):
            return rows.at[some(p["y"]), some(p["c"]), pl.ds(i * lat, lat)]

        return view

    query = [Gather(links, "zxyc", att_view(0, 0)), Gather(links, "yzxc", att_view(0, 1))]
    key = [Gather(links, "zxyc", att_view(1, 0)), Gather(links, "yzxc", att_view(1, 1))]
    value = [Gather(links, "zyxc", att_view(2, 0)), Gather(links, "xzyc", att_view(2, 1))]
    output = [Gather(links, "zyxc", att_view(3, 0)), Gather(links, "xzyc", att_view(3, 1))]
    hidden = [
        Gather(links, "zx", ff_view(0, 0)),
        Gather(links, "xz", ff_view(0, 1)),
        Gather(links, "zx", ff_view(1, 0)),
        Gather(links, "xz", ff_view(1, 1)),
    ]
    cotangent = [Gather(links, "yc", back_view)]
    ff_rows = [Gather(links, "yc", row_view(i)) for i in range(images)]
    everything = [*query, *key, *value, *output, *hidden, *cotangent, *ff_rows]

    def start(parts):
        for part in parts:
            part.start(0)

    def go(parts, step):
        for part in parts:
            part.go(step)

    links.meet()
    start(key + value)

    for i in range(images):
        low = normed(latents_ref[pl.ds(i * lat, lat)].astype(F32))[0] * norm_ref[2:3] + norm_ref[3:4]
        inputs[i, pl.ds(patches, lat)] = low.astype(BF16)

    def normalize(i):
        loads[i].wait()
        tile = 64

        def one(t, _):
            part = pl.ds(pl.multiple_of(t * tile, tile), tile)
            low = normed(tokens[i, part].astype(F32))[0] * norm_ref[0:1] + norm_ref[1:2]
            inputs[i, part] = low.astype(BF16)
            return 0

        lax.fori_loop(0, patches // tile, one, 0)

        def turn(t, _):
            part = pl.ds(pl.multiple_of(t * 128, 128), 128)
            turned[i, :, part] = inputs[i, part].T
            return 0

        lax.fori_loop(0, span // 128, turn, 0)
        outs.append(links.move(turned.at[i], turned_out.at[i]))

    normalize(0)
    go(key + value, 0)
    start(query + output)
    if images > 1:
        normalize(1)
    go(key + value, 1)
    go(query + output, 0)
    if images > 2:
        normalize(2)
    go(key + value, 2)
    go(query + output, 1)
    start(cotangent + hidden)
    for i in range(3, images):
        normalize(i)
    go(query + output, 2)
    go(key + value, 3)

    def project(i):
        def one(j, _):
            m = 1 + lax.div(j, GROUPS)
            weight = weight_block(att, m, lax.rem(j, GROUPS), sizes)
            pairs[i, j] = dot(inputs[i], weight).astype(BF16)
            return 0

        lax.fori_loop(0, 2 * GROUPS, one, 0)
        outs.append(links.move(pairs.at[i], pairs_out.at[i]))

    def attend(i):
        position = lax.broadcasted_iota(jnp.int32, (span, GROUP), 0)
        count = counts_ref[links.head * images + i]
        seen = (position < count) | (position >= patches)

        def one(g, _):
            spread = diagonal(queries[g, pl.ds(i * lat, lat)])
            probs = softmax_columns(pairs[i, g], spread, seen).astype(BF16)
            wide = dot_tn(probs, pairs[i, GROUPS + g])
            mixed[g, pl.ds(i * lat, lat)] = undiagonal(wide).astype(BF16)
            return 0

        lax.fori_loop(0, GROUPS, one, 0)

    def finish(i):
        part = pl.ds(i * lat, lat)
        whole = jnp.concatenate([mixed[g, part] for g in range(GROUPS)], axis=1)
        made = jnp.concatenate(
            [dot(whole, weight_block(att, 3, g, sizes)) for g in range(GROUPS)], axis=1
        )
        value = latents_ref[part].astype(F32) + made
        middle[part] = value
        low = normed(value)[0] * norm_ref[4:5] + norm_ref[5:6]
        rows[at["y"], at["c"], part] = low.astype(BF16)
        ff_rows[i].start(0)

    for i in range(images):
        project(i)
        if i == 0:
            go(query + output, 3)
            stack = inputs[:, patches:].reshape(images * lat, D)
            for g in range(GROUPS):
                made = dot(stack, weight_block(att, 0, g, sizes)) * HEAD ** (-0.5)
                queries[g] = made.astype(BF16)
            outs.append(links.move(queries, queries_out))
        if i == 1:
            go(cotangent + hidden, 0)
        attend(i)
        finish(i)
        if i >= 1:
            ff_rows[i - 1].go(0)
    if images == 1:
        go(cotangent + hidden, 0)
    outs.append(links.move(att, att_out))
    outs.append(links.move(mixed, mixed_out))
    outs.append(links.move(middle, middle_out))
    go(cotangent + hidden, 1)
    outs.append(links.move(back, back_out))
    outs.append(links.move(ff, ff_out))
    ff_rows[images - 1].go(0)
    for part in ff_rows:
        part.go(1)
    outs.append(links.move(rows, rows_out))
    for part in everything:
        part.close()
    for out in outs:
        out.wait()


def forward(att, expand, reduce_turned, tokens, latents, cotangent, counts, norm_params):
    sizes = grid_of(lax.axis_size("dp"), lax.axis_size("head"))
    z, x, y, c = (sizes[a] for a in "zxyc")
    images, patches, _ = tokens.shape
    lat = latents.shape[1]
    span = patches + lat
    n = images * lat
    _, row_block, col_block = att.shape
    ff_block = expand.shape[1]
    shapes = dict(
        att=((4, y, c, z, x, row_block, col_block), BF16),
        ff=((2, z, x, row_block, ff_block), BF16),
        pairs=((images, 2 * GROUPS, span, GROUP), BF16),
        turned=((images, D, span), BF16),
        queries=((GROUPS, n, GROUP), BF16),
        mixed=((GROUPS, n, GROUP), BF16),
        middle=((n, D), F32),
        rows=((y, c, n, D), BF16),
        back=((y, c, n, D), BF16),
        tokens=((images, patches, D), BF16),
        inputs=((images, span, D), BF16),
    )
    out_names = ("att", "ff", "pairs", "turned", "queries", "mixed", "middle", "rows", "back")
    scratch_names = (
        "att", "ff", "tokens", "inputs", "turned", "pairs", "queries", "mixed", "middle", "rows", "back",
    )
    per_att = sum(s - 1 for s in sizes.values())
    slots = 8 * per_att + 4 * (z + x - 2) + (1 + images) * (y + c - 2)
    vmem, anywhere = pl.BlockSpec(memory_space=pltpu.VMEM), pl.BlockSpec(memory_space=pl.ANY)
    made = pl.pallas_call(
        functools.partial(forward_kernel, sizes),
        out_shape=[jax.ShapeDtypeStruct(*shapes[k]) for k in out_names],
        in_specs=[vmem, vmem, vmem, anywhere, vmem, vmem, pl.BlockSpec(memory_space=pltpu.SMEM), vmem],
        out_specs=[anywhere] * len(out_names),
        scratch_shapes=[pltpu.VMEM(*shapes[k]) for k in scratch_names]
        + [
            pltpu.SemaphoreType.DMA((slots,)),
            pltpu.SemaphoreType.DMA((slots,)),
            pltpu.SemaphoreType.DMA((3 * images + 8,)),
        ],
        compiler_params=pltpu.CompilerParams(
            collective_id=0, has_side_effects=True, vmem_limit_bytes=58 * MIB
        ),
        name="gather_and_attend",
    )(att, expand, reduce_turned, tokens, latents.reshape(n, D), cotangent.reshape(n, D), counts, norm_params)
    return dict(zip(out_names, made))


def layer_norm(values):
    normed_values, scale = normed(values)
    return normed_values, scale


def norm_back(upstream, hat, scaled, gain_row):
    inner = upstream * gain_row
    result = scaled * (
        inner
        - jnp.mean(inner, axis=-1, keepdims=True)
        - hat * jnp.mean(inner * hat, axis=-1, keepdims=True)
    )
    lead_axes = tuple(range(upstream.ndim - 1))
    return (result, jnp.sum(upstream * hat, axis=lead_axes), jnp.sum(upstream, axis=lead_axes))


def adam_step(master, first, second, gradient, step_rate, decay_rate):
    first_new = BETA_ONE * first + (1.0 - BETA_ONE) * gradient
    second_new = BETA_TWO * second + (1.0 - BETA_TWO) * gradient * gradient
    first_hat = first_new / (1.0 - BETA_ONE**STEP)
    second_hat = second_new / (1.0 - BETA_TWO**STEP)
    master_new = master - step_rate * (
        first_hat / (jnp.sqrt(second_hat) + ADAM_EPS) + decay_rate * master
    )
    return (master_new, first_new, second_new)


def on_device(
    media_tokens, latents, cotangent, counts,
    attention_weights, attention_first, attention_second,
    expand_weight, expand_first, expand_second,
    reduce_weight, reduce_first, reduce_second,
    norm_params, norm_first, norm_second,
):
    dp_count = lax.axis_size("dp")
    head_count = lax.axis_size("head")
    images, patches, width = media_tokens.shape
    lat_rows = latents.shape[1]
    key_span = patches + lat_rows
    n = images * lat_rows
    row_block = attention_weights.shape[1]
    col_block = attention_weights.shape[2]
    got = forward(
        attention_weights, expand_weight, reduce_weight.T, media_tokens, latents, cotangent, counts, norm_params
    )
    full_weights = got["att"].reshape(4, head_count, width, col_block).transpose(0, 2, 1, 3).reshape(4, width, width)
    query_weight, key_weight, value_weight, output_weight = full_weights
    expand_full = got["ff"][0].reshape(width, -1)
    reduce_part = got["ff"][1].reshape(width, -1).T
    rows_all = got["rows"].reshape(-1, width)
    back_all = got["back"].reshape(-1, width)
    middle = got["middle"]
    ff_hat, ff_scale = layer_norm(middle)
    before = jnp.dot(rows_all, expand_full, preferred_element_type=jnp.float32)
    hidden, gelu_back = jax.vjp(jax.nn.gelu, before)
    hidden_low = hidden.astype(jnp.bfloat16)
    added = lax.psum_scatter(
        jnp.dot(hidden_low, reduce_part, preferred_element_type=jnp.float32).astype(jnp.bfloat16),
        "head", scatter_dimension=0, tiled=True,
    ).astype(jnp.float32)
    resampled = (middle + added).reshape(images, lat_rows, width).astype(jnp.bfloat16)
    reduce_grad = jnp.einsum("nf,nd->df", hidden_low, back_all, preferred_element_type=jnp.float32)
    hidden_grad = jnp.einsum("nd,fd->nf", back_all, reduce_part, preferred_element_type=jnp.float32)
    before_grad = gelu_back(hidden_grad)[0].astype(jnp.bfloat16)
    expand_grad = jnp.einsum("nd,nf->df", rows_all, before_grad, preferred_element_type=jnp.float32)
    ff_back = lax.psum_scatter(
        jnp.einsum("nf,df->nd", before_grad, expand_full, preferred_element_type=jnp.float32).astype(jnp.bfloat16),
        "head", scatter_dimension=0, tiled=True,
    ).astype(jnp.float32)
    middle_part, ff_gain_grad, ff_shift_grad = norm_back(ff_back, ff_hat, ff_scale, norm_params[4])
    middle_grad = cotangent.reshape(n, width) + middle_part
    expand_share = lax.psum_scatter(
        expand_grad.astype(jnp.bfloat16), "dp", scatter_dimension=0, tiled=True
    ).astype(jnp.float32)
    reduce_share = lax.psum_scatter(
        reduce_grad.astype(jnp.bfloat16), "dp", scatter_dimension=0, tiled=True
    ).astype(jnp.float32).T
    hidden_squares = jnp.sum(expand_share * expand_share) + jnp.sum(reduce_share * reduce_share)
    branch_low = middle_grad.astype(jnp.bfloat16)
    mixed = got["mixed"].transpose(1, 0, 2).reshape(n, width)
    output_grad = jnp.einsum("nc,nd->cd", mixed, branch_low, preferred_element_type=jnp.float32)
    mixed_grad = jnp.einsum("nd,cd->nc", branch_low, output_weight, preferred_element_type=jnp.float32).astype(jnp.bfloat16)
    pairs = got["pairs"].transpose(0, 2, 1, 3).reshape(images, key_span, 2, HEADS, HEAD)
    keys, values = pairs[:, :, 0], pairs[:, :, 1]
    queries = got["queries"].transpose(1, 0, 2).reshape(images, lat_rows, HEADS, HEAD)
    lengths = lax.dynamic_slice(counts, (lax.axis_index("head") * images,), (images,))
    positions = jnp.arange(key_span, dtype=jnp.int32)
    visible = (positions[None, :] < lengths[:, None]) | (positions[None, :] >= patches)
    scores = jnp.einsum("eqhc,ekhc->ehqk", queries, keys, preferred_element_type=jnp.float32)
    exact = jax.nn.softmax(jnp.where(visible[:, None, None, :], scores, -1e30), axis=-1)
    softened = exact.astype(jnp.bfloat16)
    mixed_heads = mixed_grad.reshape(images, lat_rows, HEADS, HEAD)
    prob_grad = jnp.einsum("eqhc,ekhc->ehqk", mixed_heads, values, preferred_element_type=jnp.float32)
    score_grad = (exact * (prob_grad - jnp.sum(exact * prob_grad, axis=-1, keepdims=True))).astype(jnp.bfloat16)
    query_rows = (jnp.einsum("ehqk,ekhc->eqhc", score_grad, keys, preferred_element_type=jnp.float32) * HEAD**-0.5).astype(jnp.bfloat16).reshape(n, width)
    key_back = jnp.einsum("ehqk,eqhc->ekhc", score_grad, queries, preferred_element_type=jnp.float32).astype(jnp.bfloat16).reshape(images * key_span, width)
    value_back = jnp.einsum("ehqk,eqhc->ekhc", softened, mixed_heads, preferred_element_type=jnp.float32).astype(jnp.bfloat16).reshape(images * key_span, width)
    inputs_turned = got["turned"].transpose(1, 0, 2).reshape(width, -1)
    key_grad = jnp.dot(inputs_turned, key_back, preferred_element_type=jnp.float32)
    value_grad = jnp.dot(inputs_turned, value_back, preferred_element_type=jnp.float32)
    latent_hat, latent_scale = layer_norm(latents.astype(jnp.float32))
    latent_low = got["turned"][:, :, patches:].transpose(0, 2, 1).reshape(n, width)
    query_grad = jnp.einsum("nd,ne->de", latent_low, query_rows, preferred_element_type=jnp.float32)
    pair_input_grad = (
        jnp.einsum("ne,de->nd", key_back, key_weight, preferred_element_type=jnp.float32)
        + jnp.einsum("ne,de->nd", value_back, value_weight, preferred_element_type=jnp.float32)
    ).reshape(images, key_span, width)
    latent_side = pair_input_grad[:, patches:] + jnp.einsum(
        "ne,de->nd", query_rows, query_weight, preferred_element_type=jnp.float32
    ).reshape(images, lat_rows, width)
    media_hat, media_scale = layer_norm(media_tokens.astype(jnp.float32))
    media_back, media_gain_grad, media_shift_grad = norm_back(pair_input_grad[:, :patches], media_hat, media_scale, norm_params[0])
    latent_back, latent_gain_grad, latent_shift_grad = norm_back(latent_side, latent_hat, latent_scale, norm_params[2])
    media_grad = media_back.astype(jnp.bfloat16)
    latent_grad = (middle_grad.reshape(images, lat_rows, width) + latent_back).astype(jnp.bfloat16)
    attention_local = jnp.stack([query_grad, key_grad, value_grad, output_grad])
    norm_local = jnp.stack([media_gain_grad, media_shift_grad, latent_gain_grad, latent_shift_grad, ff_gain_grad, ff_shift_grad])
    arranged = attention_local.astype(jnp.bfloat16).reshape(4, dp_count, row_block, head_count, col_block).transpose(1, 3, 0, 2, 4)
    arranged = arranged.reshape(dp_count * head_count, 4, row_block, col_block)
    attention_share = lax.psum_scatter(arranged, ("dp", "head"), scatter_dimension=0, tiled=True)[0].astype(jnp.float32)
    squares_here = hidden_squares + jnp.sum(attention_share * attention_share)
    norm_total, squares_total = lax.psum((norm_local, squares_here), ("dp", "head"))
    grad_norm = jnp.sqrt(squares_total + jnp.sum(norm_total * norm_total))
    clip_factor = jnp.minimum(1.0, MAX_NORM / (grad_norm + 1e-06))
    attention = adam_step(attention_weights, attention_first, attention_second, attention_share * clip_factor, MATRIX_RATE, DECAY_RATE)
    expand = adam_step(expand_weight, expand_first, expand_second, expand_share * clip_factor, MATRIX_RATE, DECAY_RATE)
    reduce = adam_step(reduce_weight, reduce_first, reduce_second, reduce_share * clip_factor, MATRIX_RATE, DECAY_RATE)
    norm = adam_step(norm_params, norm_first, norm_second, norm_total * clip_factor, NORM_RATE, 0.0)
    return (resampled, media_grad, latent_grad, grad_norm, *attention, *expand, *reduce, *norm)


def solution(mesh):
    in_specs = (
        P(("dp", "head"), None, None),
        P(("dp", "head"), None, None),
        P(("dp", "head"), None, None),
        P("dp"),
        P(None, "dp", "head"),
        P(None, "dp", "head"),
        P(None, "dp", "head"),
        P("dp", "head"),
        P("dp", "head"),
        P("dp", "head"),
        P("head", "dp"),
        P("head", "dp"),
        P("head", "dp"),
        P(),
        P(),
        P(),
    )
    out_specs = (
        P(("dp", "head"), None, None),
        P(("dp", "head"), None, None),
        P(("dp", "head"), None, None),
        P(),
        P(None, "dp", "head"),
        P(None, "dp", "head"),
        P(None, "dp", "head"),
        P("dp", "head"),
        P("dp", "head"),
        P("dp", "head"),
        P("head", "dp"),
        P("head", "dp"),
        P("head", "dp"),
        P(),
        P(),
        P(),
    )
    return jax.shard_map(
        on_device, mesh=mesh, in_specs=in_specs, out_specs=out_specs, check_vma=False
    )
```

time: 1060 us -> 572 us (0.54)
  waiting for transfers between devices: 554 us -> 81.8 us
  Pallas kernels: 0 us -> 112 us
  local copies, waits for them, and re-layouts: 174 us -> 122 us
  matrix products: 139 us -> 104 us
  other arithmetic: 86.9 us -> 54.7 us
  starting transfers between devices: 24.1 us -> 0.21 us
  blocking collectives: 54 us -> 67.4 us
    all_to_all x5 -> x0, waiting for transfers between devices: 225 us -> none  [the longest x1 123 us: on_device(): lax.all_to_all(pairs, 'head', split_axis=3, concat_axis=0, tiled=True)]
    psum x1 -> x0, waiting for transfers between devices: 189 us -> none  [on_device(): lax.psum((attention_local, norm_local, hidden_squares), ('dp', 'head'))]
    pallas_call x0 -> x1, Pallas kernels: none -> 112 us  [forward(): pl.pallas_call(functools.partial(forward_kernel, sizes), out_shape=[jax.S...]
    all_gather x5 -> x0, waiting for transfers between devices: 83.9 us -> none  [the longest x1 69.6 us: on_device(): lax.all_gather(attention_weights.astype(jnp.bfloat16)[None], ('dp', 'head...]
    reduce_scatter x0 -> x1, waiting for transfers between devices: none -> 79.7 us  [on_device(): lax.psum_scatter(arranged, ('dp', 'head'), scatter_dimension=0, tiled=True)]
    reshape x9 -> x7, local copies, waits for them, and re-layouts: 97.2 us -> 29.8 us  [the longest x1 11.6 us: on_device(): got['att'].reshape(4, head_count, width, col_block).transpose(0, 2, 1, 3)]
    reduce_scatter x1, waiting for transfers between devices: 30.9 us -> 0.02 us  [on_device(): lax.psum_scatter(jnp.dot(hidden_low, reduce_part, preferred_element_type=...]
    all_to_all x7 -> x0, local copies, waits for them, and re-layouts: 30.5 us -> none  [the longest x1 18.2 us: on_device(): lax.all_to_all(pair_back, 'head', split_axis=0, concat_axis=3, tiled=True)]
  transfers between devices with their start and end apart: 15 -> 5, of which waited for: 8 -> 2; matrix products, arithmetic and copies ran while one was open for 25% -> 44% of each run, Pallas kernels for 0% -> 0%
where the time goes in v1:
time: 572 us; the launch traced here: 560 us
  local copies, waits for them, and re-layouts  122 us (21%)
  Pallas kernels  112 us (20%)
  matrix products  104 us (18%)
  waiting for transfers between devices  81.8 us (14%)
  blocking collectives  67.4 us (12%)
  other arithmetic  54.7 us (10%)
  between operations  19.3 us (3%)
    pallas_call x1, Pallas kernels, forward(): pl.pallas_call(functools.partial(forward_kernel, sizes), out_shape=[jax.S...  112 us
    reduce_scatter x1, waiting for transfers between devices, on_device(): lax.psum_scatter(arranged, ('dp', 'head'), scatter_dimension=0, tiled=True)  79.7 us
    psum x1, blocking collectives, on_device(): lax.psum((norm_local, squares_here), ('dp', 'head'))  67.4 us
    unnamed x97, local copies, waits for them, and re-layouts  26.1 us
    transpose x1, local copies, waits for them, and re-layouts, on_device(): got['pairs'].transpose(0, 2, 1, 3).reshape(images, key_span, 2, HEADS, HEAD)  15.1 us
    dot_general x1, matrix products, on_device(): jnp.einsum('ne,de->nd', value_back, value_weight, preferred_element_type=...  12.5 us
    reshape x1, local copies, waits for them, and re-layouts, on_device(): got['att'].reshape(4, head_count, width, col_block).transpose(0, 2, 1, 3)  11.6 us
  transfers between devices with their start and end apart: 5, of which 2 were waited for; matrix products, arithmetic and copies ran while one was open for 44% of the time, Pallas kernels for 0%

profile of v1, /device:TPU:10, one launch (start us, length us, event | category | flops | bytes accessed | tf_op | source)
XLA Modules:
  0.0 560.4 jit_solution(5956354248521667323)
XLA Ops:
  9.3 111.5 %gather_and_attend.1 = (bf16[4,2,2,4,2,128,256]{6,5,4,3,2,1,0:T(8,128)(2,1)}, bf16[2,4,2,128,1024]{4,3,2,1,0:T(8,128)(2,1)}, bf16[4,8,640,256]{3,2,1,0:T(8,128)(...) custom-call(f32[4,128,256]{2,1,0:T(8,128)} %att_ref.1, ...), custom_call_target="tpu_custom_call" | custom-call | tf_op jit(solution)/shard_map/gather_and_attend/pallas_call | solution.py:429
  126.2 6.2 %fusion.29 = (bf16[1024,1024]{1,0:T(8,128)(2,1)S(1)}, f32[1024,1024]{1,0:T(8,128)}) fusion(f32[1024,1024]{1,0:T(8,128)S(1)} %fusion.82, bf16[1024,1024]{1,0:T(8,128)(2,1)S(1)} %bitcast.248, bf16[1024,1024]{1,0:T(8,128)(2,1)S(1)} %bitcast.228), kind=kOutput, calls=%fused_computation.44 | convolution fusion | flops 2168455168 | bytes 14680064 | tf_op jit(solution)/shard_map/dot_general | solution.py:501
  137.5 6.2 %convolution_convert_fusion.3 = bf16[1024,1024]{1,0:T(8,128)(2,1)} fusion(bf16[1024,1024]{1,0:T(8,128)(2,1)S(1)} %bitcast.227, f32[1024,1024]{1,0:T(8,128)} %get-tuple-element.105), kind=kOutput, calls=%fused_computation.54 | convolution fusion | flops 2157969408 | bytes 8388608 | tf_op jit(solution)/shard_map/dot_general | solution.py:505
  143.8 7.1 %convolution_convert_fusion = bf16[1024,1024]{1,0:T(8,128)(2,1)} fusion(bf16[1024,1024]{1,0:T(8,128)(2,1)} %bitcast.249, f32[1024,1024]{1,0:T(8,128)} %get-tuple-element.105), kind=kOutput, calls=%fused_computation.51 | convolution fusion | flops 2157969408 | bytes 8388608 | tf_op jit(solution)/shard_map/nf,nd->df/dot_general | solution.py:509
  151.0 6.0 %convolution_convert_fusion.1 = bf16[1024,1024]{1,0:T(8,128)(2,1)} fusion(bf16[1024,1024]{1,0:T(8,128)(2,1)} %bitcast.247, bf16[1024,1024]{1,0:T(8,128)(2,1)} %copy-done.30), kind=kOutput, calls=%fused_computation.52 | convolution fusion | flops 2148532224 | bytes 6291456 | tf_op jit(solution)/shard_map/nd,nf->df/dot_general | solution.py:512
  170.8 7.9 %copy.65 = bf16[1024,4,640]{0,2,1:T(8,128)(2,1)} copy(bf16[1024,4,640]{2,0,1:T(8,128)(2,1)} %bitcast.211) | data formatting | bytes 10485760 | tf_op jit(solution)/shard_map/transpose | solution.py:545
  178.7 6.5 %copy.94 = bf16[320,8,8,128]{3,2,1,0:T(8,128)(2,1)} copy(bf16[320,8,8,128]{3,1,2,0:T(8,128)(2,1)} %bitcast.199) | data formatting | bytes 10485760
  185.2 8.2 %copy.80 = bf16[8,128,2560,1]{2,1,3,0:T(8,128)(2,1)} copy(bf16[8,128,2560,1]{1,0,2,3:T(8,128)(2,1)} %bitcast.200) | data formatting | bytes 10485760 | tf_op jit(solution)/shard_map/reshape.166
  193.4 11.6 %copy.52 = bf16[4,4,1024,256]{2,3,1,0:T(8,128)(2,1)} copy(bf16[4,4,1024,256]{3,2,1,0:T(8,128)(2,1)} %bitcast.208) | data formatting | bytes 16777216 | tf_op jit(solution)/shard_map/reshape | solution.py:493
  205.0 6.0 %fusion.78 = (bf16[1,1024,4,256]{1,3,2,0:T(8,128)(2,1)}, bf16[1,1024,4,256]{1,3,2,0:T(8,128)(2,1)}, bf16[1,1024,4,256]{1,3,2,0:T(8,128)(2,1)}, bf16[1,1024,4,256]{1,3,2,0:T(8,128)(2,1)}) fusion(bf16[4,1024,4,256]{1,3,2,0:T(8,128)(2,1)} %bitcast.192), kind=kLoop, calls=%fused_computation.136 | loop fusion | bytes 16777216 | tf_op jit(solution)/shard_map/unstack | solution.py:494
  211.0 15.1 %copy.49 = bf16[4,640,8,256]{1,3,2,0:T(8,128)(2,1)} copy(bf16[4,640,8,256]{3,1,2,0:T(8,128)(2,1)} %bitcast.206) | data formatting | bytes 20971520 | tf_op jit(solution)/shard_map/transpose | solution.py:530
  230.2 5.3 fusion.81
  245.5 8.4 %convert_bitcast_fusion = bf16[4,640,16,64]{1,3,2,0:T(8,128)(2,1)} fusion(bf16[4,64,16,64]{1,3,2,0:T(8,128)(2,1)} %copy.57, f32[4,16,64,640]{3,2,1,0:T(8,128)} %get-tuple-element.107, f32[4,16,64]{2,1,0:T(8,128)S(1)} %get-tuple-element.106), kind=kOutput, calls=%fused_computation.29 | convolution fusion | flops 343408640 | bytes 16269312 | tf_op jit(solution)/shard_map/ehqk,eqhc->ekhc/dot_general | solution.py:544
  253.9 7.2 %multiply_reduce_fusion = (f32[4,16,64]{2,1,0:T(8,128)S(1)}, f32[4,16,64,640]{3,2,1,0:T(8,128)}) fusion(f32[4,16,64,640]{3,2,1,0:T(8,128)S(1)} %bitcast.186, f32[4,16,64]{2,1,0:T(8,128)S(1)} %get-tuple-element.106, bf16[4,64,16,64]{1,3,2,0:T(8,128)(2,1)S(1)} %copy-done.18, bf16[4,640,2,16,64]{1,4,3,2,0:T(8,128)(2,1)} %bitcast.195), kind=kOutput, calls=%fused_computation.9 | convolution fusion | flops 343404544 | bytes 26771456 | tf_op jit(solution)/shard_map/eqhc,ekhc->ehqk/dot_general | solution.py:540
  263.2 7.0 %copy.58 = bf16[4,640,16,64]{1,0,3,2:T(4,128)(2,1)S(1)} copy(bf16[4,640,16,64]{1,3,2,0:T(8,128)(2,1)} %convert_bitcast_fusion) | data formatting | bytes 10485760 | tf_op jit(solution)/shard_map/convert_element_type | solution.py:544
  273.5 5.7 %multiply_convert_fusion = bf16[4,16,64,640]{3,2,1,0:T(8,128)(2,1)S(1)} fusion(f32[4,16,64,640]{3,2,1,0:T(8,128)} %get-tuple-element.109, f32[4,16,64]{2,1,0:T(8,128)S(1)} %get-tuple-element.108, f32[4,16,64,640]{3,2,1,0:T(8,128)S(1)} %bitcast.188, f32[4,16,64]{2,1,0:T(8,128)S(1)} %get-tuple-element.106), kind=kLoop, calls=%fused_computation.8 | loop fusion | flops 10485760 | bytes 26247168 | tf_op jit(solution)/shard_map/convert_element_type | solution.py:541
  290.9 10.3 %convert_bitcast_fusion.3 = bf16[1,8,128,4,256]{4,2,3,1,0:T(8,128)(2,1)} fusion(bf16[8,128,2560,1]{2,1,3,0:T(8,128)(2,1)} %copy.80, bf16[4,256,2560,1]{2,1,0,3:T(8,128)(2,1)} %bitcast.214), kind=kOutput, calls=%fused_computation.47 | convolution fusion | flops 5369757696 | bytes 12582912 | tf_op jit(solution)/shard_map/dot_general | solution.py:547
  312.0 7.8 %convert_bitcast_fusion.4 = bf16[1,8,128,4,256]{4,2,3,1,0:T(8,128)(2,1)S(1)} fusion(bf16[8,128,2560,1]{2,1,3,0:T(8,128)(2,1)} %copy.80, bf16[4,256,2560,1]{2,1,0,3:T(8,128)(2,1)S(1)} %bitcast.217), kind=kOutput, calls=%fused_computation.48 | convolution fusion | flops 5369757696 | bytes 12582912 | tf_op jit(solution)/shard_map/dot_general | solution.py:546
  323.6 7.9 %copy.70 = bf16[32,4,128,256]{3,2,1,0:T(8,128)(2,1)} copy(bf16[32,4,128,256]{3,2,0,1:T(8,128)(2,1)} %bitcast.193) | data formatting | bytes 16777216 | tf_op jit(solution)/shard_map/reshape | solution.py:566
  349.7 11.3 %fusion.83 = f32[2560,1024]{1,0:T(8,128)} fusion(bf16[2560,1024]{0,1:T(8,128)(2,1)} %bitcast.216, bf16[1024,1024]{0,1:T(8,128)(2,1)} %bitcast.231), kind=kOutput, calls=%fused_computation.141 | convolution fusion | flops 5368709120 | bytes 17825792 | tf_op jit(solution)/shard_map/ne,de->nd/dot_general | solution.py:552
  361.0 12.5 %convolution_add_fusion = f32[2560,1024]{1,0:T(8,128)S(1)} fusion(f32[2560,1024]{1,0:T(8,128)} %fusion.83, bf16[2560,1024]{0,1:T(8,128)(2,1)} %bitcast.215, bf16[1024,1024]{0,1:T(8,128)(2,1)S(1)} %bitcast.230), kind=kOutput, calls=%fused_computation.23 | convolution fusion | flops 5371330560 | bytes 28311552 | tf_op jit(solution)/shard_map/ne,de->nd/dot_general | solution.py:553
  380.3 9.2 %fusion.9 = bf16[4,576,1024]{2,1,0:T(8,128)(2,1)} fusion(bf16[4,576,1024]{2,1,0:T(8,128)(2,1)} %tokens_ref.1, f32[4,640,1024]{2,1,0:T(8,128)} %bitcast.191, f32[4,576]{1,0:T(4,128)S(1)} %broadcast_multiply_fusion, f32[4,576]{1,0:T(4,128)S(1)} %broadcast_multiply_fusion.1, f32[1024]{0:T(1024)S(1)} %bitcast.238, f32[4,576]{1,0:T(4,128)S(1)} %add_rsqrt_fusion, ...), kind=kLoop, calls=%fused_computation.14 | loop fusion | flops 21233664 | bytes 18915328 | tf_op jit(solution)/shard_map/convert_element_type | solution.py:561
  389.5 79.7 %reduce-scatter.14.cloned.1.call-done = bf16[1,4,128,256]{3,2,1,0:T(8,128)(2,1)} async-done(((bf16[32,4,128,256]{3,2,1,0:T(8,128)(2,1)}), bf16[1,4,128,256]{3,2,1,0:T(8,128)(2,1)}) %reduce-scatter.14.cloned.1.call-update) | async-done | bytes 262160 | tf_op jit(solution)/shard_map/reduce_scatter | solution.py:567
  472.8 67.4 %all-reduce = (f32[]{:T(128)}, f32[6,1024]{1,0:T(8,128)S(1)}) all-reduce(f32[]{:T(128)S(6)} %add.159, f32[6,1024]{1,0:T(8,128)S(1)} %stack.35), channel_id=1, replica_groups=mesh['dp'=8,'head'=4] {'dp','head'}, use_global_device_ids=true, to_apply=%region_23.24 | all-reduce | flops 6145 | bytes 49160 | tf_op jit(solution)/shard_map/psum | solution.py:569
  (174 shorter events, 109.1 us)
Async XLA Ops:
  7.2 228.4 %reduce-scatter.8.cloned.1.call-start = ((), (), s32[]{:S(2)}) async-start(), calls=%async_computation.6 | async-start | bytes 2621440 | tf_op jit(solution)/shard_map/reduce_scatter | solution.py:513
  137.5 99.7 %reduce-scatter.6.cloned.1.call-start = ((), (), s32[]{:S(2)}) async-start(), calls=%async_computation.5 | async-start | bytes 2621440 | tf_op jit(solution)/shard_map/reduce_scatter | solution.py:504
  143.8 199.1 %reduce-scatter.12.cloned.1.call-start = ((), (), s32[]{:S(2)}) async-start(), calls=%async_computation.8 | async-start | bytes 2359296 | tf_op jit(solution)/shard_map/reduce_scatter | solution.py:522
  150.9 195.7 %reduce-scatter.10.cloned.1.call-start = ((), (), s32[]{:S(2)}) async-start(), calls=%async_computation.7 | async-start | bytes 2359296 | tf_op jit(solution)/shard_map/reduce_scatter | solution.py:519
  157.0 312.2 %reduce-scatter.14.cloned.1.call-start = ((), (), s32[]{:S(2)}) async-start(), calls=%async_computation.9 | async-start | bytes 8650752 | tf_op jit(solution)/shard_map/reduce_scatter | solution.py:567
  163.2 63.0 %copy-start.4 = (bf16[4,64,16,64]{1,3,2,0:T(8,128)(2,1)}, bf16[4,64,16,64]{1,3,2,0:T(8,128)(2,1)S(1)}, u32[]{:S(2)}) copy-start(bf16[4,64,16,64]{1,3,2,0:T(8,128)(2,1)S(1)} %copy.55) | copy-start | bytes 1572868
  242.6 11.3 %slice-start.2 = ((s8[10485760]{0:T(1024)(128)(4,1)}), s8[2097152]{0:T(1024)(128)(4,1)S(1)}, s32[]{:S(2)}) async-start(s8[10485760]{0:T(1024)(128)(4,1)} %bitcast.185), calls=%async_computation.12 | async-start | bytes 4194304
  263.2 10.2 %slice-start.6 = ((s8[10485760]{0:T(1024)(128)(4,1)}), s8[2097152]{0:T(1024)(128)(4,1)S(1)}, s32[]{:S(2)}) async-start(s8[10485760]{0:T(1024)(128)(4,1)} %bitcast.187), calls=%async_computation.16 | async-start | bytes 4194304
  287.5 13.8 %slice-start.8 = ((s8[10485760]{0:T(1024)(128)(4,1)}), s8[4194304]{0:T(1024)(128)(4,1)S(1)}, s32[]{:S(2)}) async-start(s8[10485760]{0:T(1024)(128)(4,1)} %bitcast.196), calls=%async_computation.18 | async-start | bytes 8388608
  287.5 13.8 %slice-start.11 = ((s8[5242880]{0:T(1024)(128)(4,1)}), s8[1048576]{0:T(1024)(128)(4,1)S(1)}, s32[]{:S(2)}) async-start(s8[5242880]{0:T(1024)(128)(4,1)} %bitcast.203), calls=%async_computation.21 | async-start | bytes 2097152
  290.9 10.3 %slice-start.9 = ((s8[10485760]{0:T(1024)(128)(4,1)}), s8[4194304]{0:T(1024)(128)(4,1)S(1)}, s32[]{:S(2)}) async-start(s8[10485760]{0:T(1024)(128)(4,1)} %bitcast.196), calls=%async_computation.19 | async-start | bytes 8388608
  290.9 10.3 %slice-start.10 = ((s8[10485760]{0:T(1024)(128)(4,1)}), s8[2097152]{0:T(1024)(128)(4,1)S(1)}, s32[]{:S(2)}) async-start(s8[10485760]{0:T(1024)(128)(4,1)} %bitcast.196), calls=%async_computation.20 | async-start | bytes 4194304
  290.9 10.3 %slice-start.12 = ((s8[5242880]{0:T(1024)(128)(4,1)}), s8[4194304]{0:T(1024)(128)(4,1)S(1)}, s32[]{:S(2)}) async-start(s8[5242880]{0:T(1024)(128)(4,1)} %bitcast.203), calls=%async_computation.22 | async-start | bytes 8388608
  349.7 11.3 %copy-start.14 = (bf16[1,1024,4,256]{1,3,2,0:T(8,128)(2,1)S(1)}, bf16[1,1024,4,256]{1,3,2,0:T(8,128)(2,1)}, u32[]{:S(2)}) copy-start(bf16[1,1024,4,256]{1,3,2,0:T(8,128)(2,1)} %get-tuple-element.95) | copy-start | bytes 6291460
  360.9 15.0 %slice-start = ((s8[4718592]{0:T(1024)(128)(4,1)}), s8[4194304]{0:T(1024)(128)(4,1)S(1)}, s32[]{:S(2)}) async-start(s8[4718592]{0:T(1024)(128)(4,1)} %bitcast.183), calls=%async_computation.10 | async-start | bytes 8388608
  360.9 12.5 %copy-start.6 = (bf16[1,1024,4,256]{1,3,2,0:T(8,128)(2,1)S(1)}, bf16[1,1024,4,256]{1,3,2,0:T(8,128)(2,1)}, u32[]{:S(2)}) copy-start(bf16[1,1024,4,256]{1,3,2,0:T(8,128)(2,1)} %get-tuple-element.94) | copy-start | bytes 6291460
  361.0 12.6 %copy-start.24 = (f32[1,1024]{1,0:T(1,128)S(1)}, f32[1,1024]{1,0:T(1,128)}, u32[]{:S(2)}) copy-start(f32[1,1024]{1,0:T(1,128)} %get-tuple-element.101) | copy-start | bytes 12292
  361.0 15.0 %slice-start.1 = ((s8[4718592]{0:T(1024)(128)(4,1)}), s8[524288]{0:T(1024)(128)(4,1)S(1)}, s32[]{:S(2)}) async-start(s8[4718592]{0:T(1024)(128)(4,1)} %bitcast.183), calls=%async_computation.11 | async-start | bytes 1048576
  380.3 91.2 %copy-start.8 = (f32[4,64,1024]{2,1,0:T(8,128)S(1)}, f32[4,64,1024]{2,1,0:T(8,128)}, u32[]{:S(2)}) copy-start(f32[4,64,1024]{2,1,0:T(8,128)} %get-tuple-element.110) | copy-start | bytes 3145732
  380.3 161.9 %copy-start.10 = (f32[1024,128]{0,1:T(8,128)S(1)}, f32[1024,128]{0,1:T(8,128)}, u32[]{:S(2)}) copy-start(f32[1024,128]{0,1:T(8,128)} %copy.47) | copy-start | bytes 1572868
  471.5 75.4 %copy-start.23 = (f32[6,1024]{1,0:T(8,128)S(1)}, f32[6,1024]{1,0:T(8,128)}, u32[]{:S(2)}) copy-start(f32[6,1024]{1,0:T(8,128)} %norm_ref.1) | copy-start | bytes 73732
  471.5 75.4 %copy-start.26 = (f32[6,1024]{1,0:T(8,128)S(1)}, f32[6,1024]{1,0:T(8,128)}, u32[]{:S(2)}) copy-start(f32[6,1024]{1,0:T(8,128)} %param.30) | copy-start | bytes 73732
  472.8 75.6 %copy-start.11 = (f32[128,1024]{1,0:T(8,128)S(1)}, f32[128,1024]{1,0:T(8,128)}, u32[]{:S(2)}) copy-start(f32[128,1024]{1,0:T(8,128)} %expand_ref.1) | copy-start | bytes 1572868
  472.8 75.6 %copy-start.16 = (bf16[128,1024]{1,0:T(8,128)(2,1)S(1)}, bf16[128,1024]{1,0:T(8,128)(2,1)}, u32[]{:S(2)}) copy-start(bf16[128,1024]{1,0:T(8,128)(2,1)} %reduce-scatter.10.cloned.1.call-done) | copy-start | bytes 786436
  (25 other events, 132.6 us)
Sparse Core Ops, SparseCore 0:
  137.6 33.8 reduce-scatter.7
  174.2 31.4 reduce-scatter.5
  209.2 67.2 reduce-scatter.11
  279.8 66.7 reduce-scatter.9
  348.8 120.3 reduce-scatter.13

commit v2 on v1

v2 whole, which is shorter than its diff:
```python
import functools
from types import SimpleNamespace

import jax
import jax.numpy as jnp
from jax import lax
from jax.experimental import pallas as pl
from jax.experimental.pallas import tpu as pltpu
from jax.sharding import PartitionSpec as P

D = 1024
HEADS = 16
HEAD = D // HEADS
GROUP = 256
GROUPS = D // GROUP
STEP = 10

LN_EPS = 1e-05
BETA_ONE = 0.9
BETA_TWO = 0.999
ADAM_EPS = 1e-08
MATRIX_RATE = 0.1
NORM_RATE = 0.6
DECAY_RATE = 0.1
MAX_NORM = 0.05

MESH = pl.DeviceIdType.MESH
F32 = jnp.float32
BF16 = jnp.bfloat16
MIB = 2**20


def grid_of(dp_count, head_count):
    x = 1
    while 4 * x * x <= dp_count:
        x *= 2
    return {"z": dp_count // x, "x": x, "y": head_count // 2, "c": 2}


class Links:
    def __init__(self, sizes, send, recv, local):
        self.sizes, self.send, self.recv, self.local = sizes, send, recv, local
        self.used = self.used_local = 0
        dp, head = lax.axis_index("dp"), lax.axis_index("head")
        self.at = {
            "z": lax.div(dp, sizes["x"]),
            "x": lax.rem(dp, sizes["x"]),
            "y": lax.div(head, sizes["c"]),
            "c": lax.rem(head, sizes["c"]),
        }
        self.head = head

    def place(self, axis, k):
        return lax.rem(self.at[axis] + k, self.sizes[axis])

    def peer(self, axis, k):
        at = dict(self.at)
        at[axis] = self.place(axis, k)
        return {
            "dp": at["z"] * self.sizes["x"] + at["x"],
            "head": at["y"] * self.sizes["c"] + at["c"],
        }

    def greet(self):
        barrier = pltpu.get_barrier_semaphore()
        for axis, n in self.sizes.items():
            for k in range(1, n):
                pl.semaphore_signal(
                    barrier, inc=1, device_id=self.peer(axis, k), device_id_type=MESH
                )

    def meet(self):
        barrier = pltpu.get_barrier_semaphore()
        pl.semaphore_wait(barrier, sum(n - 1 for n in self.sizes.values()))

    def copy(self, src, dst, slot, axis, k):
        return pltpu.make_async_remote_copy(
            src_ref=src,
            dst_ref=dst,
            send_sem=self.send.at[slot],
            recv_sem=self.recv.at[slot],
            device_id=self.peer(axis, k),
            device_id_type=MESH,
        )

    def take(self):
        self.used += 1
        return self.used - 1

    def move(self, src, dst):
        self.used_local += 1
        made = pltpu.make_async_copy(src, dst, self.local.at[self.used_local - 1])
        made.start()
        return made


class Gather:
    def __init__(self, links, order, view):
        self.links, self.order, self.view = links, order, view
        self.sent, self.coming = [], {}

    def region(self, step, place):
        at = dict(self.links.at)
        for axis in self.order[:step]:
            at[axis] = None
        at[self.order[step]] = place
        return self.view(at)

    def start(self, step):
        axis, links = self.order[step], self.links
        mine = self.region(step, links.at[axis])
        self.coming[step] = []
        for k in range(1, links.sizes[axis]):
            slot = links.take()
            copy = links.copy(mine, mine, slot, axis, k)
            copy.start()
            self.sent.append(copy)
            lands = self.region(step, links.place(axis, links.sizes[axis] - k))
            self.coming[step].append(links.copy(lands, lands, slot, axis, k))

    def wait(self, step):
        for copy in self.coming[step]:
            copy.wait_recv()

    def go(self, step):
        self.wait(step)
        if step + 1 < len(self.order):
            self.start(step + 1)

    def close(self):
        for copy in self.sent:
            copy.wait_send()


def some(place):
    return slice(None) if place is None else place


def dot(a, b):
    return lax.dot_general(a, b, (((1,), (0,)), ((), ())), preferred_element_type=F32)


def dot_nt(a, b):
    return lax.dot_general(a, b, (((1,), (1,)), ((), ())), preferred_element_type=F32)


def dot_tn(a, b):
    return lax.dot_general(a, b, (((0,), (0,)), ((), ())), preferred_element_type=F32)


def normed(values):
    center = values - jnp.mean(values, axis=-1, keepdims=True)
    scale = lax.rsqrt(jnp.mean(center * center, axis=-1, keepdims=True) + LN_EPS)
    return center * scale, scale


def diagonal(rows):
    n = GROUP // HEAD
    lat = rows.shape[0]
    tall = jnp.concatenate([rows] * n, axis=0)
    row = lax.broadcasted_iota(jnp.int32, tall.shape, 0) // lat
    col = lax.broadcasted_iota(jnp.int32, tall.shape, 1) // HEAD
    return jnp.where(row == col, tall, jnp.zeros_like(tall))


def undiagonal(tall):
    n = GROUP // HEAD
    lat = tall.shape[0] // n
    col = lax.broadcasted_iota(jnp.int32, (lat, GROUP), 1) // HEAD
    total = jnp.where(col == 0, tall[:lat], 0.0)
    for h in range(1, n):
        total = total + jnp.where(col == h, tall[h * lat : (h + 1) * lat], 0.0)
    return total


def weight_block(weights, m, g, sizes):
    block = weights.shape[-1]
    per = GROUP // block
    parts = []
    for s in range(per):
        h = g * per + s
        part = weights[m, lax.div(h, sizes["c"]), lax.rem(h, sizes["c"])]
        parts.append(part.reshape(D, block))
    return parts[0] if per == 1 else jnp.concatenate(parts, axis=1)


def softmax_columns(keys, spread_queries, seen):
    scores = dot_nt(keys, spread_queries)
    scores = jnp.where(seen, scores, -1e30)
    raised = jnp.exp(scores - jnp.max(scores, axis=0, keepdims=True))
    return raised * (1.0 / jnp.sum(raised, axis=0, keepdims=True))


def forward_kernel(
    sizes,
    att_ref,
    expand_ref,
    reduce_ref,
    tokens_ref,
    latents_ref,
    cotangent_ref,
    counts_ref,
    norm_ref,
    att_out,
    ff_out,
    pairs_out,
    turned_out,
    queries_out,
    mixed_out,
    middle_out,
    rows_out,
    back_out,
    att,
    ff,
    pairs,
    turned,
    queries,
    mixed,
    middle,
    rows,
    back,
    tokens,
    inputs,
    send,
    recv,
    local,
):
    links = Links(sizes, send, recv, local)
    links.greet()
    images, patches, _ = tokens.shape
    span = inputs.shape[1]
    lat = span - patches
    at = links.at
    outs = []

    loads = [links.move(tokens_ref.at[i], tokens.at[i]) for i in range(images)]
    for m in range(4):
        att[m, at["y"], at["c"], at["z"], at["x"]] = att_ref[m].astype(BF16)
    back[at["y"], at["c"]] = cotangent_ref[...].astype(BF16)
    ff[0, at["z"], at["x"]] = expand_ref[...].astype(BF16)
    ff[1, at["z"], at["x"]] = reduce_ref[...].astype(BF16)

    half = att.shape[5] // 2

    def att_view(m, s):
        def view(p):
            return att.at[m, some(p["y"]), some(p["c"]), some(p["z"]), some(p["x"]), pl.ds(s * half, half)]

        return view

    piece = max(16, att.shape[5] // 4)
    pieces = att.shape[5] // piece

    def ff_view(m, s):
        def view(p):
            return ff.at[m, some(p["z"]), some(p["x"]), pl.ds(s * piece, piece)]

        return view

    def back_view(p):
        return back.at[some(p["y"]), some(p["c"])]

    def row_view(i):
        def view(p):
            return rows.at[some(p["y"]), some(p["c"]), pl.ds(i * lat, lat)]

        return view

    query = [Gather(links, "zxyc", att_view(0, s)) for s in range(2)]
    key = [Gather(links, "zxyc", att_view(1, 0)), Gather(links, "yzxc", att_view(1, 1))]
    value = [Gather(links, "zyxc", att_view(2, 0)), Gather(links, "xzyc", att_view(2, 1))]
    output = [Gather(links, "zxyc", att_view(3, s)) for s in range(2)]
    hidden = [Gather(links, "zx", ff_view(m, s)) for m in range(2) for s in range(pieces)]
    cotangent = [Gather(links, "yc", back_view)]
    ff_rows = [Gather(links, "yc", row_view(i)) for i in range(images)]
    everything = [*query, *key, *value, *output, *hidden, *cotangent, *ff_rows]

    def start(parts):
        for part in parts:
            part.start(0)

    def go(parts, step):
        for part in parts:
            part.go(step)

    links.meet()
    start(key + value)

    for i in range(images):
        low = normed(latents_ref[pl.ds(i * lat, lat)].astype(F32))[0] * norm_ref[2:3] + norm_ref[3:4]
        inputs[i, pl.ds(patches, lat)] = low.astype(BF16)

    def normalize(i):
        loads[i].wait()
        tile = 64

        def one(t, _):
            part = pl.ds(pl.multiple_of(t * tile, tile), tile)
            low = normed(tokens[i, part].astype(F32))[0] * norm_ref[0:1] + norm_ref[1:2]
            inputs[i, part] = low.astype(BF16)
            return 0

        lax.fori_loop(0, patches // tile, one, 0)

    def turn(i):
        def one(t, _):
            part = pl.ds(pl.multiple_of(t * 128, 128), 128)
            turned[:, pl.ds(pl.multiple_of(i * span + t * 128, 128), 128)] = inputs[i, part].T
            return 0

        lax.fori_loop(0, span // 128, one, 0)

    steps = [
        lambda: (go(key, 0), go(value, 0), start(query + output)),
        lambda: None,
        lambda: (go(key, 1), go(value, 1), start(hidden)),
        lambda: None,
        lambda: (go(key, 2), go(value, 2)),
        lambda: go(query + output, 0),
        lambda: None,
        lambda: go(query, 1),
    ]

    def tick():
        if steps:
            steps.pop(0)()

    for i in range(images):
        normalize(i)
        tick()
        turn(i)
        tick()
    while steps:
        tick()
    outs.append(links.move(turned, turned_out))
    go(key, 3)

    def project(i, m):
        def one(g, _):
            weight = weight_block(att, m, g, sizes)
            pairs[i, (m - 1) * GROUPS + g] = dot(inputs[i], weight).astype(BF16)
            return 0

        lax.fori_loop(0, GROUPS, one, 0)

    def attend(i):
        position = lax.broadcasted_iota(jnp.int32, (span, GROUP), 0)
        count = counts_ref[links.head * images + i]
        seen = (position < count) | (position >= patches)

        def one(g, _):
            spread = diagonal(queries[g, pl.ds(i * lat, lat)])
            probs = softmax_columns(pairs[i, g], spread, seen).astype(BF16)
            wide = dot_tn(probs, pairs[i, GROUPS + g])
            mixed[g, pl.ds(i * lat, lat)] = undiagonal(wide).astype(BF16)
            return 0

        lax.fori_loop(0, GROUPS, one, 0)

    def finish(i):
        part = pl.ds(i * lat, lat)
        whole = jnp.concatenate([mixed[g, part] for g in range(GROUPS)], axis=1)
        made = jnp.concatenate(
            [dot(whole, weight_block(att, 3, g, sizes)) for g in range(GROUPS)], axis=1
        )
        value = latents_ref[part].astype(F32) + made
        middle[part] = value
        low = normed(value)[0] * norm_ref[4:5] + norm_ref[5:6]
        rows[at["y"], at["c"], part] = low.astype(BF16)
        ff_rows[i].start(0)

    def near(p):
        return lambda: go(hidden[p : p + 1], 0)

    steps += [
        lambda: go(output, 1),
        lambda: go(value, 3),
        near(0),
        lambda: None,
        lambda: go(query, 2),
        near(1),
        lambda: None,
        near(2),
    ]
    for i in range(images):
        project(i, 1)
        tick()
    if images < 2:
        tick()
    for i in range(images):
        project(i, 2)
        outs.append(links.move(pairs.at[i], pairs_out.at[i]))
        tick()
    while steps:
        tick()
    go(query, 3)
    stack = inputs[:, patches:].reshape(images * lat, D)
    for g in range(GROUPS):
        made = dot(stack, weight_block(att, 0, g, sizes)) * HEAD ** (-0.5)
        queries[g] = made.astype(BF16)
    outs.append(links.move(queries, queries_out))
    steps += [
        lambda: (go(output, 2), start(cotangent)),
        near(3),
        lambda: go(output, 3),
        near(4),
    ]
    for i in range(images):
        attend(i)
        tick()
    while steps:
        tick()
    steps += [
        near(5),
        lambda: (go(ff_rows[:1], 0), go(cotangent, 0)),
        near(6),
        lambda: go(ff_rows[1:2], 0),
    ]
    for i in range(images):
        finish(i)
        tick()
    while steps:
        tick()
    go(hidden[7:], 0)
    outs.append(links.move(att, att_out))
    outs.append(links.move(mixed, mixed_out))
    outs.append(links.move(middle, middle_out))
    go(ff_rows[2:], 0)
    go(cotangent, 1)
    outs.append(links.move(back, back_out))
    go(ff_rows, 1)
    outs.append(links.move(rows, rows_out))
    go(hidden, 1)
    outs.append(links.move(ff, ff_out))
    for part in everything:
        part.close()
    for out in outs:
        out.wait()


def forward(att, expand, reduce_turned, tokens, latents, cotangent, counts, norm_params):
    sizes = grid_of(lax.axis_size("dp"), lax.axis_size("head"))
    z, x, y, c = (sizes[a] for a in "zxyc")
    images, patches, _ = tokens.shape
    lat = latents.shape[1]
    span = patches + lat
    n = images * lat
    _, row_block, col_block = att.shape
    ff_block = expand.shape[1]
    shapes = dict(
        att=((4, y, c, z, x, row_block, col_block), BF16),
        ff=((2, z, x, row_block, ff_block), BF16),
        pairs=((images, 2 * GROUPS, span, GROUP), BF16),
        turned=((D, images * span), BF16),
        queries=((GROUPS, n, GROUP), BF16),
        mixed=((GROUPS, n, GROUP), BF16),
        middle=((n, D), F32),
        rows=((y, c, n, D), BF16),
        back=((y, c, n, D), BF16),
    )
    inside = [((images, patches, D), BF16), ((images, span, D), BF16)]
    per_att = sum(s - 1 for s in sizes.values())
    slots = 8 * per_att + 8 * (z + x - 2) + (1 + images) * (y + c - 2)
    vmem, anywhere = pl.BlockSpec(memory_space=pltpu.VMEM), pl.BlockSpec(memory_space=pl.ANY)
    made = pl.pallas_call(
        functools.partial(forward_kernel, sizes),
        out_shape=[jax.ShapeDtypeStruct(*v) for v in shapes.values()],
        in_specs=[vmem, vmem, vmem, anywhere, vmem, vmem, pl.BlockSpec(memory_space=pltpu.SMEM), vmem],
        out_specs=[anywhere] * len(shapes),
        scratch_shapes=[pltpu.VMEM(*v) for v in [*shapes.values(), *inside]]
        + [
            pltpu.SemaphoreType.DMA((slots,)),
            pltpu.SemaphoreType.DMA((slots,)),
            pltpu.SemaphoreType.DMA((3 * images + 8,)),
        ],
        compiler_params=pltpu.CompilerParams(
            collective_id=0, has_side_effects=True, vmem_limit_bytes=58 * MIB
        ),
        name="gather_and_attend",
    )(att, expand, reduce_turned, tokens, latents.reshape(n, D), cotangent.reshape(n, D), counts, norm_params)
    return SimpleNamespace(**dict(zip(shapes, made)))


class Scatter:
    def __init__(self, links, order, view, lands):
        self.links, self.order, self.view, self.lands = links, order, view, lands
        self.slots = {}

    def region(self, step, place):
        at = dict(self.links.at)
        for axis in self.order[step + 1 :]:
            at[axis] = None
        at[self.order[step]] = place
        return self.view(at)

    def copies(self, step):
        axis, links = self.order[step], self.links
        for k, slot in enumerate(self.slots[step], 1):
            yield links.copy(self.region(step, links.place(axis, k)), self.lands[step][k - 1], slot, axis, k)

    def start(self, step):
        self.slots[step] = [self.links.take() for _ in range(1, self.links.sizes[self.order[step]])]
        for copy in self.copies(step):
            copy.start()

    def wait(self, step):
        for k, slot in enumerate(self.slots[step], 1):
            land = self.lands[step][k - 1]
            self.links.copy(land, land, slot, self.order[step], k).wait_recv()

    def add(self, step, out=None):
        mine = self.region(step, self.links.at[self.order[step]])
        lands = self.lands[step]
        lead = mine.shape[0] if len(mine.shape) > 2 else None

        def total(at):
            value = mine[at].astype(F32)
            for land in lands:
                value = value + land[at].astype(F32)
            return value

        if out is not None:
            out[...] = total(Ellipsis)
        elif lead is None:
            mine[...] = total(Ellipsis).astype(BF16)
        else:

            def one(t, _):
                mine[t] = total(t).astype(BF16)
                return 0

            lax.fori_loop(0, lead, one, 0)

    def go(self, step, out=None):
        self.wait(step)
        self.add(step, out)
        if step + 1 < len(self.order):
            self.start(step + 1)

    def close(self):
        for step in self.slots:
            for copy in self.copies(step):
                copy.wait_send()


def norm_back(up, hat, scale, gain):
    inner = up * gain
    return scale * (
        inner
        - jnp.mean(inner, axis=-1, keepdims=True)
        - hat * jnp.mean(inner * hat, axis=-1, keepdims=True)
    )


def fold(rows):
    return jnp.sum(rows.reshape(rows.shape[0] // 8, 8, rows.shape[1]), axis=0)


def gelu_and_slope(v):
    root = 0.7978845608028654
    square = v * v
    t = jnp.tanh(root * v * (1.0 + 0.044715 * square))
    half = 0.5 + 0.5 * t
    slope = half + (0.5 * root) * v * (1.0 - t * t) * (1.0 + (3.0 * 0.044715) * square)
    return v * half, slope


ATT_ORDERS = {0: ("yxz", "yxz"), 1: ("yxz", "xyz"), 2: ("yxz", "yxz"), 3: ("yxz", "yxz")}


def land_shapes(sizes, order, axes, tail):
    shapes, left = [], list(axes)
    for axis in order:
        left.remove(axis)
        shapes.append((sizes[axis] - 1, *(sizes[a] for a in left), *tail))
    return shapes


def backward_kernel(sizes, dims, *refs):
    names, keys, images, patches, lat, ff_block = dims
    r = SimpleNamespace(**dict(zip(names, refs)))
    total_lands = dict(zip("cyxz", refs[len(names) :]))
    att_lands = dict(zip(keys, refs[len(names) + 4 :]))
    links = Links(sizes, r.send, r.recv, r.local)
    links.greet()
    at = links.at
    sib = links.place("c", 1)
    n = images * lat
    span = patches + lat
    zs, xs, ys, cs = (sizes[a] for a in "zxyc")
    row_block, col_block = r.att_share.shape[1:]
    xr = xs * row_block
    heads = ys * cs
    half = row_block // 2
    norm_ref, middle, cotangent, latents = r.norm, r.middle, r.cotangent, r.latents
    queries, mixed = r.queries, r.mixed
    grads_ff = r.grads_ff
    middle_grad, branch, mixed_grad, query_back = r.middle_grad, r.branch, r.mixed_grad, r.query_back
    outs = []

    units = [(m, k) for k in [*range(1, zs), 0] for m in (1, 0)]
    x_slots = {unit: [links.take() for _ in range(1, xs)] for unit in units}
    z_slots = {unit: links.take() for unit in units if unit[1]}

    def x_copies(unit):
        m, k = unit
        z = links.place("z", k)
        for j, slot in enumerate(x_slots[unit], 1):
            yield links.copy(
                grads_ff.at[m, z, links.place("x", j)], r.ff_land_x.at[m, z, j - 1], slot, "x", j
            )

    def z_copy(unit):
        m, k = unit
        return links.copy(
            grads_ff.at[m, links.place("z", k), at["x"]], r.ff_land_z.at[m, k - 1], z_slots[unit], "z", k
        )

    def ff_along(unit):
        m, k = unit
        z = links.place("z", k)
        for copy in x_copies(unit):
            copy.wait_recv()
        total = grads_ff[m, z, at["x"]].astype(F32)
        for j in range(xs - 1):
            total = total + r.ff_land_x[m, z, j].astype(F32)
        if k:
            grads_ff[m, z, at["x"]] = total.astype(BF16)
            z_copy(unit).start()
        else:
            r.ff_share[m] = total

    def ff_finish():
        for m in range(2):
            for k in range(1, zs):
                z_copy((m, k)).wait_recv()
            total = r.ff_share[m]
            for k in range(1, zs):
                total = total + r.ff_land_z[m, k - 1].astype(F32)
            r.ff_share[m] = total

    pairs = r.pairs_here
    early = [links.move(r.pairs.at[i], pairs.at[i]) for i in range(images)]

    def feed_forward(ffw, rows, back, hidden, bg, part):
        loads = [links.move(r.ff, ffw), links.move(r.rows, rows), links.move(r.back, back)]
        links.meet()
        for load in loads:
            load.wait()
        tile = min(GROUP, ff_block)

        def first(yi):
            def one(t, _):
                cols = pl.ds(pl.multiple_of(t * tile, tile), tile)
                before = dot(rows[yi].reshape(cs * n, D), ffw[0, :, :, :, cols].reshape(D, tile))
                up = dot(back[yi].reshape(cs * n, D), ffw[1, :, :, :, cols].reshape(D, tile))
                made, slope = gelu_and_slope(before)
                hidden[yi, :, :, cols] = made.astype(BF16).reshape(cs, n, tile)
                bg[yi, :, :, cols] = (up * slope).astype(BF16).reshape(cs, n, tile)
                return 0

            lax.fori_loop(0, ff_block // tile, one, 0)

        def second(kind, yi):
            left = hidden if kind else bg

            def one(z, _):
                cols = pl.ds(pl.multiple_of(z * xr, xr), xr)
                made = dot_nt(left[yi].reshape(cs * n, ff_block), ffw[kind, z].reshape(xr, ff_block))
                part[kind, yi, :, :, cols] = made.astype(BF16).reshape(cs, n, xr)
                return 0

            lax.fori_loop(0, zs, one, 0)

        sent, chip, along = [], {}, {}

        def to_sibling(kind, k):
            yi = links.place("y", k)
            slot = links.take()
            land = r.land_c.at[kind, yi]
            copy = links.copy(part.at[kind, yi, sib], land, slot, "c", 1)
            copy.start()
            sent.append(copy)
            chip[kind, k] = links.copy(land, land, slot, "c", 1)

        def along_y(kind, k):
            yi = links.place("y", k)
            chip[kind, k].wait_recv()
            summed = part[kind, yi, at["c"]].astype(F32) + r.land_c[kind, yi].astype(F32)
            r.sum_y[kind, k - 1] = summed.astype(BF16)
            slot = links.take()
            land = r.land_y.at[kind, k - 1]
            copy = links.copy(r.sum_y.at[kind, k - 1], land, slot, "y", k)
            copy.start()
            along[kind, k] = (copy, links.copy(land, land, slot, "y", k))

        for k in range(1, ys):
            yi = links.place("y", k)
            first(yi)
            second(0, yi)
            to_sibling(0, k)
            second(1, yi)
            to_sibling(1, k)
        first(at["y"])
        for k in range(1, ys):
            along_y(0, k)
        second(0, at["y"])
        to_sibling(0, 0)
        second(1, at["y"])
        to_sibling(1, 0)
        for k in range(1, ys):
            along_y(1, k)

        def gradient(unit):
            m, k = unit
            z = links.place("z", k)
            cols = pl.ds(pl.multiple_of(z * xr, xr), xr)
            left, right = (back, hidden) if m else (rows, bg)
            made = dot_tn(left[:, :, :, cols].reshape(heads * n, xr), right[...].reshape(heads * n, ff_block))
            grads_ff[m, z] = made.astype(BF16).reshape(xs, row_block, ff_block)
            for copy in x_copies(unit):
                copy.start()

        for unit in units:
            gradient(unit)
        chip[0, 0].wait_recv()
        for k in range(1, ys):
            along[0, k][1].wait_recv()

        def back_one(t, carry):
            gain, shift = carry
            rws = pl.ds(pl.multiple_of(t * lat, lat), lat)
            up = part[0, at["y"], at["c"], rws].astype(F32) + r.land_c[0, at["y"], rws].astype(F32)
            for k in range(1, ys):
                up = up + r.land_y[0, k - 1, rws].astype(F32)
            hat, scale = normed(middle[rws])
            value = cotangent[rws] + norm_back(up, hat, scale, norm_ref[4:5])
            middle_grad[rws] = value
            branch[rws] = value.astype(BF16)
            return gain + fold(up * hat), shift + fold(up)

        zero = jnp.zeros((8, D), F32)
        ff_gain, ff_shift = lax.fori_loop(0, images, back_one, (zero, zero))
        r.norm_parts[4] = ff_gain
        r.norm_parts[5] = ff_shift
        chip[1, 0].wait_recv()
        for k in range(1, ys):
            along[1, k][1].wait_recv()

        def out_one(t, _):
            rws = pl.ds(pl.multiple_of(t * lat, lat), lat)
            up = part[1, at["y"], at["c"], rws].astype(F32) + r.land_c[1, at["y"], rws].astype(F32)
            for k in range(1, ys):
                up = up + r.land_y[1, k - 1, rws].astype(F32)
            rows[at["y"], at["c"], rws] = (middle[rws] + up).astype(BF16)
            return 0

        lax.fori_loop(0, images, out_one, 0)
        leaving = links.move(rows.at[at["y"], at["c"]], r.resampled)
        for copy in sent:
            copy.wait_send()
        for copy, _ in along.values():
            copy.wait_send()
        leaving.wait()

    pl.run_scoped(
        feed_forward,
        pltpu.VMEM((2, zs, xs, row_block, ff_block), BF16),
        pltpu.VMEM((ys, cs, n, D), BF16),
        pltpu.VMEM((ys, cs, n, D), BF16),
        pltpu.VMEM((ys, cs, n, ff_block), BF16),
        pltpu.VMEM((ys, cs, n, ff_block), BF16),
        pltpu.VMEM((2, ys, cs, n, D), BF16),
    )

    steps = []

    def tick():
        if steps:
            steps.pop(0)()

    def later(f, *args):
        steps.append(lambda: f(*args))

    def attention(grads, turned_left):
        per = GROUP // col_block
        block_slots = {m: [links.take() for _ in range(ys)] for m in range(4)}

        def block_copy(m, yi):
            slot = block_slots[m][0] + yi
            return links.copy(grads.at[m, yi, sib], r.att_land_c.at[m, yi], slot, "c", 1)

        def att_scatter(m, s):
            def view(p):
                return grads.at[m, some(p["y"]), at["c"], some(p["z"]), some(p["x"]), pl.ds(s * half, half)]

            order = ATT_ORDERS[m][s]
            lands = [
                [att_lands[m, s, step].at[k] for k in range(sizes[axis] - 1)]
                for step, axis in enumerate(order)
            ]
            return Scatter(links, order, view, lands)

        scatter = {m: [att_scatter(m, s) for s in range(2)] for m in range(4)}

        def go(m, step):
            for s, part in enumerate(scatter[m]):
                part.go(step, r.att_share.at[m, pl.ds(s * half, half)] if step == 2 else None)

        def chip_sum(m):
            for yi in range(ys):
                block_copy(m, yi).wait_recv()

                def one(z, _):
                    value = grads[m, yi, at["c"], z].astype(F32) + r.att_land_c[m, yi, z].astype(F32)
                    grads[m, yi, at["c"], z] = value.astype(BF16)
                    return 0

                lax.fori_loop(0, zs, one, 0)
            for part in scatter[m]:
                part.start(0)

        def products(m, left, right, between=None):
            def of(ci, send):
                def one(yi, _):
                    made = dot(left(), right(yi * cs + ci)).astype(BF16)
                    grads[m, yi, ci] = made.reshape(zs, xs, row_block, col_block)
                    if send:
                        block_copy(m, yi).start()
                    return 0

                lax.fori_loop(0, ys, one, 0)

            of(sib, True)
            if between is not None:
                between()
            of(at["c"], False)

        def query_columns(h):
            j = lax.div(h * col_block, GROUP)
            if per == 1:
                return query_back[j]
            off = pl.multiple_of(lax.rem(h, per) * col_block, col_block)
            return query_back[j, :, pl.ds(off, col_block)]

        def columns(m):
            def right(h):
                j = lax.div(h * col_block, GROUP) + (m - 1) * GROUPS
                if per == 1:
                    return pairs[:, j].reshape(images * span, GROUP)
                off = pl.multiple_of(lax.rem(h, per) * col_block, col_block)
                return pairs[:, j, :, pl.ds(off, col_block)].reshape(images * span, col_block)

            return right

        def attend(i):
            position = lax.broadcasted_iota(jnp.int32, (span, GROUP), 0)
            count = r.counts[links.head * images + i]
            seen = (position < count) | (position >= patches)
            rws = pl.ds(i * lat, lat)

            def one(g, _):
                keys, values = pairs[i, g], pairs[i, GROUPS + g]
                spread = diagonal(queries[g, rws])
                probs = softmax_columns(keys, spread, seen)
                upstream = diagonal(mixed_grad[g, rws])
                prob_grad = dot_nt(values, upstream)
                inner = jnp.sum(probs * prob_grad, axis=0, keepdims=True)
                score_grad = (probs * (prob_grad - inner)).astype(BF16)
                back = undiagonal(dot_tn(score_grad, keys)) * HEAD ** (-0.5)
                query_back[g, rws] = back.astype(BF16)
                pairs[i, GROUPS + g] = dot(probs.astype(BF16), upstream).astype(BF16)
                pairs[i, g] = dot(score_grad, spread).astype(BF16)
                return 0

            lax.fori_loop(0, GROUPS, one, 0)

        def weights(turned, weight):
            load_weight = links.move(r.att.at[3], weight)
            load_turned = links.move(r.turned, turned)
            for g in range(GROUPS):
                turned_left[pl.ds(g * GROUP, GROUP)] = mixed[g].T
            products(
                3,
                lambda: turned_left[...],
                lambda h: branch[:, pl.ds(pl.multiple_of(h * col_block, col_block), col_block)],
            )
            load_weight.wait()
            for g in range(GROUPS):
                first = g * GROUP // row_block
                wide = []
                for h in range(heads):
                    blocks = [
                        weight[h // cs, h % cs, b // xs, b % xs] for b in range(first, first + GROUP // row_block)
                    ]
                    wide.append(jnp.concatenate(blocks, axis=0))
                mixed_grad[g] = dot_nt(branch[...], jnp.concatenate(wide, axis=1)).astype(BF16)
            ff_steps = [lambda u=u: ff_along(u) for u in units]
            steps.append(lambda: (chip_sum(3), ff_steps[0]()))
            steps.extend(ff_steps[1:])
            for i in range(images):
                attend(i)
                tick()
            load_turned.wait()
            for i in range(images):
                turned_left[:, pl.ds(i * lat, lat)] = turned[:, i * span + patches : (i + 1) * span]
            products(0, lambda: turned_left[...], query_columns)
            steps.insert(0, lambda: go(3, 0))
            steps.insert(2, lambda: chip_sum(0))
            tick()
            products(2, lambda: turned[...], columns(2), tick)
            steps.insert(1, lambda: chip_sum(2))
            tick()
            products(1, lambda: turned[...], columns(1), tick)
            tick()

        pl.run_scoped(
            weights,
            pltpu.VMEM((D, images * span), BF16),
            pltpu.VMEM((ys, cs, zs, xs, row_block, col_block), BF16),
        )

        def inputs(att, tokens, pair_grad):
            weight_loads = [links.move(r.att.at[m], att.at[m]) for m in (1, 2, 0)]
            loads = {}

            def fetch(i):
                loads[i] = links.move(r.tokens.at[i], tokens.at[i % 2])

            media_out = {}
            fetch(0)
            tick()
            steps.insert(0, lambda: chip_sum(1))
            for m, step in ((3, 1), (0, 0), (2, 0), (1, 0), (3, 2), (0, 1), (2, 1), (1, 1), (0, 2), (2, 2)):
                later(go, m, step)
            zero = jnp.zeros((8, D), F32)
            sums = (zero, zero, zero, zero)
            for load in weight_loads:
                load.wait()
            for i in range(images):
                stacked = jnp.concatenate([pairs[i, j] for j in range(2 * GROUPS)], axis=1)
                asked = jnp.concatenate([query_back[g, pl.ds(i * lat, lat)] for g in range(GROUPS)], axis=1)

                def one(z, _):
                    cols = pl.ds(pl.multiple_of(z * xr, xr), xr)
                    wide = jnp.concatenate(
                        [att[m, h // cs, h % cs, z].reshape(xr, col_block) for m in (1, 2) for h in range(heads)], axis=1
                    )
                    narrow = jnp.concatenate(
                        [att[0, h // cs, h % cs, z].reshape(xr, col_block) for h in range(heads)], axis=1
                    )
                    pair_grad[:, cols] = dot_nt(stacked, wide)
                    pair_grad[patches:, cols] += dot_nt(asked, narrow)
                    return 0

                lax.fori_loop(0, zs, one, 0)
                tick()
                tick()
                if i + 1 < images:
                    if i >= 1:
                        media_out[i - 1].wait()
                    fetch(i + 1)
                loads[i].wait()
                slot = i % 2
                tile = 64

                def media(t, carry):
                    gain, shift = carry
                    rws = pl.ds(pl.multiple_of(t * tile, tile), tile)
                    hat, scale = normed(tokens[slot, rws].astype(F32))
                    up = pair_grad[rws]
                    tokens[slot, rws] = norm_back(up, hat, scale, norm_ref[0:1]).astype(BF16)
                    return gain + fold(up * hat), shift + fold(up)

                gain, shift = lax.fori_loop(0, patches // tile, media, (sums[0], sums[1]))
                media_out[i] = links.move(tokens.at[slot], r.media_grad.at[i])
                rws = pl.ds(i * lat, lat)
                hat, scale = normed(latents[rws].astype(F32))
                up = pair_grad[patches:]
                made = middle_grad[rws] + norm_back(up, hat, scale, norm_ref[2:3])
                branch[rws] = made.astype(BF16)
                sums = (gain, shift, sums[2] + fold(up * hat), sums[3] + fold(up))
                tick()
                tick()
            for k, value in enumerate(sums):
                r.norm_parts[k] = value
            for i in range(max(0, images - 2), images):
                media_out[i].wait()

        pl.run_scoped(
            inputs,
            pltpu.VMEM((3, ys, cs, zs, xs, row_block, col_block), BF16),
            pltpu.VMEM((2, patches, D), BF16),
            pltpu.VMEM((span, D), F32),
        )
        while steps:
            tick()
        go(1, 2)
        ff_finish()
        for m in range(4):
            for yi in range(ys):
                block_copy(m, yi).wait_send()
            for part in scatter[m]:
                part.close()
        for unit in units:
            for copy in x_copies(unit):
                copy.wait_send()
            if unit[1]:
                z_copy(unit).wait_send()

    for load in early:
        load.wait()
    pl.run_scoped(
        attention,
        pltpu.VMEM((4, ys, cs, zs, xs, row_block, col_block), BF16),
        pltpu.VMEM((D, n), BF16),
    )

    outs.append(links.move(branch, r.latent_grad))
    squares = jnp.sum(r.att_share[...] * r.att_share[...]) + jnp.sum(r.ff_share[...] * r.ff_share[...])
    rows = [jnp.sum(r.norm_parts[k], axis=0, keepdims=True) for k in range(6)]
    value = jnp.concatenate([*rows, jnp.full((2, D), squares, F32)], axis=0)
    last = []
    for axis in "cyxz":
        lands = total_lands[axis]
        lands[at[axis]] = value
        coming = []
        for k in range(1, sizes[axis]):
            slot = links.take()
            mine = lands.at[at[axis]]
            copy = links.copy(mine, mine, slot, axis, k)
            copy.start()
            last.append(copy)
            land = lands.at[links.place(axis, sizes[axis] - k)]
            coming.append(links.copy(land, land, slot, axis, k))
        for copy in coming:
            copy.wait_recv()
        value = lands[0]
        for k in range(1, sizes[axis]):
            value = value + lands[k]
    r.totals[...] = value
    for copy in last:
        copy.wait_send()
    for out in outs:
        out.wait()


def backward(got, tokens, latents, cotangent, counts, norm_params, row_block, col_block, ff_block):
    sizes = grid_of(lax.axis_size("dp"), lax.axis_size("head"))
    zs, xs, ys, cs = (sizes[a] for a in "zxyc")
    images, patches, _ = tokens.shape
    lat = latents.shape[1]
    n = images * lat
    half = row_block // 2
    vmem, anywhere = pl.BlockSpec(memory_space=pltpu.VMEM), pl.BlockSpec(memory_space=pl.ANY)
    smem = pl.BlockSpec(memory_space=pltpu.SMEM)
    inputs = dict(
        att=(got.att, anywhere),
        ff=(got.ff, anywhere),
        rows=(got.rows, anywhere),
        back=(got.back, anywhere),
        pairs=(got.pairs, anywhere),
        turned=(got.turned, anywhere),
        tokens=(tokens, anywhere),
        queries=(got.queries, vmem),
        mixed=(got.mixed, vmem),
        middle=(got.middle, vmem),
        latents=(latents.reshape(n, D), vmem),
        cotangent=(cotangent.reshape(n, D), vmem),
        norm=(norm_params, vmem),
        counts=(counts, smem),
    )
    outputs = dict(
        resampled=((n, D), BF16, anywhere),
        media_grad=((images, patches, D), BF16, anywhere),
        latent_grad=((n, D), BF16, anywhere),
        att_share=((4, row_block, col_block), F32, vmem),
        ff_share=((2, row_block, ff_block), F32, vmem),
        totals=((8, D), F32, vmem),
    )
    scratch = dict(
        grads_ff=((2, zs, xs, row_block, ff_block), BF16),
        ff_land_x=((2, zs, xs - 1, row_block, ff_block), BF16),
        ff_land_z=((2, zs - 1, row_block, ff_block), BF16),
        att_land_c=((4, ys, zs, xs, row_block, col_block), BF16),
        pairs_here=(got.pairs.shape, BF16),
        land_c=((2, ys, n, D), BF16),
        land_y=((2, ys - 1, n, D), BF16),
        sum_y=((2, ys - 1, n, D), BF16),
        middle_grad=((n, D), F32),
        branch=((n, D), BF16),
        mixed_grad=((GROUPS, n, GROUP), BF16),
        query_back=((GROUPS, n, GROUP), BF16),
        norm_parts=((6, 8, D), F32),
    )
    totals = [((sizes[axis], 8, D), F32) for axis in "cyxz"]
    lands = {}
    for m, orders in ATT_ORDERS.items():
        for s, order in enumerate(orders):
            for step, shape in enumerate(land_shapes(sizes, order, "yzx", (half, col_block))):
                lands[m, s, step] = (shape, BF16)
    steps = sum(v - 1 for v in sizes.values())
    slots = 9 * steps + 2 * (zs * xs + zs) + 6 * ys
    semaphores = dict(send=slots, recv=slots, local=3 * images + 16)
    names = [*inputs, *outputs, *semaphores, *scratch]
    made = pl.pallas_call(
        functools.partial(backward_kernel, sizes, (names, tuple(lands), images, patches, lat, ff_block)),
        out_shape=[jax.ShapeDtypeStruct(shape, dtype) for shape, dtype, _ in outputs.values()],
        in_specs=[spec for _, spec in inputs.values()],
        out_specs=[spec for _, _, spec in outputs.values()],
        scratch_shapes=[pltpu.SemaphoreType.DMA((v,)) for v in semaphores.values()]
        + [pltpu.VMEM(*v) for v in [*scratch.values(), *totals, *lands.values()]],
        compiler_params=pltpu.CompilerParams(
            collective_id=1, has_side_effects=True, vmem_limit_bytes=63 * MIB + 900 * 1024
        ),
        name="backward_and_scatter",
    )(*(value for value, _ in inputs.values()))
    return SimpleNamespace(**dict(zip(outputs, made)))


def adam_step(master, first, second, gradient, step_rate, decay_rate):
    first_new = BETA_ONE * first + (1.0 - BETA_ONE) * gradient
    second_new = BETA_TWO * second + (1.0 - BETA_TWO) * gradient * gradient
    first_hat = first_new / (1.0 - BETA_ONE**STEP)
    second_hat = second_new / (1.0 - BETA_TWO**STEP)
    master_new = master - step_rate * (
        first_hat / (jnp.sqrt(second_hat) + ADAM_EPS) + decay_rate * master
    )
    return (master_new, first_new, second_new)


def on_device(
    media_tokens,
    latents,
    cotangent,
    counts,
    attention_weights,
    attention_first,
    attention_second,
    expand_weight,
    expand_first,
    expand_second,
    reduce_weight,
    reduce_first,
    reduce_second,
    norm_params,
    norm_first,
    norm_second,
):
    _, row_block, col_block = attention_weights.shape
    got = forward(
        attention_weights,
        expand_weight,
        reduce_weight.T,
        media_tokens,
        latents,
        cotangent,
        counts,
        norm_params,
    )
    back = backward(
        got, media_tokens, latents, cotangent, counts, norm_params, row_block, col_block, expand_weight.shape[1]
    )
    norm_total, squares_total = back.totals[:6], back.totals[6, 0]
    grad_norm = jnp.sqrt(squares_total + jnp.sum(norm_total * norm_total))
    clip_factor = jnp.minimum(1.0, MAX_NORM / (grad_norm + 1e-06))
    attention = adam_step(
        attention_weights,
        attention_first,
        attention_second,
        back.att_share * clip_factor,
        MATRIX_RATE,
        DECAY_RATE,
    )
    expand = adam_step(
        expand_weight, expand_first, expand_second, back.ff_share[0] * clip_factor, MATRIX_RATE, DECAY_RATE
    )
    reduce = adam_step(
        reduce_weight, reduce_first, reduce_second, back.ff_share[1].T * clip_factor, MATRIX_RATE, DECAY_RATE
    )
    norm = adam_step(norm_params, norm_first, norm_second, norm_total * clip_factor, NORM_RATE, 0.0)
    return (
        back.resampled.reshape(latents.shape),
        back.media_grad,
        back.latent_grad.reshape(latents.shape),
        grad_norm,
        *attention,
        *expand,
        *reduce,
        *norm,
    )


def solution(mesh):
    in_specs = (
        P(("dp", "head"), None, None),
        P(("dp", "head"), None, None),
        P(("dp", "head"), None, None),
        P("dp"),
        P(None, "dp", "head"),
        P(None, "dp", "head"),
        P(None, "dp", "head"),
        P("dp", "head"),
        P("dp", "head"),
        P("dp", "head"),
        P("head", "dp"),
        P("head", "dp"),
        P("head", "dp"),
        P(),
        P(),
        P(),
    )
    out_specs = (
        P(("dp", "head"), None, None),
        P(("dp", "head"), None, None),
        P(("dp", "head"), None, None),
        P(),
        P(None, "dp", "head"),
        P(None, "dp", "head"),
        P(None, "dp", "head"),
        P("dp", "head"),
        P("dp", "head"),
        P("dp", "head"),
        P("head", "dp"),
        P("head", "dp"),
        P("head", "dp"),
        P(),
        P(),
        P(),
    )
    return jax.shard_map(
        on_device, mesh=mesh, in_specs=in_specs, out_specs=out_specs, check_vma=False
    )
```

time: 572 us -> 278 us (0.49); the launches traced: 560 us -> 277 us
  Pallas kernels: 112 us -> 250 us
  local copies, waits for them, and re-layouts: 122 us -> 13.3 us
  matrix products: 104 us -> 0 us
  waiting for transfers between devices: 81.8 us -> 0 us
  blocking collectives: 67.4 us -> 0 us
  other arithmetic: 54.7 us -> 10.2 us
  between operations: 19.3 us -> 3.22 us
    pallas_call x0 -> x1, Pallas kernels: none -> 140 us  [backward(): pl.pallas_call(functools.partial(backward_kernel, sizes, (names, tuple(la...]
    dot_general x19 -> x0, matrix products: 104 us -> none  [the longest x1 12.5 us: on_device(): jnp.einsum('ne,de->nd', value_back, value_weight, preferred_element_type=...]
    reduce_scatter x5 -> x0, waiting for transfers between devices: 81.8 us -> none  [the longest x1 79.7 us: on_device(): lax.psum_scatter(arranged, ('dp', 'head'), scatter_dimension=0, tiled=True)]
    psum x1 -> x0, blocking collectives: 67.4 us -> none  [on_device(): lax.psum((norm_local, squares_here), ('dp', 'head'))]
    transpose x6 -> x0, local copies, waits for them, and re-layouts: 29.9 us -> none  [the longest x1 15.1 us: on_device(): got['pairs'].transpose(0, 2, 1, 3).reshape(images, key_span, 2, HEADS, HEAD)]
    reshape x7 -> x0, local copies, waits for them, and re-layouts: 29.8 us -> none  [the longest x1 11.6 us: on_device(): got['att'].reshape(4, head_count, width, col_block).transpose(0, 2, 1, 3)]
    reduce_sum x11 -> x0, other arithmetic: 18.5 us -> none  [the longest x2 5.75 us: norm_back(): jnp.sum(upstream * hat, axis=lead_axes)]
    convert_element_type x3 -> x0, other arithmetic: 16.1 us -> none  [the longest x1 9.22 us: on_device(): media_grad = media_back.astype(jnp.bfloat16)]
  transfers between devices with their start and end apart: 5 -> 0, of which waited for: 2 -> 0; matrix products, arithmetic and copies ran while one was open for 44% -> 0% of each run, Pallas kernels for 0% -> 0%
where the time goes in v2:
time: 278 us; the launch traced here: 277 us
  Pallas kernels  250 us (90%)
  local copies, waits for them, and re-layouts  13.3 us (5%)
  other arithmetic  10.2 us (4%)
  between operations  3.22 us (1%)
    pallas_call x1, Pallas kernels, backward(): pl.pallas_call(functools.partial(backward_kernel, sizes, (names, tuple(la...  140 us
    pallas_call x1, Pallas kernels, forward(): pl.pallas_call(functools.partial(forward_kernel, sizes), out_shape=[jax.S...  110 us
    unnamed x25, local copies, waits for them, and re-layouts  12.1 us
    sub x4, other arithmetic, adam_step(): master - step_rate * (first_hat / (jnp.sqrt(second_hat) + ADAM_EPS) + dec...  8.83 us

profile of v2, /device:TPU:10, one launch (start us, length us, event | category | flops | bytes accessed | tf_op | source)
XLA Modules:
  0.0 276.9 jit_solution(1115712652955125478)
XLA Ops:
  0.6 2.0 copy.32
  2.7 110.4 %gather_and_attend.1 = (bf16[4,2,2,4,2,128,256]{6,5,4,3,2,1,0:T(8,128)(2,1)}, bf16[2,4,2,128,1024]{4,3,2,1,0:T(8,128)(2,1)}, bf16[4,8,640,256]{3,2,1,0:T(8,128)(...) custom-call(f32[4,128,256]{2,1,0:T(8,128)} %att_ref.1, ...), custom_call_target="tpu_custom_call" | custom-call | tf_op jit(solution)/shard_map/gather_and_attend/pallas_call | solution.py:465
  113.1 0.0 copy-start.5
  113.1 139.7 %backward_and_scatter.1 = (bf16[256,1024]{1,0:T(8,128)(2,1)}, bf16[4,576,1024]{2,1,0:T(8,128)(2,1)}, bf16[256,1024]{1,0:T(8,128)(2,1)}, f32[4,128,256]{2,1,0:T(8...) custom-call(bf16[4,2,2,4,2,128,256]{6,5,4,3,2,1,0:T(8,128)(2,1)} %get-tuple-element.31.refs_0_, ...), custom_call_target="tpu_custom_call" | custom-call | tf_op jit(solution)/shard_map/backward_and_scatter/pallas_call | solution.py:1106
  252.8 0.0 copy-start
  252.8 1.2 slice.12
  254.1 1.4 multiply_reduce_fusion
  256.8 0.0 copy-done.5
  256.8 1.4 multiply_subtract_fusion.3
  258.3 1.2 copy.33
  259.5 2.0 copy.34
  261.6 1.8 multiply_subtract_fusion
  263.4 1.0 copy.37
  264.4 1.0 copy.38
  265.4 1.0 copy.39
  266.4 0.0 copy-done
  266.4 2.9 %multiply_subtract_fusion.1 = (f32[128,1024]{1,0:T(8,128)}, f32[128,1024]{1,0:T(8,128)}, f32[128,1024]{1,0:T(8,128)}) fusion(f32[128,1024]{1,0:T(8,128)S(1)} %copy-done, f32[]{:T(128)S(6)} %min_shard_map.3, f32[2,128,1024]{2,1,0:T(8,128)} %get-tuple-element.45, f32[128,1024]{1,0:T(8,128)} %param.24, f32[128,1024]{1,0:T(8,128)} %param.25), kind=kLoop, calls=%fused_computation.12 | loop fusion | flops 2097152 | bytes 3670020 | tf_op jit(solution)/shard_map/sub | solution.py:1126
  269.3 0.0 copy-done.1
  269.3 0.0 copy-done.4
  269.3 2.6 multiply_subtract_fusion.2
  271.9 0.0 copy-done.3
  271.9 0.8 copy.43
  272.7 2.2 copy.44
  274.9 0.8 copy.45
  (10 shorter events, 0.0 us)
Async XLA Ops:
  113.1 143.7 %copy-start.5 = (f32[6,1024]{1,0:T(8,128)S(1)}, f32[6,1024]{1,0:T(8,128)}, u32[]{:S(2)}) copy-start(f32[6,1024]{1,0:T(8,128)} %refs_12_.1) | copy-start | bytes 73732
  252.8 13.6 %copy-start = (f32[128,1024]{1,0:T(8,128)S(1)}, f32[128,1024]{1,0:T(8,128)}, u32[]{:S(2)}) copy-start(f32[128,1024]{1,0:T(8,128)} %expand_ref.1) | copy-start | bytes 1572868
  261.6 7.8 %copy-start.1 = (f32[4,128,256]{2,1,0:T(8,128)S(1)}, f32[4,128,256]{2,1,0:T(8,128)}, u32[]{:S(2)}) copy-start(f32[4,128,256]{2,1,0:T(8,128)} %att_ref.1) | copy-start | bytes 1572868
  264.4 7.5 %copy-start.3 = (bf16[256,1024]{1,0:T(8,128)(2,1)S(1)}, bf16[256,1024]{1,0:T(8,128)(2,1)}, u32[]{:S(2)}) copy-start(bf16[256,1024]{1,0:T(8,128)(2,1)} %get-tuple-element.40) | copy-start | bytes 1572868
  264.4 8.3 %slice-start = ((s8[4718592]{0:T(1024)(128)(4,1)}), s8[524288]{0:T(1024)(128)(4,1)S(1)}, s32[]{:S(2)}) async-start(s8[4718592]{0:T(1024)(128)(4,1)} %bitcast.22), calls=%async_computation | async-start | bytes 1048576
  265.4 3.9 %copy-start.4 = (f32[4,128,256]{2,1,0:T(8,128)S(1)}, f32[4,128,256]{2,1,0:T(8,128)}, u32[]{:S(2)}) copy-start(f32[4,128,256]{2,1,0:T(8,128)} %param.21) | copy-start | bytes 1572868
  266.4 6.4 %slice-start.1 = ((s8[4718592]{0:T(1024)(128)(4,1)}), s8[4194304]{0:T(1024)(128)(4,1)S(1)}, s32[]{:S(2)}) async-start(s8[4718592]{0:T(1024)(128)(4,1)} %bitcast.22), calls=%async_computation.1 | async-start | bytes 8388608
  272.7 2.2 copy-start.2

commit v3 on v2

--- a/solution.py
+++ b/solution.py
@@ -154,6 +154,28 @@
     return center * scale, scale
 
 
+def norm_back(up, hat, scale, gain):
+    inner = up * gain
+    return scale * (
+        inner
+        - jnp.mean(inner, axis=-1, keepdims=True)
+        - hat * jnp.mean(inner * hat, axis=-1, keepdims=True)
+    )
+
+
+def fold(rows):
+    return jnp.sum(rows.reshape(rows.shape[0] // 8, 8, rows.shape[1]), axis=0)
+
+
+def gelu_and_slope(v):
+    root = 0.7978845608028654
+    square = v * v
+    t = jnp.tanh(root * v * (1.0 + 0.044715 * square))
+    half = 0.5 + 0.5 * t
+    slope = half + (0.5 * root) * v * (1.0 - t * t) * (1.0 + (3.0 * 0.044715) * square)
+    return v * half, slope
+
+
 def diagonal(rows):
     n = GROUP // HEAD
     lat = rows.shape[0]
@@ -202,23 +224,34 @@
     counts_ref,
     norm_ref,
     att_out,
-    ff_out,
     pairs_out,
     turned_out,
     queries_out,
     mixed_out,
+    ff_grad_out,
+    added_out,
     middle_out,
-    rows_out,
-    back_out,
+    middle_grad_out,
+    branch_out,
+    ff_norm_out,
     att,
-    ff,
     pairs,
     turned,
     queries,
     mixed,
+    ff,
+    added,
     middle,
+    middle_grad,
+    branch,
+    ff_norm,
     rows,
     back,
+    hid,
+    bg,
+    part,
+    land_c,
+    land_y,
     tokens,
     inputs,
     send,
@@ -227,18 +260,27 @@
 ):
     links = Links(sizes, send, recv, local)
     links.greet()
-    images, patches, _ = tokens.shape
-    span = inputs.shape[1]
+    images, span, _ = inputs.shape
+    patches = tokens_ref.shape[1]
     lat = span - patches
     at = links.at
     outs = []
 
-    loads = [links.move(tokens_ref.at[i], tokens.at[i]) for i in range(images)]
+    loads = {}
+
+    def fetch(i):
+        if i < images:
+            loads[i] = links.move(tokens_ref.at[i], tokens.at[i % 2])
+
+    fetch(0)
+    fetch(1)
     for m in range(4):
         att[m, at["y"], at["c"], at["z"], at["x"]] = att_ref[m].astype(BF16)
     back[at["y"], at["c"]] = cotangent_ref[...].astype(BF16)
-    ff[0, at["z"], at["x"]] = expand_ref[...].astype(BF16)
-    ff[1, at["z"], at["x"]] = reduce_ref[...].astype(BF16)
+    quarters, tile = ff.shape[0], ff.shape[-1]
+    for q in range(quarters):
+        ff[q, 0, at["z"], at["x"]] = expand_ref[:, q * tile : (q + 1) * tile].astype(BF16)
+        ff[q, 1, at["z"], at["x"]] = reduce_ref[q * tile : (q + 1) * tile].T.astype(BF16)
 
     half = att.shape[5] // 2
 
@@ -248,12 +290,9 @@
 
         return view
 
-    piece = max(16, att.shape[5] // 4)
-    pieces = att.shape[5] // piece
-
-    def ff_view(m, s):
+    def ff_view(q, m):
         def view(p):
-            return ff.at[m, some(p["z"]), some(p["x"]), pl.ds(s * piece, piece)]
+            return ff.at[q, m, some(p["z"]), some(p["x"])]
 
         return view
 
@@ -266,11 +305,8 @@
 
         return view
 
-    query = [Gather(links, "zxyc", att_view(0, s)) for s in range(2)]
-    key = [Gather(links, "zxyc", att_view(1, 0)), Gather(links, "yzxc", att_view(1, 1))]
-    value = [Gather(links, "zyxc", att_view(2, 0)), Gather(links, "xzyc", att_view(2, 1))]
-    output = [Gather(links, "zxyc", att_view(3, s)) for s in range(2)]
-    hidden = [Gather(links, "zx", ff_view(m, s)) for m in range(2) for s in range(pieces)]
+    query, key, value, output = ([Gather(links, "zxyc", att_view(m, s)) for s in range(2)] for m in range(4))
+    hidden = [Gather(links, "zx", ff_view(q, m)) for q in range(quarters) for m in range(2)]
     cotangent = [Gather(links, "yc", back_view)]
     ff_rows = [Gather(links, "yc", row_view(i)) for i in range(images)]
     everything = [*query, *key, *value, *output, *hidden, *cotangent, *ff_rows]
@@ -284,7 +320,7 @@
             part.go(step)
 
     links.meet()
-    start(key + value)
+    start(key + value + hidden[:1] + query + hidden[1:2] + output)
 
     for i in range(images):
         low = normed(latents_ref[pl.ds(i * lat, lat)].astype(F32))[0] * norm_ref[2:3] + norm_ref[3:4]
@@ -292,47 +328,69 @@
 
     def normalize(i):
         loads[i].wait()
-        tile = 64
+        some_rows = 64
 
         def one(t, _):
-            part = pl.ds(pl.multiple_of(t * tile, tile), tile)
-            low = normed(tokens[i, part].astype(F32))[0] * norm_ref[0:1] + norm_ref[1:2]
+            part = pl.ds(pl.multiple_of(t * some_rows, some_rows), some_rows)
+            low = normed(tokens[i % 2, part].astype(F32))[0] * norm_ref[0:1] + norm_ref[1:2]
             inputs[i, part] = low.astype(BF16)
             return 0
 
-        lax.fori_loop(0, patches // tile, one, 0)
+        lax.fori_loop(0, patches // some_rows, one, 0)
+        fetch(i + 2)
+
+    turning = {}
 
     def turn(i):
+        if i >= 2:
+            turning[i - 2].wait()
+
         def one(t, _):
             part = pl.ds(pl.multiple_of(t * 128, 128), 128)
-            turned[:, pl.ds(pl.multiple_of(i * span + t * 128, 128), 128)] = inputs[i, part].T
+            turned[i % 2, :, part] = inputs[i, part].T
             return 0
 
         lax.fori_loop(0, span // 128, one, 0)
-
-    steps = [
-        lambda: (go(key, 0), go(value, 0), start(query + output)),
-        lambda: None,
-        lambda: (go(key, 1), go(value, 1), start(hidden)),
-        lambda: None,
-        lambda: (go(key, 2), go(value, 2)),
-        lambda: go(query + output, 0),
-        lambda: None,
-        lambda: go(query, 1),
-    ]
+        turning[i] = links.move(turned.at[i % 2], turned_out.at[:, pl.ds(i * span, span)])
+
+    k0, k1, v0, v1, q0, q1, o0, o1 = *key, *value, *query, *output
+    f = [*hidden, *[None] * (8 - len(hidden))]
+    steps = []
+
+    def plan(*ticks):
+        steps.extend(ticks)
+
+    plan(
+        [(k0, 0)],
+        [(k1, 0)],
+        [(k0, 1), (v0, 0)],
+        [(k1, 1), (v1, 0)],
+        [(v0, 1)],
+        [(k0, 2), (v1, 1)],
+        [(f[0], 0)],
+        [(k1, 2), (q0, 0)],
+    )
 
     def tick():
-        if steps:
-            steps.pop(0)()
+        for part, step in steps.pop(0) if steps else ():
+            if part is not None:
+                part.go(step)
+            if part in hidden:
+                start(hidden[hidden.index(part) + 2 :][:1])
+
+    def rest():
+        while steps:
+            tick()
 
     for i in range(images):
         normalize(i)
         tick()
         turn(i)
         tick()
-    while steps:
-        tick()
-    outs.append(links.move(turned, turned_out))
+    plan([(q1, 0), (v0, 2), (q0, 1)])
+    rest()
+    for i in range(max(0, images - 2), images):
+        turning[i].wait()
     go(key, 3)
 
     def project(i, m):
@@ -369,76 +427,150 @@
         rows[at["y"], at["c"], part] = low.astype(BF16)
         ff_rows[i].start(0)
 
-    def near(p):
-        return lambda: go(hidden[p : p + 1], 0)
-
-    steps += [
-        lambda: go(output, 1),
-        lambda: go(value, 3),
-        near(0),
-        lambda: None,
-        lambda: go(query, 2),
-        near(1),
-        lambda: None,
-        near(2),
-    ]
+    plan([], [(q1, 1)], [(f[1], 0)], [(v1, 2)])
     for i in range(images):
         project(i, 1)
         tick()
-    if images < 2:
-        tick()
+    plan([(o0, 0), (q0, 2), (o1, 0)])
+    rest()
+    go(value, 3)
+    plan([(o0, 1)], [(q1, 2)], [(f[2], 0), (o1, 1)], [(f[3], 0)])
     for i in range(images):
         project(i, 2)
         outs.append(links.move(pairs.at[i], pairs_out.at[i]))
         tick()
-    while steps:
-        tick()
+    plan([(o0, 2)])
+    rest()
     go(query, 3)
     stack = inputs[:, patches:].reshape(images * lat, D)
     for g in range(GROUPS):
         made = dot(stack, weight_block(att, 0, g, sizes)) * HEAD ** (-0.5)
         queries[g] = made.astype(BF16)
     outs.append(links.move(queries, queries_out))
-    steps += [
-        lambda: (go(output, 2), start(cotangent)),
-        near(3),
-        lambda: go(output, 3),
-        near(4),
-    ]
+    plan([(f[4], 0)], [(o1, 2)], [(f[5], 0)])
     for i in range(images):
         attend(i)
         tick()
-    while steps:
-        tick()
-    steps += [
-        near(5),
-        lambda: (go(ff_rows[:1], 0), go(cotangent, 0)),
-        near(6),
-        lambda: go(ff_rows[1:2], 0),
-    ]
+        if i == 0:
+            start(cotangent)
+    rest()
+    go(output, 3)
+    outs.append(links.move(att, att_out))
+    outs.append(links.move(mixed, mixed_out))
+    plan([], [(f[6], 0)], [(cotangent[0], 0)], [(f[7], 0)])
     for i in range(images):
         finish(i)
         tick()
-    while steps:
-        tick()
-    go(hidden[7:], 0)
-    outs.append(links.move(att, att_out))
-    outs.append(links.move(mixed, mixed_out))
+    rest()
     outs.append(links.move(middle, middle_out))
-    go(ff_rows[2:], 0)
     go(cotangent, 1)
-    outs.append(links.move(back, back_out))
+    go(ff_rows, 0)
+    n = images * lat
+    cs, ys, zs = (sizes[a] for a in "cyz")
+    sib = links.place("c", 1)
+    xr = sizes["x"] * att.shape[5]
+
+    def first(q):
+        def one(yi, _):
+            before = dot(rows[yi].reshape(cs * n, D), ff[q, 0].reshape(D, tile))
+            up = dot(back[yi].reshape(cs * n, D), ff[q, 1].reshape(D, tile))
+            made, slope = gelu_and_slope(before)
+            hid[yi, :, :, q * tile : (q + 1) * tile] = made.astype(BF16).reshape(cs, n, tile)
+            bg[yi, :, :, q * tile : (q + 1) * tile] = (up * slope).astype(BF16).reshape(cs, n, tile)
+            return 0
+
+        lax.fori_loop(0, ys, one, 0)
+
     go(ff_rows, 1)
-    outs.append(links.move(rows, rows_out))
-    go(hidden, 1)
-    outs.append(links.move(ff, ff_out))
-    for part in everything:
-        part.close()
+    for q in range(quarters):
+        go(hidden[2 * q : 2 * q + 2], 1)
+        first(q)
+
+    ff_block = quarters * tile
+
+    def second(kind, yi):
+        wide = (hid if kind else bg)[yi].reshape(cs * n, ff_block)
+        made = added if kind else part
+
+        def one(z, _):
+            cols = pl.ds(pl.multiple_of(z * xr, xr), xr)
+            weight = jnp.concatenate([ff[q, kind, z].reshape(xr, tile) for q in range(quarters)], axis=1)
+            made[yi, :, :, cols] = dot_nt(wide, weight).astype(BF16).reshape(cs, n, xr)
+            return 0
+
+        lax.fori_loop(0, zs, one, 0)
+
+    sent, chip, along = [], {}, {}
+    for k in [*range(1, ys), 0]:
+        yi = links.place("y", k)
+        second(0, yi)
+        slot = links.take()
+        land = land_c.at[yi]
+        copy = links.copy(part.at[yi, sib], land, slot, "c", 1)
+        copy.start()
+        sent.append(copy)
+        chip[k] = links.copy(land, land, slot, "c", 1)
+    for k in range(1, ys):
+        yi = links.place("y", k)
+        chip[k].wait_recv()
+        summed = part[yi, at["c"]].astype(F32) + land_c[yi].astype(F32)
+        part[yi, at["c"]] = summed.astype(BF16)
+        slot = links.take()
+        land = land_y.at[k - 1]
+        copy = links.copy(part.at[yi, at["c"]], land, slot, "y", k)
+        copy.start()
+        sent.append(copy)
+        along[k] = links.copy(land, land, slot, "y", k)
+    for yi in range(ys):
+        second(1, yi)
+    outs.append(links.move(added, added_out))
+    for gather in hidden:
+        gather.close()
+
+    for m, (left, right) in ((1, (back, hid)), (0, (rows, bg))):
+
+        def one(z, _):
+            cols = pl.ds(pl.multiple_of(z * xr, xr), xr)
+            made = dot_tn(
+                left[:, :, :, cols].reshape(ys * cs * n, xr), right[...].reshape(ys * cs * n, ff_block)
+            ).astype(BF16)
+            for q in range(quarters):
+                ff[q, m, z] = made[:, q * tile : (q + 1) * tile].reshape(*ff.shape[3:5], tile)
+            return 0
+
+        lax.fori_loop(0, zs, one, 0)
+    outs.append(links.move(ff, ff_grad_out))
+    chip[0].wait_recv()
+    for k in range(1, ys):
+        along[k].wait_recv()
+
+    def back_one(t, carry):
+        gain, shift = carry
+        rws = pl.ds(pl.multiple_of(t * lat, lat), lat)
+        up = part[at["y"], at["c"], rws].astype(F32) + land_c[at["y"], rws].astype(F32)
+        for k in range(1, ys):
+            up = up + land_y[k - 1, rws].astype(F32)
+        hat, scale = normed(middle[rws])
+        value = cotangent_ref[rws] + norm_back(up, hat, scale, norm_ref[4:5])
+        middle_grad[rws] = value
+        branch[rws] = value.astype(BF16)
+        return gain + fold(up * hat), shift + fold(up)
+
+    zero = jnp.zeros((8, D), F32)
+    ff_norm[0], ff_norm[1] = lax.fori_loop(0, images, back_one, (zero, zero))
+    outs.append(links.move(middle_grad, middle_grad_out))
+    outs.append(links.move(branch, branch_out))
+    outs.append(links.move(ff_norm, ff_norm_out))
+    for copy in sent:
+        copy.wait_send()
+    for gather in everything:
+        if gather not in hidden:
+            gather.close()
     for out in outs:
         out.wait()
 
 
-def forward(att, expand, reduce_turned, tokens, latents, cotangent, counts, norm_params):
+def forward(att, expand, reduce, tokens, latents, cotangent, counts, norm_params):
     sizes = grid_of(lax.axis_size("dp"), lax.axis_size("head"))
     z, x, y, c = (sizes[a] for a in "zxyc")
     images, patches, _ = tokens.shape
@@ -447,37 +579,53 @@
     n = images * lat
     _, row_block, col_block = att.shape
     ff_block = expand.shape[1]
+    tile = min(GROUP, ff_block)
+    quarters = ff_block // tile
     shapes = dict(
         att=((4, y, c, z, x, row_block, col_block), BF16),
-        ff=((2, z, x, row_block, ff_block), BF16),
         pairs=((images, 2 * GROUPS, span, GROUP), BF16),
         turned=((D, images * span), BF16),
         queries=((GROUPS, n, GROUP), BF16),
         mixed=((GROUPS, n, GROUP), BF16),
+        ff=((quarters, 2, z, x, row_block, tile), BF16),
+        added=((y, c, n, D), BF16),
         middle=((n, D), F32),
-        rows=((y, c, n, D), BF16),
-        back=((y, c, n, D), BF16),
-    )
-    inside = [((images, patches, D), BF16), ((images, span, D), BF16)]
+        middle_grad=((n, D), F32),
+        branch=((n, D), BF16),
+        ff_norm=((2, 8, D), F32),
+    )
+    held = dict(shapes)
+    held.update(turned=((2, D, span), BF16))
+    inside = [
+        ((y, c, n, D), BF16),
+        ((y, c, n, D), BF16),
+        ((y, c, n, ff_block), BF16),
+        ((y, c, n, ff_block), BF16),
+        ((y, c, n, D), BF16),
+        ((y, n, D), BF16),
+        ((y - 1, n, D), BF16),
+        ((2, patches, D), BF16),
+        ((images, span, D), BF16),
+    ]
     per_att = sum(s - 1 for s in sizes.values())
-    slots = 8 * per_att + 8 * (z + x - 2) + (1 + images) * (y + c - 2)
+    slots = 8 * per_att + 8 * (z + x - 2) + (1 + images) * (y + c - 2) + 2 * y
     vmem, anywhere = pl.BlockSpec(memory_space=pltpu.VMEM), pl.BlockSpec(memory_space=pl.ANY)
     made = pl.pallas_call(
         functools.partial(forward_kernel, sizes),
         out_shape=[jax.ShapeDtypeStruct(*v) for v in shapes.values()],
         in_specs=[vmem, vmem, vmem, anywhere, vmem, vmem, pl.BlockSpec(memory_space=pltpu.SMEM), vmem],
         out_specs=[anywhere] * len(shapes),
-        scratch_shapes=[pltpu.VMEM(*v) for v in [*shapes.values(), *inside]]
+        scratch_shapes=[pltpu.VMEM(*v) for v in [*held.values(), *inside]]
         + [
             pltpu.SemaphoreType.DMA((slots,)),
             pltpu.SemaphoreType.DMA((slots,)),
-            pltpu.SemaphoreType.DMA((3 * images + 8,)),
+            pltpu.SemaphoreType.DMA((2 * images + 20,)),
         ],
         compiler_params=pltpu.CompilerParams(
-            collective_id=0, has_side_effects=True, vmem_limit_bytes=58 * MIB
+            collective_id=0, has_side_effects=True, vmem_limit_bytes=63 * MIB + 900 * 1024
         ),
         name="gather_and_attend",
-    )(att, expand, reduce_turned, tokens, latents.reshape(n, D), cotangent.reshape(n, D), counts, norm_params)
+    )(att, expand, reduce, tokens, latents.reshape(n, D), cotangent.reshape(n, D), counts, norm_params)
     return SimpleNamespace(**dict(zip(shapes, made)))
 
 
@@ -541,28 +689,6 @@
         for step in self.slots:
             for copy in self.copies(step):
                 copy.wait_send()
-
-
-def norm_back(up, hat, scale, gain):
-    inner = up * gain
-    return scale * (
-        inner
-        - jnp.mean(inner, axis=-1, keepdims=True)
-        - hat * jnp.mean(inner * hat, axis=-1, keepdims=True)
-    )
-
-
-def fold(rows):
-    return jnp.sum(rows.reshape(rows.shape[0] // 8, 8, rows.shape[1]), axis=0)
-
-
-def gelu_and_slope(v):
-    root = 0.7978845608028654
-    square = v * v
-    t = jnp.tanh(root * v * (1.0 + 0.044715 * square))
-    half = 0.5 + 0.5 * t
-    slope = half + (0.5 * root) * v * (1.0 - t * t) * (1.0 + (3.0 * 0.044715) * square)
-    return v * half, slope
 
 
 ATT_ORDERS = {0: ("yxz", "yxz"), 1: ("yxz", "xyz"), 2: ("yxz", "yxz"), 3: ("yxz", "yxz")}
@@ -592,10 +718,11 @@
     xr = xs * row_block
     heads = ys * cs
     half = row_block // 2
-    norm_ref, middle, cotangent, latents = r.norm, r.middle, r.cotangent, r.latents
+    norm_ref, latents = r.norm, r.latents
     queries, mixed = r.queries, r.mixed
     grads_ff = r.grads_ff
-    middle_grad, branch, mixed_grad, query_back = r.middle_grad, r.branch, r.mixed_grad, r.query_back
+    middle_grad, branch, latent_low = r.middle_grad, r.branch, r.latent_low
+    mixed_grad, query_back = r.mixed_grad, r.query_back
     outs = []
 
     units = [(m, k) for k in [*range(1, zs), 0] for m in (1, 0)]
@@ -607,171 +734,99 @@
         z = links.place("z", k)
         for j, slot in enumerate(x_slots[unit], 1):
             yield links.copy(
-                grads_ff.at[m, z, links.place("x", j)], r.ff_land_x.at[m, z, j - 1], slot, "x", j
+                grads_ff.at[:, m, z, links.place("x", j)], r.ff_land_x.at[m, z, j - 1], slot, "x", j
             )
 
     def z_copy(unit):
         m, k = unit
         return links.copy(
-            grads_ff.at[m, links.place("z", k), at["x"]], r.ff_land_z.at[m, k - 1], z_slots[unit], "z", k
+            grads_ff.at[:, m, links.place("z", k), at["x"]], r.ff_land_z.at[m, k - 1], z_slots[unit], "z", k
         )
+
+    quarters, tile = grads_ff.shape[0], grads_ff.shape[-1]
 
     def ff_along(unit):
         m, k = unit
         z = links.place("z", k)
         for copy in x_copies(unit):
             copy.wait_recv()
-        total = grads_ff[m, z, at["x"]].astype(F32)
-        for j in range(xs - 1):
-            total = total + r.ff_land_x[m, z, j].astype(F32)
+        for q in range(quarters):
+            total = grads_ff[q, m, z, at["x"]].astype(F32)
+            for j in range(xs - 1):
+                total = total + r.ff_land_x[m, z, j, q].astype(F32)
+            if k:
+                grads_ff[q, m, z, at["x"]] = total.astype(BF16)
+            else:
+                r.ff_share[m, :, q * tile : (q + 1) * tile] = total
         if k:
-            grads_ff[m, z, at["x"]] = total.astype(BF16)
             z_copy(unit).start()
-        else:
-            r.ff_share[m] = total
 
     def ff_finish():
         for m in range(2):
             for k in range(1, zs):
                 z_copy((m, k)).wait_recv()
-            total = r.ff_share[m]
-            for k in range(1, zs):
-                total = total + r.ff_land_z[m, k - 1].astype(F32)
-            r.ff_share[m] = total
+            for q in range(quarters):
+                cols = pl.ds(q * tile, tile)
+                total = r.ff_share[m, :, cols]
+                for k in range(1, zs):
+                    total = total + r.ff_land_z[m, k - 1, q].astype(F32)
+                r.ff_share[m, :, cols] = total
 
     pairs = r.pairs_here
     early = [links.move(r.pairs.at[i], pairs.at[i]) for i in range(images)]
 
-    def feed_forward(ffw, rows, back, hidden, bg, part):
-        loads = [links.move(r.ff, ffw), links.move(r.rows, rows), links.move(r.back, back)]
-        links.meet()
-        for load in loads:
-            load.wait()
-        tile = min(GROUP, ff_block)
-
-        def first(yi):
-            def one(t, _):
-                cols = pl.ds(pl.multiple_of(t * tile, tile), tile)
-                before = dot(rows[yi].reshape(cs * n, D), ffw[0, :, :, :, cols].reshape(D, tile))
-                up = dot(back[yi].reshape(cs * n, D), ffw[1, :, :, :, cols].reshape(D, tile))
-                made, slope = gelu_and_slope(before)
-                hidden[yi, :, :, cols] = made.astype(BF16).reshape(cs, n, tile)
-                bg[yi, :, :, cols] = (up * slope).astype(BF16).reshape(cs, n, tile)
-                return 0
-
-            lax.fori_loop(0, ff_block // tile, one, 0)
-
-        def second(kind, yi):
-            left = hidden if kind else bg
-
-            def one(z, _):
-                cols = pl.ds(pl.multiple_of(z * xr, xr), xr)
-                made = dot_nt(left[yi].reshape(cs * n, ff_block), ffw[kind, z].reshape(xr, ff_block))
-                part[kind, yi, :, :, cols] = made.astype(BF16).reshape(cs, n, xr)
-                return 0
-
-            lax.fori_loop(0, zs, one, 0)
-
-        sent, chip, along = [], {}, {}
-
-        def to_sibling(kind, k):
-            yi = links.place("y", k)
-            slot = links.take()
-            land = r.land_c.at[kind, yi]
-            copy = links.copy(part.at[kind, yi, sib], land, slot, "c", 1)
+    load = links.move(r.ff_grad, grads_ff)
+    own = links.move(r.added.at[:, at["c"]], r.added_here)
+    links.meet()
+    load.wait()
+    for unit in units:
+        for copy in x_copies(unit):
             copy.start()
-            sent.append(copy)
-            chip[kind, k] = links.copy(land, land, slot, "c", 1)
-
-        def along_y(kind, k):
-            yi = links.place("y", k)
-            chip[kind, k].wait_recv()
-            summed = part[kind, yi, at["c"]].astype(F32) + r.land_c[kind, yi].astype(F32)
-            r.sum_y[kind, k - 1] = summed.astype(BF16)
-            slot = links.take()
-            land = r.land_y.at[kind, k - 1]
-            copy = links.copy(r.sum_y.at[kind, k - 1], land, slot, "y", k)
-            copy.start()
-            along[kind, k] = (copy, links.copy(land, land, slot, "y", k))
-
+
+    c_slots = [links.take() for _ in range(ys)]
+    y_slots = [links.take() for _ in range(1, ys)]
+
+    def added_chip(k):
+        yi = links.place("y", k)
+        return links.copy(r.added.at[yi, sib], r.added_land_c.at[yi], c_slots[k], "c", 1)
+
+    def added_along(k):
+        return links.copy(r.added_here.at[links.place("y", k)], r.added_land_y.at[k - 1], y_slots[k - 1], "y", k)
+
+    for k in range(ys):
+        added_chip(k).start()
+    own.wait()
+
+    def added_out():
         for k in range(1, ys):
             yi = links.place("y", k)
-            first(yi)
-            second(0, yi)
-            to_sibling(0, k)
-            second(1, yi)
-            to_sibling(1, k)
-        first(at["y"])
+            added_chip(k).wait_recv()
+            summed = r.added_here[yi].astype(F32) + r.added_land_c[yi].astype(F32)
+            r.added_here[yi] = summed.astype(BF16)
+            added_along(k).start()
+
+    def added_finish():
+        added_chip(0).wait_recv()
         for k in range(1, ys):
-            along_y(0, k)
-        second(0, at["y"])
-        to_sibling(0, 0)
-        second(1, at["y"])
-        to_sibling(1, 0)
+            added_along(k).wait_recv()
+
+        def one(t, _):
+            rws = pl.ds(pl.multiple_of(t * lat, lat), lat)
+            up = r.added_here[at["y"], rws].astype(F32) + r.added_land_c[at["y"], rws].astype(F32)
+            for k in range(1, ys):
+                up = up + r.added_land_y[k - 1, rws].astype(F32)
+            latent_low[rws] = (r.middle[rws] + up).astype(BF16)
+            return 0
+
+        lax.fori_loop(0, images, one, 0)
+        for k in range(ys):
+            added_chip(k).wait_send()
         for k in range(1, ys):
-            along_y(1, k)
-
-        def gradient(unit):
-            m, k = unit
-            z = links.place("z", k)
-            cols = pl.ds(pl.multiple_of(z * xr, xr), xr)
-            left, right = (back, hidden) if m else (rows, bg)
-            made = dot_tn(left[:, :, :, cols].reshape(heads * n, xr), right[...].reshape(heads * n, ff_block))
-            grads_ff[m, z] = made.astype(BF16).reshape(xs, row_block, ff_block)
-            for copy in x_copies(unit):
-                copy.start()
-
-        for unit in units:
-            gradient(unit)
-        chip[0, 0].wait_recv()
-        for k in range(1, ys):
-            along[0, k][1].wait_recv()
-
-        def back_one(t, carry):
-            gain, shift = carry
-            rws = pl.ds(pl.multiple_of(t * lat, lat), lat)
-            up = part[0, at["y"], at["c"], rws].astype(F32) + r.land_c[0, at["y"], rws].astype(F32)
-            for k in range(1, ys):
-                up = up + r.land_y[0, k - 1, rws].astype(F32)
-            hat, scale = normed(middle[rws])
-            value = cotangent[rws] + norm_back(up, hat, scale, norm_ref[4:5])
-            middle_grad[rws] = value
-            branch[rws] = value.astype(BF16)
-            return gain + fold(up * hat), shift + fold(up)
-
-        zero = jnp.zeros((8, D), F32)
-        ff_gain, ff_shift = lax.fori_loop(0, images, back_one, (zero, zero))
-        r.norm_parts[4] = ff_gain
-        r.norm_parts[5] = ff_shift
-        chip[1, 0].wait_recv()
-        for k in range(1, ys):
-            along[1, k][1].wait_recv()
-
-        def out_one(t, _):
-            rws = pl.ds(pl.multiple_of(t * lat, lat), lat)
-            up = part[1, at["y"], at["c"], rws].astype(F32) + r.land_c[1, at["y"], rws].astype(F32)
-            for k in range(1, ys):
-                up = up + r.land_y[1, k - 1, rws].astype(F32)
-            rows[at["y"], at["c"], rws] = (middle[rws] + up).astype(BF16)
-            return 0
-
-        lax.fori_loop(0, images, out_one, 0)
-        leaving = links.move(rows.at[at["y"], at["c"]], r.resampled)
-        for copy in sent:
-            copy.wait_send()
-        for copy, _ in along.values():
-            copy.wait_send()
-        leaving.wait()
-
-    pl.run_scoped(
-        feed_forward,
-        pltpu.VMEM((2, zs, xs, row_block, ff_block), BF16),
-        pltpu.VMEM((ys, cs, n, D), BF16),
-        pltpu.VMEM((ys, cs, n, D), BF16),
-        pltpu.VMEM((ys, cs, n, ff_block), BF16),
-        pltpu.VMEM((ys, cs, n, ff_block), BF16),
-        pltpu.VMEM((2, ys, cs, n, D), BF16),
-    )
+            added_along(k).wait_send()
+        return links.move(latent_low, r.resampled)
+
+    r.norm_parts[4] = r.ff_norm[0]
+    r.norm_parts[5] = r.ff_norm[1]
 
     steps = []
 
@@ -896,7 +951,7 @@
                     wide.append(jnp.concatenate(blocks, axis=0))
                 mixed_grad[g] = dot_nt(branch[...], jnp.concatenate(wide, axis=1)).astype(BF16)
             ff_steps = [lambda u=u: ff_along(u) for u in units]
-            steps.append(lambda: (chip_sum(3), ff_steps[0]()))
+            steps.append(lambda: (chip_sum(3), ff_steps[0](), added_out()))
             steps.extend(ff_steps[1:])
             for i in range(images):
                 attend(i)
@@ -905,6 +960,7 @@
             for i in range(images):
                 turned_left[:, pl.ds(i * lat, lat)] = turned[:, i * span + patches : (i + 1) * span]
             products(0, lambda: turned_left[...], query_columns)
+            resampled = added_finish()
             steps.insert(0, lambda: go(3, 0))
             steps.insert(2, lambda: chip_sum(0))
             tick()
@@ -913,6 +969,7 @@
             tick()
             products(1, lambda: turned[...], columns(1), tick)
             tick()
+            resampled.wait()
 
         pl.run_scoped(
             weights,
@@ -978,7 +1035,7 @@
                 hat, scale = normed(latents[rws].astype(F32))
                 up = pair_grad[patches:]
                 made = middle_grad[rws] + norm_back(up, hat, scale, norm_ref[2:3])
-                branch[rws] = made.astype(BF16)
+                latent_low[rws] = made.astype(BF16)
                 sums = (gain, shift, sums[2] + fold(up * hat), sums[3] + fold(up))
                 tick()
                 tick()
@@ -1016,7 +1073,7 @@
         pltpu.VMEM((D, n), BF16),
     )
 
-    outs.append(links.move(branch, r.latent_grad))
+    outs.append(links.move(latent_low, r.latent_grad))
     squares = jnp.sum(r.att_share[...] * r.att_share[...]) + jnp.sum(r.ff_share[...] * r.ff_share[...])
     rows = [jnp.sum(r.norm_parts[k], axis=0, keepdims=True) for k in range(6)]
     value = jnp.concatenate([*rows, jnp.full((2, D), squares, F32)], axis=0)
@@ -1045,7 +1102,7 @@
         out.wait()
 
 
-def backward(got, tokens, latents, cotangent, counts, norm_params, row_block, col_block, ff_block):
+def backward(got, tokens, latents, counts, norm_params, row_block, col_block, ff_block):
     sizes = grid_of(lax.axis_size("dp"), lax.axis_size("head"))
     zs, xs, ys, cs = (sizes[a] for a in "zxyc")
     images, patches, _ = tokens.shape
@@ -1056,17 +1113,18 @@
     smem = pl.BlockSpec(memory_space=pltpu.SMEM)
     inputs = dict(
         att=(got.att, anywhere),
-        ff=(got.ff, anywhere),
-        rows=(got.rows, anywhere),
-        back=(got.back, anywhere),
+        ff_grad=(got.ff, anywhere),
+        added=(got.added, anywhere),
+        middle=(got.middle, vmem),
         pairs=(got.pairs, anywhere),
         turned=(got.turned, anywhere),
         tokens=(tokens, anywhere),
         queries=(got.queries, vmem),
         mixed=(got.mixed, vmem),
-        middle=(got.middle, vmem),
+        middle_grad=(got.middle_grad, vmem),
+        branch=(got.branch, vmem),
+        ff_norm=(got.ff_norm, vmem),
         latents=(latents.reshape(n, D), vmem),
-        cotangent=(cotangent.reshape(n, D), vmem),
         norm=(norm_params, vmem),
         counts=(counts, smem),
     )
@@ -1079,16 +1137,15 @@
         totals=((8, D), F32, vmem),
     )
     scratch = dict(
-        grads_ff=((2, zs, xs, row_block, ff_block), BF16),
-        ff_land_x=((2, zs, xs - 1, row_block, ff_block), BF16),
-        ff_land_z=((2, zs - 1, row_block, ff_block), BF16),
+        grads_ff=(got.ff.shape, BF16),
+        ff_land_x=((2, zs, xs - 1, got.ff.shape[0], row_block, got.ff.shape[-1]), BF16),
+        ff_land_z=((2, zs - 1, got.ff.shape[0], row_block, got.ff.shape[-1]), BF16),
+        added_here=((ys, n, D), BF16),
+        added_land_c=((ys, n, D), BF16),
+        added_land_y=((ys - 1, n, D), BF16),
         att_land_c=((4, ys, zs, xs, row_block, col_block), BF16),
         pairs_here=(got.pairs.shape, BF16),
-        land_c=((2, ys, n, D), BF16),
-        land_y=((2, ys - 1, n, D), BF16),
-        sum_y=((2, ys - 1, n, D), BF16),
-        middle_grad=((n, D), F32),
-        branch=((n, D), BF16),
+        latent_low=((n, D), BF16),
         mixed_grad=((GROUPS, n, GROUP), BF16),
         query_back=((GROUPS, n, GROUP), BF16),
         norm_parts=((6, 8, D), F32),
@@ -1101,7 +1158,7 @@
                 lands[m, s, step] = (shape, BF16)
     steps = sum(v - 1 for v in sizes.values())
     slots = 9 * steps + 2 * (zs * xs + zs) + 6 * ys
-    semaphores = dict(send=slots, recv=slots, local=3 * images + 16)
+    semaphores = dict(send=slots, recv=slots, local=3 * images + 30)
     names = [*inputs, *outputs, *semaphores, *scratch]
     made = pl.pallas_call(
         functools.partial(backward_kernel, sizes, (names, tuple(lands), images, patches, lat, ff_block)),
@@ -1127,6 +1184,69 @@
         first_hat / (jnp.sqrt(second_hat) + ADAM_EPS) + decay_rate * master
     )
     return (master_new, first_new, second_new)
+
+
+def update_kernel(cuts, *refs):
+    shares, refs = refs[:4], refs[4:]
+    att, expand, reduce, norm, refs = refs[:3], refs[3:6], refs[6:9], refs[9:12], refs[12:]
+    carried, refs = refs[:3], refs[3:]
+    att_out, expand_out, reduce_out, norm_out, refs = refs[:3], refs[3:6], refs[6:9], refs[9:12], refs[12:]
+    size_out, carried_out = refs[0], refs[1:4]
+    att_share, expand_share, reduce_share, totals = shares
+    step = pl.program_id(0)
+    for a, b in zip(carried, carried_out):
+        b[...] = a[...]
+    norm_total = totals[:6]
+    squares = totals[6:7, :1] + jnp.sum(norm_total * norm_total).reshape(1, 1)
+    size = jnp.sqrt(squares)
+    clip = jnp.minimum(1.0, MAX_NORM / (size + 1e-06))
+
+    def write(outs, values):
+        for out, value in zip(outs, values):
+            out[...] = value
+
+    write(att_out, adam_step(*(v[...] for v in att), att_share[...] * clip[None], MATRIX_RATE, DECAY_RATE))
+    write(expand_out, adam_step(*(v[...] for v in expand), expand_share[0] * clip, MATRIX_RATE, DECAY_RATE))
+    write(reduce_out, adam_step(*(v[...] for v in reduce), reduce_share[0].T * clip, MATRIX_RATE, DECAY_RATE))
+
+    @pl.when(step == cuts - 1)
+    def _():
+        size_out[...] = size
+        write(norm_out, adam_step(*(v[...] for v in norm), norm_total * clip, NORM_RATE, 0.0))
+
+
+def update(back, attention, expand, reduce, norm):
+    cuts = 4
+    _, row_block, col_block = attention[0].shape
+    ff_block = expand[0].shape[1]
+    att_spec = pl.BlockSpec((1, row_block, col_block), lambda j: (j, 0, 0))
+    expand_spec = pl.BlockSpec((row_block // cuts, ff_block), lambda j: (j, 0))
+    reduce_spec = pl.BlockSpec((ff_block // cuts, row_block), lambda j: (j, 0))
+    norm_spec = pl.BlockSpec(norm[0].shape, lambda j: (0, 0))
+    shapes = [*attention, *expand, *reduce, *norm]
+    specs = [att_spec] * 3 + [expand_spec] * 3 + [reduce_spec] * 3 + [norm_spec] * 3
+    carried = [back.resampled, back.media_grad.reshape(-1, D), back.latent_grad]
+    carried_specs = [pl.BlockSpec((v.shape[0] // cuts, D), lambda j: (j, 0)) for v in carried]
+    out_shape = [jax.ShapeDtypeStruct(v.shape, v.dtype) for v in shapes]
+    out_shape += [jax.ShapeDtypeStruct((1, 1), F32)]
+    out_shape += [jax.ShapeDtypeStruct(v.shape, v.dtype) for v in carried]
+    made = pl.pallas_call(
+        functools.partial(update_kernel, cuts),
+        grid=(cuts,),
+        out_shape=out_shape,
+        in_specs=[
+            att_spec,
+            pl.BlockSpec((1, row_block // cuts, ff_block), lambda j: (0, j, 0)),
+            pl.BlockSpec((1, row_block, ff_block // cuts), lambda j: (1, 0, j)),
+            pl.BlockSpec((8, D), lambda j: (0, 0)),
+            *specs,
+            *carried_specs,
+        ],
+        out_specs=[*specs, pl.BlockSpec((1, 1), lambda j: (0, 0)), *carried_specs],
+        compiler_params=pltpu.CompilerParams(vmem_limit_bytes=63 * MIB),
+        name="update_kernel",
+    )(back.att_share, back.ff_share, back.ff_share, back.totals, *shapes, *carried)
+    return made[:12], made[12], made[13:]
 
 
 def on_device(
@@ -1151,7 +1271,7 @@
     got = forward(
         attention_weights,
         expand_weight,
-        reduce_weight.T,
+        reduce_weight,
         media_tokens,
         latents,
         cotangent,
@@ -1159,35 +1279,21 @@
         norm_params,
     )
     back = backward(
-        got, media_tokens, latents, cotangent, counts, norm_params, row_block, col_block, expand_weight.shape[1]
-    )
-    norm_total, squares_total = back.totals[:6], back.totals[6, 0]
-    grad_norm = jnp.sqrt(squares_total + jnp.sum(norm_total * norm_total))
-    clip_factor = jnp.minimum(1.0, MAX_NORM / (grad_norm + 1e-06))
-    attention = adam_step(
-        attention_weights,
-        attention_first,
-        attention_second,
-        back.att_share * clip_factor,
-        MATRIX_RATE,
-        DECAY_RATE,
-    )
-    expand = adam_step(
-        expand_weight, expand_first, expand_second, back.ff_share[0] * clip_factor, MATRIX_RATE, DECAY_RATE
-    )
-    reduce = adam_step(
-        reduce_weight, reduce_first, reduce_second, back.ff_share[1].T * clip_factor, MATRIX_RATE, DECAY_RATE
-    )
-    norm = adam_step(norm_params, norm_first, norm_second, norm_total * clip_factor, NORM_RATE, 0.0)
+        got, media_tokens, latents, counts, norm_params, row_block, col_block, expand_weight.shape[1]
+    )
+    made, size, (resampled, media_grad, latent_grad) = update(
+        back,
+        (attention_weights, attention_first, attention_second),
+        (expand_weight, expand_first, expand_second),
+        (reduce_weight, reduce_first, reduce_second),
+        (norm_params, norm_first, norm_second),
+    )
     return (
-        back.resampled.reshape(latents.shape),
-        back.media_grad,
-        back.latent_grad.reshape(latents.shape),
-        grad_norm,
-        *attention,
-        *expand,
-        *reduce,
-        *norm,
+        resampled.reshape(latents.shape),
+        media_grad.reshape(media_tokens.shape),
+        latent_grad.reshape(latents.shape),
+        size.reshape(()),
+        *made,
     )
 
 

time: 278 us -> 248 us (0.89)
  local copies, waits for them, and re-layouts: 13.3 us -> 0 us
  other arithmetic: 10.2 us -> 0 us
  Pallas kernels: 250 us -> 245 us
    pallas_call x1, Pallas kernels: 140 us -> 117 us  [backward(): pl.pallas_call(functools.partial(backward_kernel, sizes, (names, tuple(la...]
    unnamed x25 -> x0, local copies, waits for them, and re-layouts: 12.1 us -> none
    pallas_call x0 -> x1, Pallas kernels: none -> 9.62 us  [update(): pl.pallas_call(functools.partial(update_kernel, cuts), grid=(cuts,), out_...]
    sub x4 -> x0, other arithmetic: 8.83 us -> none  [adam_step(): master - step_rate * (first_hat / (jnp.sqrt(second_hat) + ADAM_EPS) + dec...]
    pallas_call x1, Pallas kernels: 110 us -> 118 us  [forward(): pl.pallas_call(functools.partial(forward_kernel, sizes), out_shape=[jax.S...]
where the time goes in v3:
time: 248 us; the launch traced here: 246 us
  Pallas kernels  245 us (99%)
    pallas_call x1, Pallas kernels, forward(): pl.pallas_call(functools.partial(forward_kernel, sizes), out_shape=[jax.S...  118 us
    pallas_call x1, Pallas kernels, backward(): pl.pallas_call(functools.partial(backward_kernel, sizes, (names, tuple(la...  117 us
    pallas_call x1, Pallas kernels, update(): pl.pallas_call(functools.partial(update_kernel, cuts), grid=(cuts,), out_...  9.62 us

profile of v3, /device:TPU:10, one launch (start us, length us, event | category | flops | bytes accessed | tf_op | source)
XLA Modules:
  0.0 245.9 jit_solution(18089214350468391940)
XLA Ops:
  0.6 118.4 %gather_and_attend.1 = (bf16[4,2,2,4,2,128,256]{6,5,4,3,2,1,0:T(8,128)(2,1)}, bf16[4,8,640,256]{3,2,1,0:T(8,128)(2,1)}, bf16[1024,2560]{1,0:T(8,128)(2,1)}, bf16...) custom-call(f32[4,128,256]{2,1,0:T(8,128)} %refs_4_.1, ...), custom_call_target="tpu_custom_call" | custom-call | tf_op jit(solution)/shard_map/gather_and_attend/pallas_call | solution.py:613
  119.1 117.0 %backward_and_scatter.1 = (bf16[256,1024]{1,0:T(8,128)(2,1)}, bf16[4,576,1024]{2,1,0:T(8,128)(2,1)}, bf16[256,1024]{1,0:T(8,128)(2,1)}, f32[4,128,256]{2,1,0:T(8...) custom-call(bf16[4,2,2,4,2,128,256]{6,5,4,3,2,1,0:T(8,128)(2,1)} %get-tuple-element.49.refs_0_, ...), custom_call_target="tpu_custom_call" | custom-call | tf_op jit(solution)/shard_map/backward_and_scatter/pallas_call | solution.py:1163
  236.1 9.6 %update_kernel.1 = (f32[4,128,256]{2,1,0:T(8,128)}, f32[4,128,256]{2,1,0:T(8,128)}, f32[4,128,256]{2,1,0:T(8,128)}, f32[128,1024]{1,0:T(8,128)}, f32[128,1024]{1...) custom-call(f32[4,128,256]{2,1,0:T(8,128)} %get-tuple-element.60.ref, ...), custom_call_target="tpu_custom_call" | custom-call | tf_op jit(solution)/shard_map/update_kernel/pallas_call | solution.py:1233

commit v4 on v3

--- a/solution.py
+++ b/solution.py
@@ -28,6 +28,7 @@
 F32 = jnp.float32
 BF16 = jnp.bfloat16
 MIB = 2**20
+EARLY = 2
 
 
 def grid_of(dp_count, head_count):
@@ -53,33 +54,40 @@
     def place(self, axis, k):
         return lax.rem(self.at[axis] + k, self.sizes[axis])
 
-    def peer(self, axis, k):
+    def peer(self, steps):
         at = dict(self.at)
-        at[axis] = self.place(axis, k)
+        for axis, k in steps.items():
+            at[axis] = self.place(axis, k)
         return {
             "dp": at["z"] * self.sizes["x"] + at["x"],
             "head": at["y"] * self.sizes["c"] + at["c"],
         }
 
-    def greet(self):
+    def around(self, axes):
+        ways = [{}]
+        for axis in axes:
+            ways = [{**way, axis: k} for way in ways for k in range(self.sizes[axis])]
+        return ways[1:]
+
+    def greet(self, *groups):
         barrier = pltpu.get_barrier_semaphore()
-        for axis, n in self.sizes.items():
-            for k in range(1, n):
-                pl.semaphore_signal(
-                    barrier, inc=1, device_id=self.peer(axis, k), device_id_type=MESH
-                )
+        self.met = [way for axes in groups for way in self.around(axes)]
+        for way in self.met:
+            pl.semaphore_signal(barrier, inc=1, device_id=self.peer(way), device_id_type=MESH)
 
     def meet(self):
-        barrier = pltpu.get_barrier_semaphore()
-        pl.semaphore_wait(barrier, sum(n - 1 for n in self.sizes.values()))
+        pl.semaphore_wait(pltpu.get_barrier_semaphore(), len(self.met))
 
     def copy(self, src, dst, slot, axis, k):
+        return self.send_to(src, dst, slot, {axis: k})
+
+    def send_to(self, src, dst, slot, way):
         return pltpu.make_async_remote_copy(
             src_ref=src,
             dst_ref=dst,
             send_sem=self.send.at[slot],
             recv_sem=self.recv.at[slot],
-            device_id=self.peer(axis, k),
+            device_id=self.peer(way),
             device_id_type=MESH,
         )
 
@@ -252,6 +260,7 @@
     part,
     land_c,
     land_y,
+    land_x,
     tokens,
     inputs,
     send,
@@ -259,7 +268,7 @@
     local,
 ):
     links = Links(sizes, send, recv, local)
-    links.greet()
+    links.greet(*"zxyc")
     images, span, _ = inputs.shape
     patches = tokens_ref.shape[1]
     lat = span - patches
@@ -521,25 +530,46 @@
         copy.start()
         sent.append(copy)
         along[k] = links.copy(land, land, slot, "y", k)
+    for gather in hidden:
+        gather.close()
+
+    def gradient(m, z):
+        left, right = (back, hid) if m else (rows, bg)
+        cols = pl.ds(pl.multiple_of(z * xr, xr), xr)
+        made = dot_tn(
+            left[:, :, :, cols].reshape(ys * cs * n, xr), right[...].reshape(ys * cs * n, ff_block)
+        ).astype(BF16)
+        for q in range(quarters):
+            ff[q, m, z] = made[:, q * tile : (q + 1) * tile].reshape(*ff.shape[3:5], tile)
+
+    xs = sizes["x"]
+    early = range(1, 1 + land_x.shape[0])
+    x_slots = {k: [links.take() for _ in range(1, xs)] for k in early}
+
+    def x_copies(k):
+        for j, slot in enumerate(x_slots[k], 1):
+            block = ff.at[:, 0, links.place("z", k), links.place("x", j)]
+            yield links.copy(block, land_x.at[k - 1, j - 1], slot, "x", j)
+
+    for k in early:
+        gradient(0, links.place("z", k))
+        for copy in x_copies(k):
+            copy.start()
     for yi in range(ys):
         second(1, yi)
     outs.append(links.move(added, added_out))
-    for gather in hidden:
-        gather.close()
-
-    for m, (left, right) in ((1, (back, hid)), (0, (rows, bg))):
-
-        def one(z, _):
-            cols = pl.ds(pl.multiple_of(z * xr, xr), xr)
-            made = dot_tn(
-                left[:, :, :, cols].reshape(ys * cs * n, xr), right[...].reshape(ys * cs * n, ff_block)
-            ).astype(BF16)
-            for q in range(quarters):
-                ff[q, m, z] = made[:, q * tile : (q + 1) * tile].reshape(*ff.shape[3:5], tile)
-            return 0
-
-        lax.fori_loop(0, zs, one, 0)
-    outs.append(links.move(ff, ff_grad_out))
+
+    def other(k, _):
+        gradient(0, links.place("z", k))
+        return 0
+
+    lax.fori_loop(1 + len(early), zs + 1, other, 0)
+
+    def both(z, _):
+        gradient(1, z)
+        return 0
+
+    lax.fori_loop(0, zs, both, 0)
     chip[0].wait_recv()
     for k in range(1, ys):
         along[k].wait_recv()
@@ -561,6 +591,18 @@
     outs.append(links.move(middle_grad, middle_grad_out))
     outs.append(links.move(branch, branch_out))
     outs.append(links.move(ff_norm, ff_norm_out))
+    for k in early:
+        for copy in x_copies(k):
+            copy.wait_recv()
+        z = links.place("z", k)
+        for q in range(quarters):
+            total = ff[q, 0, z, at["x"]].astype(F32)
+            for j in range(xs - 1):
+                total = total + land_x[k - 1, j, q].astype(F32)
+            ff[q, 0, z, at["x"]] = total.astype(BF16)
+        for copy in x_copies(k):
+            copy.wait_send()
+    outs.append(links.move(ff, ff_grad_out))
     for copy in sent:
         copy.wait_send()
     for gather in everything:
@@ -604,11 +646,12 @@
         ((y, c, n, D), BF16),
         ((y, n, D), BF16),
         ((y - 1, n, D), BF16),
+        ((EARLY, x - 1, quarters, row_block, tile), BF16),
         ((2, patches, D), BF16),
         ((images, span, D), BF16),
     ]
     per_att = sum(s - 1 for s in sizes.values())
-    slots = 8 * per_att + 8 * (z + x - 2) + (1 + images) * (y + c - 2) + 2 * y
+    slots = 8 * per_att + 8 * (z + x - 2) + (1 + images) * (y + c - 2) + 2 * y + EARLY * x
     vmem, anywhere = pl.BlockSpec(memory_space=pltpu.VMEM), pl.BlockSpec(memory_space=pl.ANY)
     made = pl.pallas_call(
         functools.partial(forward_kernel, sizes),
@@ -691,7 +734,7 @@
                 copy.wait_send()
 
 
-ATT_ORDERS = {0: ("yxz", "yxz"), 1: ("yxz", "xyz"), 2: ("yxz", "yxz"), 3: ("yxz", "yxz")}
+ATT_ORDERS = {0: ("yxz", "yxz"), 1: ("yxz", "xyz"), 2: ("yxz", "xyz"), 3: ("yxz", "yxz")}
 
 
 def land_shapes(sizes, order, axes, tail):
@@ -706,9 +749,10 @@
     names, keys, images, patches, lat, ff_block = dims
     r = SimpleNamespace(**dict(zip(names, refs)))
     total_lands = dict(zip("cyxz", refs[len(names) :]))
-    att_lands = dict(zip(keys, refs[len(names) + 4 :]))
+    r.square_lands = refs[len(names) + 4 : len(names) + 6]
+    att_lands = dict(zip(keys, refs[len(names) + 6 :]))
     links = Links(sizes, r.send, r.recv, r.local)
-    links.greet()
+    links.greet("zx", "yc")
     at = links.at
     sib = links.place("c", 1)
     n = images * lat
@@ -725,9 +769,11 @@
     mixed_grad, query_back = r.mixed_grad, r.query_back
     outs = []
 
-    units = [(m, k) for k in [*range(1, zs), 0] for m in (1, 0)]
+    units = [(m, k) for k in [*range(1, zs), 0] for m in range(2)]
+    ready = [(0, k) for k in range(1, 1 + EARLY)]
+    units = [unit for unit in units if unit not in ready]
     x_slots = {unit: [links.take() for _ in range(1, xs)] for unit in units}
-    z_slots = {unit: links.take() for unit in units if unit[1]}
+    z_slots = {unit: links.take() for unit in units + ready if unit[1]}
 
     def x_copies(unit):
         m, k = unit
@@ -782,6 +828,8 @@
     for unit in units:
         for copy in x_copies(unit):
             copy.start()
+    for unit in ready:
+        z_copy(unit).start()
 
     c_slots = [links.take() for _ in range(ys)]
     y_slots = [links.take() for _ in range(1, ys)]
@@ -805,6 +853,8 @@
             r.added_here[yi] = summed.astype(BF16)
             added_along(k).start()
 
+    resampled_low = r.added_here.at[at["y"]]
+
     def added_finish():
         added_chip(0).wait_recv()
         for k in range(1, ys):
@@ -815,7 +865,7 @@
             up = r.added_here[at["y"], rws].astype(F32) + r.added_land_c[at["y"], rws].astype(F32)
             for k in range(1, ys):
                 up = up + r.added_land_y[k - 1, rws].astype(F32)
-            latent_low[rws] = (r.middle[rws] + up).astype(BF16)
+            resampled_low[rws] = (r.middle[rws] + up).astype(BF16)
             return 0
 
         lax.fori_loop(0, images, one, 0)
@@ -823,7 +873,7 @@
             added_chip(k).wait_send()
         for k in range(1, ys):
             added_along(k).wait_send()
-        return links.move(latent_low, r.resampled)
+        return links.move(resampled_low, r.resampled)
 
     r.norm_parts[4] = r.ff_norm[0]
     r.norm_parts[5] = r.ff_norm[1]
@@ -834,8 +884,10 @@
         if steps:
             steps.pop(0)()
 
-    def later(f, *args):
-        steps.append(lambda: f(*args))
+    def plan(*calls):
+        steps.append(lambda: [f(*args) for f, *args in calls])
+
+    waiting = []
 
     def attention(grads, turned_left):
         per = GROUP // col_block
@@ -951,25 +1003,25 @@
                     wide.append(jnp.concatenate(blocks, axis=0))
                 mixed_grad[g] = dot_nt(branch[...], jnp.concatenate(wide, axis=1)).astype(BF16)
             ff_steps = [lambda u=u: ff_along(u) for u in units]
-            steps.append(lambda: (chip_sum(3), ff_steps[0](), added_out()))
-            steps.extend(ff_steps[1:])
+            plan((chip_sum, 3), (ff_steps[0],))
+            plan((ff_steps[1],))
+            plan()
+            plan((ff_steps[2],))
             for i in range(images):
                 attend(i)
+                tick()
+            while steps:
                 tick()
             load_turned.wait()
             for i in range(images):
                 turned_left[:, pl.ds(i * lat, lat)] = turned[:, i * span + patches : (i + 1) * span]
             products(0, lambda: turned_left[...], query_columns)
-            resampled = added_finish()
-            steps.insert(0, lambda: go(3, 0))
-            steps.insert(2, lambda: chip_sum(0))
-            tick()
+            late = ff_steps[3:]
+            plan((late.pop(0),), (chip_sum, 0))
             products(2, lambda: turned[...], columns(2), tick)
-            steps.insert(1, lambda: chip_sum(2))
-            tick()
+            plan((late.pop(0),), (chip_sum, 2), (go, 3, 0))
             products(1, lambda: turned[...], columns(1), tick)
-            tick()
-            resampled.wait()
+            waiting.extend(late)
 
         pl.run_scoped(
             weights,
@@ -986,10 +1038,15 @@
 
             media_out = {}
             fetch(0)
-            tick()
-            steps.insert(0, lambda: chip_sum(1))
-            for m, step in ((3, 1), (0, 0), (2, 0), (1, 0), (3, 2), (0, 1), (2, 1), (1, 1), (0, 2), (2, 2)):
-                later(go, m, step)
+            few = len(waiting) // 2
+            plan((chip_sum, 1), (added_out,), *[(f,) for f in waiting[:few]])
+            plan((go, 0, 0))
+            plan(*[(f,) for f in waiting[few:]])
+            plan((go, 3, 1), (go, 2, 0))
+            plan((go, 0, 1))
+            plan((go, 1, 0), (go, 3, 2))
+            plan((go, 2, 1))
+            plan((go, 0, 2))
             zero = jnp.zeros((8, D), F32)
             sums = (zero, zero, zero, zero)
             for load in weight_loads:
@@ -1012,7 +1069,6 @@
 
                 lax.fori_loop(0, zs, one, 0)
                 tick()
-                tick()
                 if i + 1 < images:
                     if i >= 1:
                         media_out[i - 1].wait()
@@ -1038,7 +1094,6 @@
                 latent_low[rws] = made.astype(BF16)
                 sums = (gain, shift, sums[2] + fold(up * hat), sums[3] + fold(up))
                 tick()
-                tick()
             for k, value in enumerate(sums):
                 r.norm_parts[k] = value
             for i in range(max(0, images - 2), images):
@@ -1050,10 +1105,49 @@
             pltpu.VMEM((2, patches, D), BF16),
             pltpu.VMEM((span, D), F32),
         )
+        sums = [jnp.sum(r.norm_parts[k], axis=0, keepdims=True) for k in range(6)]
+        r.totals[...] = jnp.concatenate([*sums, jnp.zeros((2, D), F32)], axis=0)
+        total_slots = {axis: [links.take() for _ in range(1, sizes[axis])] for axis in "cyxz"}
+
+        def total_copies(axis):
+            mine = total_lands[axis].at[at[axis]]
+            for k, slot in enumerate(total_slots[axis], 1):
+                yield links.copy(mine, mine, slot, axis, k)
+
+        def total_start(axis):
+            total_lands[axis][at[axis]] = r.totals[...]
+            for copy in total_copies(axis):
+                copy.start()
+
+        def total_finish(axis):
+            lands = total_lands[axis]
+            for k, slot in enumerate(total_slots[axis], 1):
+                land = lands.at[links.place(axis, sizes[axis] - k)]
+                links.copy(land, land, slot, axis, k).wait_recv()
+            value = lands[0]
+            for k in range(1, sizes[axis]):
+                value = value + lands[k]
+            r.totals[...] = value
+
+        total_start("c")
         while steps:
             tick()
+        total_finish("c")
+        total_start("y")
+        go(1, 1)
+        total_finish("y")
+        total_start("x")
+        go(2, 2)
+        total_finish("x")
+        total_start("z")
+        ff_finish()
         go(1, 2)
-        ff_finish()
+        resampled = added_finish()
+        total_finish("z")
+        for axis in "cyxz":
+            for copy in total_copies(axis):
+                copy.wait_send()
+        resampled.wait()
         for m in range(4):
             for yi in range(ys):
                 block_copy(m, yi).wait_send()
@@ -1064,6 +1158,8 @@
                 copy.wait_send()
             if unit[1]:
                 z_copy(unit).wait_send()
+        for unit in ready:
+            z_copy(unit).wait_send()
 
     for load in early:
         load.wait()
@@ -1075,27 +1171,30 @@
 
     outs.append(links.move(latent_low, r.latent_grad))
     squares = jnp.sum(r.att_share[...] * r.att_share[...]) + jnp.sum(r.ff_share[...] * r.ff_share[...])
-    rows = [jnp.sum(r.norm_parts[k], axis=0, keepdims=True) for k in range(6)]
-    value = jnp.concatenate([*rows, jnp.full((2, D), squares, F32)], axis=0)
+    value = jnp.full((8, 128), squares, F32)
     last = []
-    for axis in "cyxz":
-        lands = total_lands[axis]
-        lands[at[axis]] = value
+    for axes, lands in zip(("yc", "zx"), r.square_lands):
+        first, second = axes
+
+        def spot(way):
+            return links.place(first, way.get(first, 0)) * sizes[second] + links.place(second, way.get(second, 0))
+
+        mine = lands.at[spot({})]
+        mine[...] = value
         coming = []
-        for k in range(1, sizes[axis]):
+        for way in links.around(axes):
             slot = links.take()
-            mine = lands.at[at[axis]]
-            copy = links.copy(mine, mine, slot, axis, k)
+            copy = links.send_to(mine, mine, slot, way)
             copy.start()
             last.append(copy)
-            land = lands.at[links.place(axis, sizes[axis] - k)]
-            coming.append(links.copy(land, land, slot, axis, k))
+            land = lands.at[spot({axis: sizes[axis] - k for axis, k in way.items()})]
+            coming.append(links.send_to(land, land, slot, way))
         for copy in coming:
             copy.wait_recv()
         value = lands[0]
-        for k in range(1, sizes[axis]):
+        for k in range(1, lands.shape[0]):
             value = value + lands[k]
-    r.totals[...] = value
+    r.squares[...] = value
     for copy in last:
         copy.wait_send()
     for out in outs:
@@ -1135,6 +1234,7 @@
         att_share=((4, row_block, col_block), F32, vmem),
         ff_share=((2, row_block, ff_block), F32, vmem),
         totals=((8, D), F32, vmem),
+        squares=((8, 128), F32, vmem),
     )
     scratch = dict(
         grads_ff=(got.ff.shape, BF16),
@@ -1151,13 +1251,14 @@
         norm_parts=((6, 8, D), F32),
     )
     totals = [((sizes[axis], 8, D), F32) for axis in "cyxz"]
+    totals += [((sizes[a] * sizes[b], 8, 128), F32) for a, b in ("yc", "zx")]
     lands = {}
     for m, orders in ATT_ORDERS.items():
         for s, order in enumerate(orders):
             for step, shape in enumerate(land_shapes(sizes, order, "yzx", (half, col_block))):
                 lands[m, s, step] = (shape, BF16)
     steps = sum(v - 1 for v in sizes.values())
-    slots = 9 * steps + 2 * (zs * xs + zs) + 6 * ys
+    slots = 9 * steps + 2 * (zs * xs + zs) + 6 * ys + zs * xs + ys * cs
     semaphores = dict(send=slots, recv=slots, local=3 * images + 30)
     names = [*inputs, *outputs, *semaphores, *scratch]
     made = pl.pallas_call(
@@ -1187,17 +1288,17 @@
 
 
 def update_kernel(cuts, *refs):
-    shares, refs = refs[:4], refs[4:]
+    shares, refs = refs[:5], refs[5:]
     att, expand, reduce, norm, refs = refs[:3], refs[3:6], refs[6:9], refs[9:12], refs[12:]
     carried, refs = refs[:3], refs[3:]
     att_out, expand_out, reduce_out, norm_out, refs = refs[:3], refs[3:6], refs[6:9], refs[9:12], refs[12:]
     size_out, carried_out = refs[0], refs[1:4]
-    att_share, expand_share, reduce_share, totals = shares
+    att_share, expand_share, reduce_share, totals, local_squares = shares
     step = pl.program_id(0)
     for a, b in zip(carried, carried_out):
         b[...] = a[...]
     norm_total = totals[:6]
-    squares = totals[6:7, :1] + jnp.sum(norm_total * norm_total).reshape(1, 1)
+    squares = local_squares[:1, :1] + jnp.sum(norm_total * norm_total).reshape(1, 1)
     size = jnp.sqrt(squares)
     clip = jnp.minimum(1.0, MAX_NORM / (size + 1e-06))
 
@@ -1239,13 +1340,14 @@
             pl.BlockSpec((1, row_block // cuts, ff_block), lambda j: (0, j, 0)),
             pl.BlockSpec((1, row_block, ff_block // cuts), lambda j: (1, 0, j)),
             pl.BlockSpec((8, D), lambda j: (0, 0)),
+            pl.BlockSpec((8, 128), lambda j: (0, 0)),
             *specs,
             *carried_specs,
         ],
         out_specs=[*specs, pl.BlockSpec((1, 1), lambda j: (0, 0)), *carried_specs],
         compiler_params=pltpu.CompilerParams(vmem_limit_bytes=63 * MIB),
         name="update_kernel",
-    )(back.att_share, back.ff_share, back.ff_share, back.totals, *shapes, *carried)
+    )(back.att_share, back.ff_share, back.ff_share, back.totals, back.squares, *shapes, *carried)
     return made[:12], made[12], made[13:]
 
 

time: 248 us -> 236 us (0.952)
  Pallas kernels: 245 us -> 233 us
    pallas_call x1, Pallas kernels: 117 us -> 102 us  [backward(): pl.pallas_call(functools.partial(backward_kernel, sizes, (names, tuple(la...]
    pallas_call x1, Pallas kernels: 118 us -> 121 us  [forward(): pl.pallas_call(functools.partial(forward_kernel, sizes), out_shape=[jax.S...]
where the time goes in v4:
time: 236 us; the launch traced here: 234 us
  Pallas kernels  233 us (99%)
    pallas_call x1, Pallas kernels, forward(): pl.pallas_call(functools.partial(forward_kernel, sizes), out_shape=[jax.S...  121 us
    pallas_call x1, Pallas kernels, backward(): pl.pallas_call(functools.partial(backward_kernel, sizes, (names, tuple(la...  102 us
    pallas_call x1, Pallas kernels, update(): pl.pallas_call(functools.partial(update_kernel, cuts), grid=(cuts,), out_...  9.67 us

profile of v4, /device:TPU:10, one launch (start us, length us, event | category | flops | bytes accessed | tf_op | source)
XLA Modules:
  0.0 233.7 jit_solution(466536452942134320)
XLA Ops:
  0.6 121.0 %gather_and_attend.1 = (bf16[4,2,2,4,2,128,256]{6,5,4,3,2,1,0:T(8,128)(2,1)}, bf16[4,8,640,256]{3,2,1,0:T(8,128)(2,1)}, bf16[1024,2560]{1,0:T(8,128)(2,1)}, bf16...) custom-call(f32[4,128,256]{2,1,0:T(8,128)} %refs_5_.1, ...), custom_call_target="tpu_custom_call" | custom-call | tf_op jit(solution)/shard_map/gather_and_attend/pallas_call | solution.py:656
  121.6 102.2 %backward_and_scatter.1 = (bf16[256,1024]{1,0:T(8,128)(2,1)}, bf16[4,576,1024]{2,1,0:T(8,128)(2,1)}, bf16[256,1024]{1,0:T(8,128)(2,1)}, f32[4,128,256]{2,1,0:T(8...) custom-call(bf16[4,2,2,4,2,128,256]{6,5,4,3,2,1,0:T(8,128)(2,1)} %get-tuple-element.50.refs_0_, ...), custom_call_target="tpu_custom_call" | custom-call | tf_op jit(solution)/shard_map/backward_and_scatter/pallas_call | solution.py:1264
  223.8 9.7 %update_kernel.1 = (f32[4,128,256]{2,1,0:T(8,128)}, f32[4,128,256]{2,1,0:T(8,128)}, f32[4,128,256]{2,1,0:T(8,128)}, f32[128,1024]{1,0:T(8,128)}, f32[128,1024]{1...) custom-call(f32[4,128,256]{2,1,0:T(8,128)} %get-tuple-element.61.ref, ...), custom_call_target="tpu_custom_call" | custom-call | tf_op jit(solution)/shard_map/update_kernel/pallas_call | solution.py:1334
